TPU v7x, 32 devices: a whole 2x2x4 slice. The times are simulated.
32 devices in a mesh: pix: 2 (over y), date: 16 (over z, x, core).
Axes of the slice: x: 2, y: 2, z: 4, core: 2. Of those that a mesh axis runs over, the one named last changes fastest.
Arguments:
- pixel_factors: float32 [8192, 256], P(('pix', 'date')), may hold values from -1.5 to 1.5
- date_factors: float32 [4096, 256], P('date'), may hold values from -1.5 to 1.5
- block_ids: int32 [2, 16, 2, 80], P('pix', 'date'), may hold values from 0 to 31, as said below
- block_counts: int32 [2, 16], P('pix', 'date'), may hold values from 20 to 80, as said below
- block_values: bfloat16 [2, 16, 80, 8192], P('pix', 'date'), may hold values from -6 to 6
- block_weights: bfloat16 [2, 16, 80, 8192], P('pix', 'date'), may hold values from 0 to 1
Outputs:
- pixel_out: float32 [8192, 256], P(('pix', 'date'))
- date_out: float32 [4096, 256], P('date')
Inputs may be any that keep to these rules, and one draw needn't show every extreme that they name: block_ids[p, q, 0, s] is a row-block below 32 and block_ids[p, q, 1, s] a date-block below 4; the 80 pairs of one device are distinct, including those beyond its count. `block_counts`: some device holds exactly 80 observed blocks.
All inputs are finite; a program needn't handle non-finite values.
Results may differ from a plain program's by a relative error of at most 0.01.
Values may be sent and summed in bfloat16 or wider, within the bound.
No kernel may reach another device: no remote copies, remote signals or barrier semaphores. Data moves between devices by JAX's collectives and lax.ppermute only.
A program may use at most 128 MiB of HBM per device.

v0:
```python
import jax
import jax.numpy as jnp
from jax import lax
from jax.sharding import PartitionSpec as P

STEPS = 2


DECAY = 0.05
STEP_SCALE = 48.0


def shards(pixel_factors, date_factors, block_ids, block_counts, block_values, block_weights):
    loop_size = lax.axis_size("date")
    own_rows = pixel_factors.shape[0]
    group_rows = own_rows * loop_size
    local_dates = date_factors.shape[0]
    all_dates = local_dates * loop_size
    all_pixels = group_rows * lax.axis_size("pix")
    block_list = block_ids[0, 0]
    slots = block_list.shape[1]
    filled = block_counts[0, 0]
    row_scale = STEP_SCALE / all_dates
    own_factors = pixel_factors
    dates_now = date_factors
    valid = (jnp.arange(slots, dtype=jnp.int32) < filled).astype(jnp.bfloat16)
    row_onehot = (
        block_list[0][None, :] == jnp.arange(group_rows // 128, dtype=jnp.int32)[:, None]
    ).astype(jnp.bfloat16) * valid[None, :]
    date_onehot = (
        block_list[1][None, :] == jnp.arange(local_dates // 64, dtype=jnp.int32)[:, None]
    ).astype(jnp.bfloat16)

    def place(blocks):
        tiles = blocks[0, 0].reshape(slots, 128, 64)
        columns = []
        for column_block in range(local_dates // 64):
            selector = row_onehot * date_onehot[column_block][None, :]
            columns.append(
                jnp.einsum(
                    "kb,bij->kij", selector, tiles, preferred_element_type=jnp.float32
                ).astype(jnp.bfloat16)
            )
        return jnp.stack(columns, axis=2).reshape(group_rows, local_dates)

    observed = place(block_values).astype(jnp.float32)
    weights_panel = place(block_weights).astype(jnp.float32)
    for iteration in range(STEPS):
        group_bf = lax.all_gather(own_factors.astype(jnp.bfloat16), "date", axis=0, tiled=True)
        dates_bf = dates_now.astype(jnp.bfloat16)
        predicted = jnp.einsum("gr,dr->gd", group_bf, dates_bf, preferred_element_type=jnp.float32)
        errors = (weights_panel * (predicted - observed)).astype(jnp.bfloat16)

        def term_rows(start, count, errors=errors, dates_bf=dates_bf):
            return jnp.dot(errors, dates_bf, preferred_element_type=jnp.float32)

        row_grad = lax.psum_scatter(
            term_rows(jnp.int32(0), lax.axis_size("date") * own_rows).astype(jnp.bfloat16),
            "date",
            scatter_dimension=0,
            tiled=True,
        ).astype(jnp.float32)
        date_term = jnp.einsum("gd,gr->dr", errors, group_bf, preferred_element_type=jnp.float32)
        total = lax.psum(date_term.astype(jnp.bfloat16), "pix").astype(jnp.float32)
        dates_now = (1.0 - DECAY) * dates_now - STEP_SCALE / all_pixels * total
        own_factors = (1.0 - DECAY) * own_factors - row_scale * row_grad
    return (own_factors, dates_now)


def solution(mesh):
    placed = (
        P(("pix", "date"), None),
        P("date", None),
        P("pix", "date", None, None),
        P("pix", "date"),
        P("pix", "date", None, None),
        P("pix", "date", None, None),
    )
    return jax.shard_map(
        shards,
        mesh=mesh,
        in_specs=placed,
        out_specs=(P(("pix", "date"), None), P("date", None)),
        check_vma=False,
    )
```

profile of v0, /device:TPU:0, one launch (start us, length us, event | category | flops | bytes accessed | tf_op | source)
XLA Modules:
  0.0 292.4 jit_solution(13227571516325774195)
XLA Ops:
  7.2 1.6 convert_element_type.97
  9.6 4.8 %reshape_squeeze.7 = bf16[80,128,64]{2,1,0:T(8,128)(2,1)} reshape(bf16[1,1,80,8192]{3,2,1,0:T(8,128)(2,1)} %param.10) | data formatting | bytes 2621440 | tf_op jit(solution)/shard_map/reshape;squeeze | solution.py:35
  14.4 3.8 %copy.23 = bf16[80,128,64]{1,0,2:T(8,128)(2,1)S(1)} copy(bf16[80,128,64]{2,1,0:T(8,128)(2,1)} %reshape_squeeze.7) | data formatting | bytes 2621440 | tf_op jit(solution)/shard_map/reshape;squeeze | solution.py:35
  18.6 0.3 fusion.10
  18.9 0.3 fusion.9
  19.2 0.3 fusion.8
  19.6 0.3 maximum_convert_fusion.1
  19.9 5.8 %copy.35 = f32[32,8,32,128]{3,1,2,0:T(8,128)} copy(f32[32,8,32,128]{3,2,1,0:T(8,128)S(1)} %bitcast.80) | data formatting | bytes 8388608
  25.7 5.7 %copy.27 = f32[4096,256]{1,0:T(8,128)} copy(f32[4096,256]{0,1:T(8,128)} %bitcast.82) | data formatting | bytes 8388608 | tf_op jit(solution)/shard_map/convert_element_type | solution.py:46
  31.4 3.9 %reshape_squeeze.6 = bf16[80,128,64]{2,1,0:T(8,128)(2,1)} reshape(bf16[1,1,80,8192]{3,2,1,0:T(8,128)(2,1)S(1)} %copy-done.3) | data formatting | bytes 2621440 | tf_op jit(solution)/shard_map/reshape;squeeze | solution.py:35
  35.3 4.0 %copy.19 = bf16[80,128,64]{1,0,2:T(8,128)(2,1)S(1)} copy(bf16[80,128,64]{2,1,0:T(8,128)(2,1)} %reshape_squeeze.6) | data formatting | bytes 2621440 | tf_op jit(solution)/shard_map/reshape;squeeze | solution.py:35
  39.3 0.3 fusion.7
  39.6 0.3 fusion.6
  40.3 0.3 fusion.4
  40.6 0.3 maximum_convert_fusion
  40.9 5.8 %copy.36 = f32[32,8,32,128]{3,1,2,0:T(8,128)} copy(f32[32,8,32,128]{3,2,1,0:T(8,128)S(1)} %bitcast.81) | data formatting | bytes 8388608
  46.7 5.7 %copy.28 = f32[4096,256]{1,0:T(8,128)} copy(f32[4096,256]{0,1:T(8,128)} %bitcast.83) | data formatting | bytes 8388608 | tf_op jit(solution)/shard_map/convert_element_type | solution.py:47
  52.4 2.5 all-gather.3.cloned.1.call-done
  54.9 4.8 %fusion.2 = bf16[4096,256]{1,0:T(8,128)(2,1)S(1)} fusion(f32[4096,256]{1,0:T(8,128)} %copy.28, f32[4096,256]{1,0:T(8,128)} %copy.27, bf16[4096,256]{1,0:T(8,128)(2,1)} %all-gather.3.cloned.1.call-done, f32[256,256]{1,0:T(8,128)S(1)} %copy-done), kind=kOutput, calls=%fused_computation.6 | convolution fusion | flops 540082176 | bytes 12845056 | tf_op jit(solution)/shard_map/gr,dr->gd/dot_general | solution.py:51
  59.7 2.1 convolution_convert_fusion.1
  61.9 3.0 %convolution_convert_fusion.11 = bf16[256,256]{1,0:T(8,128)(2,1)} fusion(bf16[4096,256]{1,0:T(8,128)(2,1)S(1)} %fusion.2, bf16[4096,256]{1,0:T(8,128)(2,1)} %all-gather.3.cloned.1.call-done), kind=kOutput, calls=%fused_computation.29 | convolution fusion | flops 536936448 | bytes 4325376 | tf_op jit(solution)/shard_map/gd,gr->dr/dot_general | solution.py:63
  65.0 58.8 %reduce-scatter.3.cloned.1.call-done = bf16[256,256]{1,0:T(8,128)(2,1)} async-done(((bf16[4096,256]{1,0:T(8,128)(2,1)}), bf16[256,256]{1,0:T(8,128)(2,1)}) %reduce-scatter.3.cloned.1.call-update) | async-done | bytes 131088 | tf_op jit(solution)/shard_map/reduce_scatter | solution.py:57
  123.7 1.6 fusion.12
  125.4 21.7 %all-reduce.3.cloned.1.call-done = bf16[256,256]{1,0:T(8,128)(2,1)} async-done(((bf16[256,256]{1,0:T(8,128)(2,1)}), bf16[256,256]{1,0:T(8,128)(2,1)}) %all-reduce.3.cloned.1.call-update) | async-done | bytes 131088 | tf_op jit(solution)/shard_map/psum | solution.py:64
  147.2 44.3 %all-gather.5.cloned.1.call-done = bf16[4096,256]{1,0:T(8,128)(2,1)} async-done(((bf16[256,256]{1,0:T(8,128)(2,1)}), bf16[4096,256]{1,0:T(8,128)(2,1)}) %all-gather.5.cloned.1.call-update) | async-done | bytes 2097168 | tf_op jit(solution)/shard_map/all_gather | solution.py:49
  191.4 5.0 %fusion.3 = bf16[4096,256]{1,0:T(8,128)(2,1)S(1)} fusion(f32[4096,256]{1,0:T(8,128)} %copy.28, f32[4096,256]{1,0:T(8,128)} %copy.27, bf16[4096,256]{1,0:T(8,128)(2,1)} %all-gather.5.cloned.1.call-done, bf16[256,256]{1,0:T(8,128)(2,1)} %all-reduce.3.cloned.1.call-done, f32[256,256]{1,0:T(8,128)S(1)} %copy-done), kind=kOutput, calls=%fused_computation.7 | convolution fusion | flops 540344320 | bytes 12976128 | tf_op jit(solution)/shard_map/gr,dr->gd/dot_general | solution.py:51
  196.4 1.4 convolution_convert_fusion.10
  197.9 2.1 convolution_convert_fusion
  200.0 18.2 %all-reduce.5.cloned.1.call-done = bf16[256,256]{1,0:T(8,128)(2,1)} async-done(((bf16[256,256]{1,0:T(8,128)(2,1)}), bf16[256,256]{1,0:T(8,128)(2,1)}) %all-reduce.5.cloned.1.call-update) | async-done | bytes 131088 | tf_op jit(solution)/shard_map/psum | solution.py:64
  218.2 1.7 multiply_subtract_fusion
  219.9 64.0 %reduce-scatter.5.cloned.1.call-done = bf16[256,256]{1,0:T(8,128)(2,1)} async-done(((bf16[4096,256]{1,0:T(8,128)(2,1)}), bf16[256,256]{1,0:T(8,128)(2,1)}) %reduce-scatter.5.cloned.1.call-update) | async-done | bytes 131088 | tf_op jit(solution)/shard_map/reduce_scatter | solution.py:57
  283.9 1.7 multiply_subtract_fusion.1
  (32 shorter events, 1.0 us)
Async XLA Ops:
  7.2 47.7 %all-gather.3.cloned.1.call-start = ((), (), s32[]{:S(2)}) async-start(), calls=%async_computation.2 | async-start | bytes 2228224 | tf_op jit(solution)/shard_map/all_gather | solution.py:49
  8.9 114.9 %reduce-scatter.3.cloned.1.call-start = ((), (), s32[]{:S(2)}) async-start(), calls=%async_computation.3 | async-start | bytes 2228224 | tf_op jit(solution)/shard_map/reduce_scatter | solution.py:57
  14.4 3.9 %copy-start.6 = (s32[1,1,2,80]{3,2,1,0:T(2,128)S(1)}, s32[1,1,2,80]{3,2,1,0:T(2,128)}, u32[]{:S(2)}) copy-start(s32[1,1,2,80]{3,2,1,0:T(2,128)} %param.8) | copy-start | bytes 1924
  25.7 5.7 %copy-start.3 = (bf16[1,1,80,8192]{3,2,1,0:T(8,128)(2,1)S(1)}, bf16[1,1,80,8192]{3,2,1,0:T(8,128)(2,1)}, u32[]{:S(2)}) copy-start(bf16[1,1,80,8192]{3,2,1,0:T(8,128)(2,1)} %param.11) | copy-start | bytes 3932164
  46.7 8.2 %copy-start = (f32[256,256]{1,0:T(8,128)S(1)}, f32[256,256]{1,0:T(8,128)}, u32[]{:S(2)}) copy-start(f32[256,256]{1,0:T(8,128)} %param.7) | copy-start | bytes 786436
  61.8 61.9 %copy-start.1 = (f32[256,256]{1,0:T(8,128)S(1)}, f32[256,256]{1,0:T(8,128)}, u32[]{:S(2)}) copy-start(f32[256,256]{1,0:T(8,128)} %param.6) | copy-start | bytes 786436
  61.8 85.4 %all-reduce.3.cloned.1.call-start = ((), (), s32[]{:S(2)}) async-start(), calls=%async_computation.5 | async-start | bytes 262144 | tf_op jit(solution)/shard_map/psum | solution.py:64
  64.9 126.5 %all-gather.5.cloned.1.call-start = ((), (), s32[]{:S(2)}) async-start(), calls=%async_computation.4 | async-start | bytes 2228224 | tf_op jit(solution)/shard_map/all_gather | solution.py:49
  125.4 92.9 %all-reduce.5.cloned.1.call-start = ((), (), s32[]{:S(2)}) async-start(), calls=%async_computation.7 | async-start | bytes 262144 | tf_op jit(solution)/shard_map/psum | solution.py:64
  191.4 5.0 %copy-start.2 = (bf16[4096,256]{1,0:T(8,128)(2,1)S(1)}, bf16[4096,256]{1,0:T(8,128)(2,1)}, u32[]{:S(2)}) copy-start(bf16[4096,256]{1,0:T(8,128)(2,1)} %all-gather.5.cloned.1.call-done) | copy-start | bytes 6291460
  196.4 1.5 copy-start.4
  197.9 86.0 %reduce-scatter.5.cloned.1.call-start = ((), (), s32[]{:S(2)}) async-start(), calls=%async_computation.6 | async-start | bytes 2228224 | tf_op jit(solution)/shard_map/reduce_scatter | solution.py:57
  200.0 83.9 %copy-start.5 = (bf16[256,256]{1,0:T(8,128)(2,1)S(1)}, bf16[256,256]{1,0:T(8,128)(2,1)}, u32[]{:S(2)}) copy-start(bf16[256,256]{1,0:T(8,128)(2,1)} %reduce-scatter.3.cloned.1.call-done) | copy-start | bytes 393220
Sparse Core Ops, SparseCore 0:
  10.7 44.0 all-gather.2
  61.9 61.7 reduce-scatter.2
  126.7 20.4 all-reduce.2
  150.0 41.3 all-gather.4
  198.0 20.1 all-reduce.4
  222.3 61.5 reduce-scatter.4
where the time goes:
time: 293 us; the launch traced here: 292 us
  waiting for transfers between devices  210 us (72%)
  local copies, waits for them, and re-layouts  39.5 us (13%)
  matrix products  20.9 us (7%)
  between operations  14.9 us (5%)
  other arithmetic  7.28 us (2%)
    reduce_scatter x2, waiting for transfers between devices, shards(): lax.psum_scatter(term_rows(jnp.int32(0), lax.axis_size('date') * own_rows...  123 us
    all_gather x2, waiting for transfers between devices, shards(): lax.all_gather(own_factors.astype(jnp.bfloat16), 'date', axis=0, tiled=True)  46.7 us
    psum x2, waiting for transfers between devices, shards(): total = lax.psum(date_term.astype(jnp.bfloat16), 'pix').astype(jnp.float32)  40 us
    another operation x4, local copies, waits for them, and re-layouts, place(): tiles = blocks[0, 0].reshape(slots, 128, 64)  16.5 us
    unnamed x16, local copies, waits for them, and re-layouts  11.5 us
    dot_general x2, matrix products, shards(): jnp.einsum('gr,dr->gd', group_bf, dates_bf, preferred_element_type=jnp.fl...  9.8 us
  transfers between devices with their start and end apart: 6, of which 6 were waited for; matrix products, arithmetic and copies ran while one was open for 17% of the time, Pallas kernels for 0%

commit v1 on v0

v1 whole, which is shorter than its diff:
```python
import functools

import jax
import jax.numpy as jnp
from jax import lax
from jax.experimental import pallas as pl
from jax.experimental.pallas import tpu as pltpu
from jax.sharding import PartitionSpec as P

STEPS = 2
DECAY = 0.05
STEP_SCALE = 48.0
BLOCK_ROWS = 128
BLOCK_DATES = 64
LANES = 128
GROUP = 16
F32 = jnp.float32
BF16 = jnp.bfloat16
VMEM = pl.BlockSpec(memory_space=pltpu.VMEM)
SMEM = pl.BlockSpec(memory_space=pltpu.SMEM)


def params(mib):
    return pltpu.CompilerParams(vmem_limit_bytes=mib << 20)


def cost(flops, bytes_accessed):
    return pl.CostEstimate(flops=flops, bytes_accessed=bytes_accessed, transcendentals=0)


def row_pieces(rows):
    half = BLOCK_ROWS // 2
    for block in range(rows // BLOCK_ROWS):
        for odd in range(2):
            yield block * BLOCK_ROWS + odd * half, pl.ds(block * BLOCK_ROWS + odd, half, stride=2), half


def prepare_kernel(pixel_ref, date_ref, pixel_now_ref, pixel_bf_ref, date_bf_ref, slab):
    rows, rank = pixel_ref.shape
    for lane in range(0, rank, LANES):
        slab[lane // LANES] = pixel_ref[:, lane : lane + LANES]
    for to, source, half in row_pieces(rows):
        for lane in range(0, rank, LANES):
            piece = slab[lane // LANES, source, :]
            pixel_now_ref[to : to + half, lane : lane + LANES] = piece
            pixel_bf_ref[to : to + half, lane : lane + LANES] = piece.astype(BF16)
    date_bf_ref[...] = date_ref[...].astype(BF16)


def place_kernel(chip_blocks, place_ref, count_ref, ids_ref, values_ref, weights_ref, mine_ref, other_ref, flat):
    tiles = values_ref.shape[1] // LANES
    core_blocks = chip_blocks // 2
    chip, core = place_ref[0], place_ref[1]
    mine_ref[...] = jnp.zeros_like(mine_ref)
    other_ref[...] = jnp.zeros_like(other_ref)
    count = count_ref[0, 0]

    def group(g, carry):
        first = pl.multiple_of(g * GROUP, GROUP)
        for which, ref in enumerate((values_ref, weights_ref)):
            for t in range(tiles):
                flat[which, t * GROUP : (t + 1) * GROUP, :] = ref[
                    pl.ds(first, GROUP), t * LANES : (t + 1) * LANES
                ].astype(F32)
        for s in range(GROUP):
            row_block, date_block = ids_ref[0, first + s], ids_ref[1, first + s]
            target = lax.bitwise_xor(lax.div(row_block, chip_blocks), chip)
            inside = lax.rem(row_block, chip_blocks)
            parity = lax.div(inside, core_blocks)
            row = pl.multiple_of((target * core_blocks + lax.rem(inside, core_blocks)) * tiles, tiles)
            lane = pl.multiple_of(date_block * LANES, LANES)
            listed = first + s < count

            def put(ref, s=s, row=row, lane=lane):
                for which in range(2):
                    tile = flat[which, pl.ds(s, tiles, stride=GROUP), :]
                    ref[which, pl.ds(row, tiles), pl.ds(lane, LANES)] = tile.astype(BF16)

            pl.when(jnp.logical_and(listed, parity == core))(functools.partial(put, mine_ref))
            pl.when(jnp.logical_and(listed, parity != core))(functools.partial(put, other_ref))
        return carry

    lax.fori_loop(0, lax.div(count + GROUP - 1, GROUP), group, 0)


def apart(ref, which, first, rows):
    low = lax.broadcasted_iota(jnp.int32, (rows, LANES), 1) < BLOCK_DATES
    even, odd = [], []
    for pair in range(ref.shape[2] // (2 * LANES)):
        a = ref[which, first : first + rows, 2 * pair * LANES : (2 * pair + 1) * LANES].astype(F32)
        b = ref[which, first : first + rows, (2 * pair + 1) * LANES : (2 * pair + 2) * LANES].astype(F32)
        even.append(jnp.where(low, a, pltpu.roll(b, BLOCK_DATES, 1)))
        odd.append(jnp.where(low, pltpu.roll(a, BLOCK_DATES, 1), b))
    return jnp.concatenate([jnp.concatenate(even, axis=1), jnp.concatenate(odd, axis=1)], axis=0)


def chunk_kernel(n_recv, pixel_ref, dates_ref, dates_other_ref, mine_ref, other_ref, *rest):
    recv_refs, (term_ref, errors_ref) = rest[:n_recv], rest[n_recv:]
    half = BLOCK_ROWS // 2
    local = dates_ref.shape[0]
    for block in range(pixel_ref.shape[0] // BLOCK_ROWS):
        rows = slice(block * BLOCK_ROWS, (block + 1) * BLOCK_ROWS)
        total = None
        for k, (panel, dates) in enumerate(((mine_ref, dates_ref), (other_ref, dates_other_ref))):
            predicted = lax.dot_general(
                pixel_ref[rows, :], dates[...], (((1,), (1,)), ((), ())), preferred_element_type=F32
            )
            observed = apart(panel, 0, block * half, half)
            weights = apart(panel, 1, block * half, half)
            errors = (weights * (predicted - observed)).astype(BF16)
            errors_ref[rows, k * local : (k + 1) * local] = errors
            term = jnp.dot(errors, dates[...], preferred_element_type=F32)
            total = term if total is None else total + term
        for ref in recv_refs:
            total = total + ref[rows, :].astype(F32)
        term_ref[rows, :] = total.astype(term_ref.dtype)


def chunk(index, pixel_bf, dates_bf, dates_other, mine, other, recv, kind):
    rows, rank = pixel_bf.shape
    local = dates_bf.shape[0]
    panel = pl.BlockSpec((2, rows // 2, mine.shape[2]), lambda i: (0, index, 0))
    whole = lambda a: pl.BlockSpec(a.shape, lambda i: (0,) * a.ndim)
    return pl.pallas_call(
        functools.partial(chunk_kernel, len(recv)),
        grid=(1,),
        out_shape=(
            jax.ShapeDtypeStruct((rows, rank), kind),
            jax.ShapeDtypeStruct((rows, 2 * local), BF16),
        ),
        in_specs=[whole(pixel_bf), whole(dates_bf), whole(dates_other), panel, panel] + [whole(r) for r in recv],
        out_specs=(pl.BlockSpec((rows, rank), lambda i: (0, 0)), pl.BlockSpec((rows, 2 * local), lambda i: (0, 0))),
        compiler_params=params(24),
        cost_estimate=cost(8 * rows * rank * local, 1200000),
    )(pixel_bf, dates_bf, dates_other, mine, other, *recv)


def date_kernel(n, *refs):
    errors_refs, pixel_refs, (own_ref, other_ref) = refs[:n], refs[n : 2 * n], refs[2 * n :]
    local = own_ref.shape[0]
    for k, out in enumerate((own_ref, other_ref)):
        total = None
        for errors, pixels in zip(errors_refs, pixel_refs):
            term = lax.dot_general(
                errors[:, k * local : (k + 1) * local], pixels[...],
                (((0,), (0,)), ((), ())), preferred_element_type=F32,
            )
            total = term if total is None else total + term
        out[...] = total.astype(out.dtype)


def date_gradient(errors, pixels, local):
    rank = pixels[0].shape[1]
    n = len(errors)
    return pl.pallas_call(
        functools.partial(date_kernel, n),
        out_shape=(jax.ShapeDtypeStruct((local, rank), F32), jax.ShapeDtypeStruct((local, rank), BF16)),
        in_specs=[VMEM] * (2 * n),
        out_specs=(VMEM, VMEM),
        compiler_params=params(32),
        cost_estimate=cost(4 * n * pixels[0].shape[0] * rank * local, n * 400000),
    )(*errors, *pixels)


def pixel_kernel(scale, last, now_ref, *rest):
    parts, outs = rest[:-2], rest[-2:]
    rows, rank = now_ref.shape
    for start, target, half in row_pieces(rows):
        for lane in range(0, rank, LANES):
            at = (slice(start, start + half), slice(lane, lane + LANES))
            grad = parts[0][at].astype(F32)
            for part in parts[1:]:
                grad = grad + part[at].astype(F32)
            new = (1.0 - DECAY) * now_ref[at] - scale * grad
            if last:
                outs[1][lane // LANES, target, :] = new
            else:
                outs[0][at] = new
                outs[1][at] = new.astype(BF16)
    if last:
        for lane in range(0, rank, LANES):
            outs[0][:, lane : lane + LANES] = outs[1][lane // LANES]


def pixel_update(scale, last, now, parts):
    full = jax.ShapeDtypeStruct(now.shape, F32)
    return pl.pallas_call(
        functools.partial(pixel_kernel, scale, last),
        out_shape=(full,) if last else (full, jax.ShapeDtypeStruct(now.shape, BF16)),
        in_specs=[VMEM] * (1 + len(parts)),
        out_specs=(VMEM,) if last else (VMEM, VMEM),
        scratch_shapes=[pltpu.VMEM((now.shape[1] // LANES, now.shape[0], LANES), F32)] if last else [],
        compiler_params=params(16),
        cost_estimate=cost(10 * now.size, 8 * now.size),
    )(now, *parts)


def shards(pixel_factors, date_factors, block_ids, block_counts, block_values, block_weights):
    loop_size, groups = lax.axis_size("date"), lax.axis_size("pix")
    own_rows, rank = pixel_factors.shape
    local = date_factors.shape[0]
    chips = loop_size // 2
    high = min(4, chips)
    low = chips // high
    all_pixels = own_rows * loop_size * groups
    all_dates = local * loop_size
    slots, flat = block_values.shape[2:]
    me = lax.axis_index("date")
    tiles = flat // LANES
    core_blocks = own_rows // BLOCK_ROWS

    def swap(x, mask, axis="date"):
        return lax.ppermute(x, axis, [(i, i ^ mask) for i in range(lax.axis_size(axis))])

    shape = jax.ShapeDtypeStruct
    pixel_now, pixel_bf, dates_bf = pl.pallas_call(
        prepare_kernel,
        out_shape=(shape((own_rows, rank), F32), shape((own_rows, rank), BF16), shape((local, rank), BF16)),
        in_specs=[VMEM, VMEM],
        out_specs=(VMEM, VMEM, VMEM),
        scratch_shapes=[pltpu.VMEM((rank // LANES, own_rows, LANES), F32)],
        compiler_params=params(16),
        cost_estimate=cost(own_rows * rank, own_rows * rank * 16),
    )(pixel_factors, date_factors)
    dates_now = date_factors
    dates_other = swap(dates_bf, 1)

    panel = shape((2, chips * core_blocks * tiles, (local // BLOCK_DATES) * LANES), BF16)
    mine, other = pl.pallas_call(
        functools.partial(place_kernel, 2 * core_blocks),
        out_shape=(panel, panel),
        in_specs=[SMEM, SMEM, SMEM, VMEM, VMEM],
        out_specs=(VMEM, VMEM),
        scratch_shapes=[pltpu.VMEM((2, tiles * GROUP, LANES), F32)],
        compiler_params=params(32),
        cost_estimate=cost(slots * flat * 8, slots * flat * 8),
    )(
        jnp.stack([me // 2, me % 2]).astype(jnp.int32),
        block_counts,
        block_ids.reshape(2, slots),
        block_values.reshape(slots, flat),
        block_weights.reshape(slots, flat),
    )
    other = swap(other, 1)

    order = list(range(high - 1, -1, -1))
    for step in range(STEPS):
        last = step == STEPS - 1
        pixels = {}
        for hi in order:
            pixels[hi, 0] = swap(pixel_bf, 2 * low * hi) if hi else pixel_bf
        for hi in order:
            for lo in range(1, low):
                pixels[hi, lo] = swap(pixels[hi, 0], 2 * lo)
        errors, parts = {}, []
        for hi in order:
            recv = []
            for lo in range(1, low):
                term, errors[hi, lo] = chunk(
                    hi * low + lo, pixels[hi, lo], dates_bf, dates_other, mine, other, [], BF16
                )
                recv.append(swap(term, 2 * lo))
            term, errors[hi, 0] = chunk(
                hi * low, pixels[hi, 0], dates_bf, dates_other, mine, other, recv, BF16 if hi else F32
            )
            parts.append(swap(term, 2 * low * hi) if hi else term)
        keys = list(errors)
        own, partner = date_gradient([errors[k] for k in keys], [pixels[k] for k in keys], local)
        total = own + swap(partner, 1).astype(F32)
        mask = 1
        while mask < groups:
            rounded = total.astype(BF16)
            total = rounded.astype(F32) + swap(rounded, mask, "pix").astype(F32)
            mask *= 2
        dates_now = (1.0 - DECAY) * dates_now - STEP_SCALE / all_pixels * total
        if not last:
            dates_bf = dates_now.astype(BF16)
            dates_other = swap(dates_bf, 1)
            pixel_now, pixel_bf = pixel_update(STEP_SCALE / all_dates, False, pixel_now, parts)
        else:
            (pixel_now,) = pixel_update(STEP_SCALE / all_dates, True, pixel_now, parts)
    return (pixel_now, dates_now)


def solution(mesh):
    placed = (
        P(("pix", "date"), None),
        P("date", None),
        P("pix", "date", None, None),
        P("pix", "date"),
        P("pix", "date", None, None),
        P("pix", "date", None, None),
    )
    return jax.shard_map(
        shards,
        mesh=mesh,
        in_specs=placed,
        out_specs=(P(("pix", "date"), None), P("date", None)),
        check_vma=False,
    )
```

time: 293 us -> 116 us (0.40)
  waiting for transfers between devices: 210 us -> 54.5 us
  starting transfers between devices: 0.25 us -> 40 us
  local copies, waits for them, and re-layouts: 39.5 us -> 3.32 us
  matrix products: 20.9 us -> 0 us
  Pallas kernels: 0 us -> 15.7 us
  between operations: 14.9 us -> 1.57 us
  other arithmetic: 7.28 us -> 1.03 us
    reduce_scatter x2 -> x0, waiting for transfers between devices: 123 us -> none  [shards(): lax.psum_scatter(term_rows(jnp.int32(0), lax.axis_size('date') * own_rows...]
    ppermute x0 -> x35, waiting for transfers between devices: none -> 54.5 us  [swap(): lax.ppermute(x, axis, [(i, i ^ mask) for i in range(lax.axis_size(axis))])]
    all_gather x2 -> x0, waiting for transfers between devices: 46.7 us -> none  [shards(): lax.all_gather(own_factors.astype(jnp.bfloat16), 'date', axis=0, tiled=True)]
    ppermute x0 -> x35, starting transfers between devices: none -> 40 us  [swap(): lax.ppermute(x, axis, [(i, i ^ mask) for i in range(lax.axis_size(axis))])]
    psum x2 -> x0, waiting for transfers between devices: 40 us -> none  [shards(): total = lax.psum(date_term.astype(jnp.bfloat16), 'pix').astype(jnp.float32)]
    dot_general x14 -> x0, matrix products: 20.9 us -> none  [the longest x2 9.8 us: shards(): jnp.einsum('gr,dr->gd', group_bf, dates_bf, preferred_element_type=jnp.fl...]
    another operation x4 -> x0, local copies, waits for them, and re-layouts: 16.5 us -> none  [place(): tiles = blocks[0, 0].reshape(slots, 128, 64)]
    pallas_call x0 -> x22, Pallas kernels: none -> 15.7 us  [the longest x16 10.1 us: chunk(): pl.pallas_call(functools.partial(chunk_kernel, len(recv)), grid=(1,), out...]
  transfers between devices with their start and end apart: 6 -> 35, of which waited for: 6 -> 22; matrix products, arithmetic and copies ran while one was open for 17% -> 0% of each run, Pallas kernels for 0% -> 8%
where the time goes in v1:
time: 116 us
  waiting for transfers between devices  54.5 us (47%)
  starting transfers between devices  40 us (34%)
  Pallas kernels  15.7 us (14%)
  local copies, waits for them, and re-layouts  3.32 us (3%)
  between operations  1.57 us (1%)
    ppermute x35, waiting for transfers between devices, swap(): lax.ppermute(x, axis, [(i, i ^ mask) for i in range(lax.axis_size(axis))])  54.5 us
    ppermute x35, starting transfers between devices, swap(): lax.ppermute(x, axis, [(i, i ^ mask) for i in range(lax.axis_size(axis))])  40 us
    pallas_call x16, Pallas kernels, chunk(): pl.pallas_call(functools.partial(chunk_kernel, len(recv)), grid=(1,), out...  10.1 us
    unnamed x10, local copies, waits for them, and re-layouts  3.32 us
    pallas_call x1, Pallas kernels, shards(): pl.pallas_call(functools.partial(place_kernel, 2 * core_blocks), out_shap...  3.18 us
  transfers between devices with their start and end apart: 35, of which 22 were waited for; matrix products, arithmetic and copies ran while one was open for 0% of the time, Pallas kernels for 8%

profile of v1, /device:TPU:0, one launch (start us, length us, event | category | flops | bytes accessed | tf_op | source)
XLA Modules:
  0.0 116.1 jit_solution(6553589425560911340)
XLA Ops:
  1.4 1.3 %copy-done.1 = bf16[1,1,80,8192]{3,2,1,0:T(8,128)(2,1)S(1)} copy-done((bf16[1,1,80,8192]{3,2,1,0:T(8,128)(2,1)S(1)}, bf16[1,1,80,8192]{3,2,1,0:T(8,128)(2,1)}, u32[]{:S(2)}) %copy-start.1) | copy-done | bytes 1310744
  2.7 1.3 %copy-done.2 = bf16[1,1,80,8192]{3,2,1,0:T(8,128)(2,1)S(1)} copy-done((bf16[1,1,80,8192]{3,2,1,0:T(8,128)(2,1)S(1)}, bf16[1,1,80,8192]{3,2,1,0:T(8,128)(2,1)}, u32[]{:S(2)}) %copy-start.2) | copy-done | bytes 1310744
  4.7 3.2 %shard_map.78 = (bf16[2,1024,512]{2,1,0:T(8,128)(2,1)S(1)}, bf16[2,1024,512]{2,1,0:T(8,128)(2,1)S(1)}) custom-call(s32[2]{0:T(128)S(1)} %pad_add_fusion.place_ref, s32[1,1]{1,0:T(1,128)S(6)} %copy.8.count_ref, s32[2,80]{1,0:T(2,128)S(1)} %bitcast.7, bf16[80,8192]{1,0:T(8,128)(2,1)S(1)} %bitcast.5, bf16[80,8192]{1,0:T(8,128)(2,1)S(1)} %bitcast.6), custom_call_target="tpu_custom_call" | custom-call | flops 5242880 | bytes 5242880 | tf_op jit(solution)/shard_map/pallas_call | solution.py:229
  7.9 2.4 %collective-permute-start.2 = (bf16[2,1024,512]{2,1,0:T(8,128)(2,1)S(1)}, bf16[2,1024,512]{2,1,0:T(8,128)(2,1)S(1)}, u32[]{:S(2)}, u32[]{:S(2)}) collective-permute-start(bf16[2,1024,512]{2,1,0:T(8,128)(2,1)S(1)} %get-tuple-element.49), channel_id=1, source_target_pairs={{0,1},{1,0},{2,3},{3,2},{4,5},{5,4},{6,7},{7,6},{8,9},{9,8},{10,11... | collective-permute-start | bytes 6291464 | tf_op jit(solution)/shard_map/ppermute | solution.py:213
  10.4 1.6 %collective-permute-start.14 = (bf16[256,256]{1,0:T(8,128)(2,1)S(1)}, bf16[256,256]{1,0:T(8,128)(2,1)S(1)}, u32[]{:S(2)}, u32[]{:S(2)}) collective-permute-start(bf16[256,256]{1,0:T(8,128)(2,1)S(1)} %get-tuple-element.46.pixel_ref.refs_15_), channel_id=1, source_target_pairs={{0,2},{1,3},{2,0},{3,1},{4,6},{5,7},{6,4},{7,5},{8,10},{9,11},{10,... | collective-permute-start | bytes 393224 | tf_op jit(solution)/shard_map/ppermute | solution.py:213
  12.1 2.6 %collective-permute-start.10 = (bf16[256,256]{1,0:T(8,128)(2,1)S(1)}, bf16[256,256]{1,0:T(8,128)(2,1)S(1)}, u32[]{:S(2)}, u32[]{:S(2)}) collective-permute-start(bf16[256,256]{1,0:T(8,128)(2,1)S(1)} %get-tuple-element.46.pixel_ref.refs_15_), channel_id=1, source_target_pairs={{0,4},{1,5},{2,6},{3,7},{4,0},{5,1},{6,2},{7,3},{8,12},{9,13},{10,... | collective-permute-start | bytes 393224 | tf_op jit(solution)/shard_map/ppermute | solution.py:213
  14.6 1.4 %collective-permute-start.6 = (bf16[256,256]{1,0:T(8,128)(2,1)S(1)}, bf16[256,256]{1,0:T(8,128)(2,1)S(1)}, u32[]{:S(2)}, u32[]{:S(2)}) collective-permute-start(bf16[256,256]{1,0:T(8,128)(2,1)S(1)} %get-tuple-element.46.pixel_ref.refs_15_), channel_id=1, source_target_pairs={{0,8},{1,9},{2,10},{3,11},{4,12},{5,13},{6,14},{7,15},{8,0},{9,1},... | collective-permute-start | bytes 393224 | tf_op jit(solution)/shard_map/ppermute | solution.py:213
  16.0 1.1 collective-permute-start
  17.1 3.3 %collective-permute-done.10.pixel_ref.refs_13_ = bf16[256,256]{1,0:T(8,128)(2,1)S(1)} collective-permute-done((bf16[256,256]{1,0:T(8,128)(2,1)S(1)}, bf16[256,256]{1,0:T(8,128)(2,1)S(1)}, u32[]{:S(2)}, u32[]{:S(2)}) %collective-permute-start.10) | collective-permute-done | bytes 131104 | tf_op jit(solution)/shard_map/ppermute | solution.py:213
  20.9 6.6 %collective-permute-done.6.pixel_ref.refs_11_ = bf16[256,256]{1,0:T(8,128)(2,1)S(1)} collective-permute-done((bf16[256,256]{1,0:T(8,128)(2,1)S(1)}, bf16[256,256]{1,0:T(8,128)(2,1)S(1)}, u32[]{:S(2)}, u32[]{:S(2)}) %collective-permute-start.6) | collective-permute-done | bytes 131104 | tf_op jit(solution)/shard_map/ppermute | solution.py:213
  28.3 1.3 %collective-permute-start.3 = (bf16[256,256]{1,0:T(8,128)(2,1)S(1)}, bf16[256,256]{1,0:T(8,128)(2,1)S(1)}, u32[]{:S(2)}, u32[]{:S(2)}) collective-permute-start(bf16[256,256]{1,0:T(8,128)(2,1)S(1)} %collective-permute-done.pixel_ref.refs_9_), channel_id=1, source_target_pairs={{0,2},{1,3},{2,0},{3,1},{4,6},{5,7},{6,4},{7,5},{8,10},{9,11},{10,... | collective-permute-start | bytes 393224 | tf_op jit(solution)/shard_map/ppermute | solution.py:213
  31.7 1.4 %collective-permute-start.12 = (bf16[256,256]{1,0:T(8,128)(2,1)S(1)}, bf16[256,256]{1,0:T(8,128)(2,1)S(1)}, u32[]{:S(2)}, u32[]{:S(2)}) collective-permute-start(bf16[256,256]{1,0:T(8,128)(2,1)S(1)} %get-tuple-element.54), channel_id=1, source_target_pairs={{0,2},{1,3},{2,0},{3,1},{4,6},{5,7},{6,4},{7,5},{8,10},{9,11},{10,... | collective-permute-start | bytes 393224 | tf_op jit(solution)/shard_map/ppermute | solution.py:213
  35.3 1.3 %collective-permute-done.3.pixel_ref.refs_8_ = bf16[256,256]{1,0:T(8,128)(2,1)S(1)} collective-permute-done((bf16[256,256]{1,0:T(8,128)(2,1)S(1)}, bf16[256,256]{1,0:T(8,128)(2,1)S(1)}, u32[]{:S(2)}, u32[]{:S(2)}) %collective-permute-start.3) | collective-permute-done | bytes 131104 | tf_op jit(solution)/shard_map/ppermute | solution.py:213
  38.2 1.3 %collective-permute-done.15.rest_0_ = bf16[256,256]{1,0:T(8,128)(2,1)S(1)} collective-permute-done((bf16[256,256]{1,0:T(8,128)(2,1)S(1)}, bf16[256,256]{1,0:T(8,128)(2,1)S(1)}, u32[]{:S(2)}, u32[]{:S(2)}) %collective-permute-start.15) | collective-permute-done | bytes 131104 | tf_op jit(solution)/shard_map/ppermute | solution.py:213
  45.2 2.4 %collective-permute-start.13 = (bf16[256,256]{1,0:T(8,128)(2,1)S(1)}, bf16[256,256]{1,0:T(8,128)(2,1)S(1)}, u32[]{:S(2)}, u32[]{:S(2)}) collective-permute-start(bf16[256,256]{1,0:T(8,128)(2,1)S(1)} %get-tuple-element.55), channel_id=1, source_target_pairs={{0,4},{1,5},{2,6},{3,7},{4,0},{5,1},{6,2},{7,3},{8,12},{9,13},{10,... | collective-permute-start | bytes 393224 | tf_op jit(solution)/shard_map/ppermute | solution.py:213
  47.6 2.1 %collective-permute-start.9 = (bf16[256,256]{1,0:T(8,128)(2,1)S(1)}, bf16[256,256]{1,0:T(8,128)(2,1)S(1)}, u32[]{:S(2)}, u32[]{:S(2)}) collective-permute-start(bf16[256,256]{1,0:T(8,128)(2,1)S(1)} %get-tuple-element.53), channel_id=1, source_target_pairs={{0,8},{1,9},{2,10},{3,11},{4,12},{5,13},{6,14},{7,15},{8,0},{9,1},... | collective-permute-start | bytes 393224 | tf_op jit(solution)/shard_map/ppermute | solution.py:213
  50.6 3.2 %collective-permute-done.13.rest_2_ = bf16[256,256]{1,0:T(8,128)(2,1)S(1)} collective-permute-done((bf16[256,256]{1,0:T(8,128)(2,1)S(1)}, bf16[256,256]{1,0:T(8,128)(2,1)S(1)}, u32[]{:S(2)}, u32[]{:S(2)}) %collective-permute-start.13) | collective-permute-done | bytes 131104 | tf_op jit(solution)/shard_map/ppermute | solution.py:213
  53.8 6.7 %collective-permute-done.9.rest_1_ = bf16[256,256]{1,0:T(8,128)(2,1)S(1)} collective-permute-done((bf16[256,256]{1,0:T(8,128)(2,1)S(1)}, bf16[256,256]{1,0:T(8,128)(2,1)S(1)}, u32[]{:S(2)}, u32[]{:S(2)}) %collective-permute-start.9) | collective-permute-done | bytes 131104 | tf_op jit(solution)/shard_map/ppermute | solution.py:213
  60.6 2.7 %collective-permute-start.27 = (bf16[256,256]{1,0:T(8,128)(2,1)S(1)}, bf16[256,256]{1,0:T(8,128)(2,1)S(1)}, u32[]{:S(2)}, u32[]{:S(2)}) collective-permute-start(bf16[256,256]{1,0:T(8,128)(2,1)S(1)} %get-tuple-element.59.pixel_ref.refs_15_), channel_id=1, source_target_pairs={{0,4},{1,5},{2,6},{3,7},{4,0},{5,1},{6,2},{7,3},{8,12},{9,13},{10,... | collective-permute-start | bytes 393224 | tf_op jit(solution)/shard_map/ppermute | solution.py:213
  64.0 1.7 %collective-permute-start.16 = (bf16[256,256]{1,0:T(8,128)(2,1)S(1)}, bf16[256,256]{1,0:T(8,128)(2,1)S(1)}, u32[]{:S(2)}, u32[]{:S(2)}) collective-permute-start(bf16[256,256]{1,0:T(8,128)(2,1)S(1)} %get-tuple-element.59.pixel_ref.refs_15_), channel_id=1, source_target_pairs={{0,12},{1,13},{2,14},{3,15},{4,8},{5,9},{6,10},{7,11},{8,4},{9,5},... | collective-permute-start | bytes 393224 | tf_op jit(solution)/shard_map/ppermute | solution.py:213
  65.9 7.8 %collective-permute-done.16.pixel_ref.refs_9_ = bf16[256,256]{1,0:T(8,128)(2,1)S(1)} collective-permute-done((bf16[256,256]{1,0:T(8,128)(2,1)S(1)}, bf16[256,256]{1,0:T(8,128)(2,1)S(1)}, u32[]{:S(2)}, u32[]{:S(2)}) %collective-permute-start.16) | collective-permute-done | bytes 131104 | tf_op jit(solution)/shard_map/ppermute | solution.py:213
  74.5 1.1 collective-permute-done.23.pixel_ref.refs_11_
  76.3 1.3 %collective-permute-start.28 = (bf16[256,256]{1,0:T(8,128)(2,1)S(1)}, bf16[256,256]{1,0:T(8,128)(2,1)S(1)}, u32[]{:S(2)}, u32[]{:S(2)}) collective-permute-start(bf16[256,256]{1,0:T(8,128)(2,1)S(1)} %collective-permute-done.27.pixel_ref.refs_13_), channel_id=1, source_target_pairs={{0,2},{1,3},{2,0},{3,1},{4,6},{5,7},{6,4},{7,5},{8,10},{9,11},{10,... | collective-permute-start | bytes 393224 | tf_op jit(solution)/shard_map/ppermute | solution.py:213
  78.3 1.8 %collective-permute-done.20.pixel_ref.refs_8_ = bf16[256,256]{1,0:T(8,128)(2,1)S(1)} collective-permute-done((bf16[256,256]{1,0:T(8,128)(2,1)S(1)}, bf16[256,256]{1,0:T(8,128)(2,1)S(1)}, u32[]{:S(2)}, u32[]{:S(2)}) %collective-permute-start.20) | collective-permute-done | bytes 131104 | tf_op jit(solution)/shard_map/ppermute | solution.py:213
  81.6 1.3 %collective-permute-done.24.pixel_ref.refs_10_ = bf16[256,256]{1,0:T(8,128)(2,1)S(1)} collective-permute-done((bf16[256,256]{1,0:T(8,128)(2,1)S(1)}, bf16[256,256]{1,0:T(8,128)(2,1)S(1)}, u32[]{:S(2)}, u32[]{:S(2)}) %collective-permute-start.24) | collective-permute-done | bytes 131104 | tf_op jit(solution)/shard_map/ppermute | solution.py:213
  84.4 1.3 %collective-permute-done.28.pixel_ref.refs_12_ = bf16[256,256]{1,0:T(8,128)(2,1)S(1)} collective-permute-done((bf16[256,256]{1,0:T(8,128)(2,1)S(1)}, bf16[256,256]{1,0:T(8,128)(2,1)S(1)}, u32[]{:S(2)}, u32[]{:S(2)}) %collective-permute-start.28) | collective-permute-done | bytes 131104 | tf_op jit(solution)/shard_map/ppermute | solution.py:213
  87.2 1.3 %collective-permute-done.31.pixel_ref.refs_14_ = bf16[256,256]{1,0:T(8,128)(2,1)S(1)} collective-permute-done((bf16[256,256]{1,0:T(8,128)(2,1)S(1)}, bf16[256,256]{1,0:T(8,128)(2,1)S(1)}, u32[]{:S(2)}, u32[]{:S(2)}) %collective-permute-start.31) | collective-permute-done | bytes 131104 | tf_op jit(solution)/shard_map/ppermute | solution.py:213
  90.0 1.3 %collective-permute-done.21.rest_0_ = bf16[256,256]{1,0:T(8,128)(2,1)S(1)} collective-permute-done((bf16[256,256]{1,0:T(8,128)(2,1)S(1)}, bf16[256,256]{1,0:T(8,128)(2,1)S(1)}, u32[]{:S(2)}, u32[]{:S(2)}) %collective-permute-start.21) | collective-permute-done | bytes 131104 | tf_op jit(solution)/shard_map/ppermute | solution.py:213
  92.0 2.1 %collective-permute-done.25.rest_0_ = bf16[256,256]{1,0:T(8,128)(2,1)S(1)} collective-permute-done((bf16[256,256]{1,0:T(8,128)(2,1)S(1)}, bf16[256,256]{1,0:T(8,128)(2,1)S(1)}, u32[]{:S(2)}, u32[]{:S(2)}) %collective-permute-start.25) | collective-permute-done | bytes 131104 | tf_op jit(solution)/shard_map/ppermute | solution.py:213
  98.4 1.8 %collective-permute-start.22 = (bf16[256,256]{1,0:T(8,128)(2,1)S(1)}, bf16[256,256]{1,0:T(8,128)(2,1)S(1)}, u32[]{:S(2)}, u32[]{:S(2)}) collective-permute-start(bf16[256,256]{1,0:T(8,128)(2,1)S(1)} %get-tuple-element.71), channel_id=1, source_target_pairs={{0,12},{1,13},{2,14},{3,15},{4,8},{5,9},{6,10},{7,11},{8,4},{9,5},... | collective-permute-start | bytes 393224 | tf_op jit(solution)/shard_map/ppermute | solution.py:213
  100.2 4.3 %collective-permute-start.26 = (bf16[256,256]{1,0:T(8,128)(2,1)S(1)}, bf16[256,256]{1,0:T(8,128)(2,1)S(1)}, u32[]{:S(2)}, u32[]{:S(2)}) collective-permute-start(bf16[256,256]{1,0:T(8,128)(2,1)S(1)} %get-tuple-element.73), channel_id=1, source_target_pairs={{0,8},{1,9},{2,10},{3,11},{4,12},{5,13},{6,14},{7,15},{8,0},{9,1},... | collective-permute-start | bytes 393224 | tf_op jit(solution)/shard_map/ppermute | solution.py:213
  106.1 8.4 %collective-permute-done.26.rest_1_ = bf16[256,256]{1,0:T(8,128)(2,1)S(1)} collective-permute-done((bf16[256,256]{1,0:T(8,128)(2,1)S(1)}, bf16[256,256]{1,0:T(8,128)(2,1)S(1)}, u32[]{:S(2)}, u32[]{:S(2)}) %collective-permute-start.26) | collective-permute-done | bytes 131104 | tf_op jit(solution)/shard_map/ppermute | solution.py:213
  (75 shorter events, 31.6 us)
Async XLA Ops:
  7.9 21.6 %collective-permute-start.2 = (bf16[2,1024,512]{2,1,0:T(8,128)(2,1)S(1)}, bf16[2,1024,512]{2,1,0:T(8,128)(2,1)S(1)}, u32[]{:S(2)}, u32[]{:S(2)}) collective-permute-start(bf16[2,1024,512]{2,1,0:T(8,128)(2,1)S(1)} %get-tuple-element.49), channel_id=1, source_target_pairs={{0,1},{1,0},{2,3},{3,2},{4,5},{5,4},{6,7},{7,6},{8,9},{9,8},{10,11... | collective-permute-start | bytes 6291464 | tf_op jit(solution)/shard_map/ppermute | solution.py:213
  10.4 6.7 %collective-permute-start.14 = (bf16[256,256]{1,0:T(8,128)(2,1)S(1)}, bf16[256,256]{1,0:T(8,128)(2,1)S(1)}, u32[]{:S(2)}, u32[]{:S(2)}) collective-permute-start(bf16[256,256]{1,0:T(8,128)(2,1)S(1)} %get-tuple-element.46.pixel_ref.refs_15_), channel_id=1, source_target_pairs={{0,2},{1,3},{2,0},{3,1},{4,6},{5,7},{6,4},{7,5},{8,10},{9,11},{10,... | collective-permute-start | bytes 393224 | tf_op jit(solution)/shard_map/ppermute | solution.py:213
  12.1 8.4 %collective-permute-start.10 = (bf16[256,256]{1,0:T(8,128)(2,1)S(1)}, bf16[256,256]{1,0:T(8,128)(2,1)S(1)}, u32[]{:S(2)}, u32[]{:S(2)}) collective-permute-start(bf16[256,256]{1,0:T(8,128)(2,1)S(1)} %get-tuple-element.46.pixel_ref.refs_15_), channel_id=1, source_target_pairs={{0,4},{1,5},{2,6},{3,7},{4,0},{5,1},{6,2},{7,3},{8,12},{9,13},{10,... | collective-permute-start | bytes 393224 | tf_op jit(solution)/shard_map/ppermute | solution.py:213
  14.6 12.9 %collective-permute-start.6 = (bf16[256,256]{1,0:T(8,128)(2,1)S(1)}, bf16[256,256]{1,0:T(8,128)(2,1)S(1)}, u32[]{:S(2)}, u32[]{:S(2)}) collective-permute-start(bf16[256,256]{1,0:T(8,128)(2,1)S(1)} %get-tuple-element.46.pixel_ref.refs_15_), channel_id=1, source_target_pairs={{0,8},{1,9},{2,10},{3,11},{4,12},{5,13},{6,14},{7,15},{8,0},{9,1},... | collective-permute-start | bytes 393224 | tf_op jit(solution)/shard_map/ppermute | solution.py:213
  16.0 12.2 %collective-permute-start = (bf16[256,256]{1,0:T(8,128)(2,1)S(1)}, bf16[256,256]{1,0:T(8,128)(2,1)S(1)}, u32[]{:S(2)}, u32[]{:S(2)}) collective-permute-start(bf16[256,256]{1,0:T(8,128)(2,1)S(1)} %get-tuple-element.46.pixel_ref.refs_15_), channel_id=1, source_target_pairs={{0,12},{1,13},{2,14},{3,15},{4,8},{5,9},{6,10},{7,11},{8,4},{9,5},... | collective-permute-start | bytes 393224 | tf_op jit(solution)/shard_map/ppermute | solution.py:213
  17.1 12.4 %collective-permute-start.1 = (bf16[256,256]{1,0:T(8,128)(2,1)S(1)}, bf16[256,256]{1,0:T(8,128)(2,1)S(1)}, u32[]{:S(2)}, u32[]{:S(2)}) collective-permute-start(bf16[256,256]{1,0:T(8,128)(2,1)S(1)} %get-tuple-element.47.dates_ref), channel_id=1, source_target_pairs={{0,1},{1,0},{2,3},{3,2},{4,5},{5,4},{6,7},{7,6},{8,9},{9,8},{10,11... | collective-permute-start | bytes 393224 | tf_op jit(solution)/shard_map/ppermute | solution.py:213
  20.4 10.6 %collective-permute-start.11 = (bf16[256,256]{1,0:T(8,128)(2,1)S(1)}, bf16[256,256]{1,0:T(8,128)(2,1)S(1)}, u32[]{:S(2)}, u32[]{:S(2)}) collective-permute-start(bf16[256,256]{1,0:T(8,128)(2,1)S(1)} %collective-permute-done.10.pixel_ref.refs_13_), channel_id=1, source_target_pairs={{0,2},{1,3},{2,0},{3,1},{4,6},{5,7},{6,4},{7,5},{8,10},{9,11},{10,... | collective-permute-start | bytes 393224 | tf_op jit(solution)/shard_map/ppermute | solution.py:213
  28.3 8.4 %collective-permute-start.3 = (bf16[256,256]{1,0:T(8,128)(2,1)S(1)}, bf16[256,256]{1,0:T(8,128)(2,1)S(1)}, u32[]{:S(2)}, u32[]{:S(2)}) collective-permute-start(bf16[256,256]{1,0:T(8,128)(2,1)S(1)} %collective-permute-done.pixel_ref.refs_9_), channel_id=1, source_target_pairs={{0,2},{1,3},{2,0},{3,1},{4,6},{5,7},{6,4},{7,5},{8,10},{9,11},{10,... | collective-permute-start | bytes 393224 | tf_op jit(solution)/shard_map/ppermute | solution.py:213
  30.2 9.3 %collective-permute-start.15 = (bf16[256,256]{1,0:T(8,128)(2,1)S(1)}, bf16[256,256]{1,0:T(8,128)(2,1)S(1)}, u32[]{:S(2)}, u32[]{:S(2)}) collective-permute-start(bf16[256,256]{1,0:T(8,128)(2,1)S(1)} %get-tuple-element.56), channel_id=1, source_target_pairs={{0,2},{1,3},{2,0},{3,1},{4,6},{5,7},{6,4},{7,5},{8,10},{9,11},{10,... | collective-permute-start | bytes 393224 | tf_op jit(solution)/shard_map/ppermute | solution.py:213
  31.7 9.3 %collective-permute-start.12 = (bf16[256,256]{1,0:T(8,128)(2,1)S(1)}, bf16[256,256]{1,0:T(8,128)(2,1)S(1)}, u32[]{:S(2)}, u32[]{:S(2)}) collective-permute-start(bf16[256,256]{1,0:T(8,128)(2,1)S(1)} %get-tuple-element.54), channel_id=1, source_target_pairs={{0,2},{1,3},{2,0},{3,1},{4,6},{5,7},{6,4},{7,5},{8,10},{9,11},{10,... | collective-permute-start | bytes 393224 | tf_op jit(solution)/shard_map/ppermute | solution.py:213
  34.5 7.9 %collective-permute-start.8 = (bf16[256,256]{1,0:T(8,128)(2,1)S(1)}, bf16[256,256]{1,0:T(8,128)(2,1)S(1)}, u32[]{:S(2)}, u32[]{:S(2)}) collective-permute-start(bf16[256,256]{1,0:T(8,128)(2,1)S(1)} %get-tuple-element.52), channel_id=1, source_target_pairs={{0,2},{1,3},{2,0},{3,1},{4,6},{5,7},{6,4},{7,5},{8,10},{9,11},{10,... | collective-permute-start | bytes 393224 | tf_op jit(solution)/shard_map/ppermute | solution.py:213
  37.3 6.5 %collective-permute-start.4 = (bf16[256,256]{1,0:T(8,128)(2,1)S(1)}, bf16[256,256]{1,0:T(8,128)(2,1)S(1)}, u32[]{:S(2)}, u32[]{:S(2)}) collective-permute-start(bf16[256,256]{1,0:T(8,128)(2,1)S(1)} %get-tuple-element.50), channel_id=1, source_target_pairs={{0,2},{1,3},{2,0},{3,1},{4,6},{5,7},{6,4},{7,5},{8,10},{9,11},{10,... | collective-permute-start | bytes 393224 | tf_op jit(solution)/shard_map/ppermute | solution.py:213
  45.2 8.5 %collective-permute-start.13 = (bf16[256,256]{1,0:T(8,128)(2,1)S(1)}, bf16[256,256]{1,0:T(8,128)(2,1)S(1)}, u32[]{:S(2)}, u32[]{:S(2)}) collective-permute-start(bf16[256,256]{1,0:T(8,128)(2,1)S(1)} %get-tuple-element.55), channel_id=1, source_target_pairs={{0,4},{1,5},{2,6},{3,7},{4,0},{5,1},{6,2},{7,3},{8,12},{9,13},{10,... | collective-permute-start | bytes 393224 | tf_op jit(solution)/shard_map/ppermute | solution.py:213
  47.6 12.9 %collective-permute-start.9 = (bf16[256,256]{1,0:T(8,128)(2,1)S(1)}, bf16[256,256]{1,0:T(8,128)(2,1)S(1)}, u32[]{:S(2)}, u32[]{:S(2)}) collective-permute-start(bf16[256,256]{1,0:T(8,128)(2,1)S(1)} %get-tuple-element.53), channel_id=1, source_target_pairs={{0,8},{1,9},{2,10},{3,11},{4,12},{5,13},{6,14},{7,15},{8,0},{9,1},... | collective-permute-start | bytes 393224 | tf_op jit(solution)/shard_map/ppermute | solution.py:213
  49.7 10.8 %collective-permute-start.5 = (bf16[256,256]{1,0:T(8,128)(2,1)S(1)}, bf16[256,256]{1,0:T(8,128)(2,1)S(1)}, u32[]{:S(2)}, u32[]{:S(2)}) collective-permute-start(bf16[256,256]{1,0:T(8,128)(2,1)S(1)} %get-tuple-element.51), channel_id=1, source_target_pairs={{0,12},{1,13},{2,14},{3,15},{4,8},{5,9},{6,10},{7,11},{8,4},{9,5},... | collective-permute-start | bytes 393224 | tf_op jit(solution)/shard_map/ppermute | solution.py:213
  50.1 15.6 %collective-permute-start.18 = (bf16[256,256]{1,0:T(8,128)(2,1)S(1)}, bf16[256,256]{1,0:T(8,128)(2,1)S(1)}, u32[]{:S(2)}, u32[]{:S(2)}) collective-permute-start(bf16[256,256]{1,0:T(8,128)(2,1)S(1)} %add_convert_fusion.1), channel_id=1, source_target_pairs={{0,16},{16,0},{1,17},{17,1},{2,18},{18,2},{3,19},{19,3},{4,20},{20... | collective-permute-start | bytes 393224 | tf_op jit(solution)/shard_map/ppermute | solution.py:213
  60.6 15.7 %collective-permute-start.27 = (bf16[256,256]{1,0:T(8,128)(2,1)S(1)}, bf16[256,256]{1,0:T(8,128)(2,1)S(1)}, u32[]{:S(2)}, u32[]{:S(2)}) collective-permute-start(bf16[256,256]{1,0:T(8,128)(2,1)S(1)} %get-tuple-element.59.pixel_ref.refs_15_), channel_id=1, source_target_pairs={{0,4},{1,5},{2,6},{3,7},{4,0},{5,1},{6,2},{7,3},{8,12},{9,13},{10,... | collective-permute-start | bytes 393224 | tf_op jit(solution)/shard_map/ppermute | solution.py:213
  63.3 12.3 %collective-permute-start.23 = (bf16[256,256]{1,0:T(8,128)(2,1)S(1)}, bf16[256,256]{1,0:T(8,128)(2,1)S(1)}, u32[]{:S(2)}, u32[]{:S(2)}) collective-permute-start(bf16[256,256]{1,0:T(8,128)(2,1)S(1)} %get-tuple-element.59.pixel_ref.refs_15_), channel_id=1, source_target_pairs={{0,8},{1,9},{2,10},{3,11},{4,12},{5,13},{6,14},{7,15},{8,0},{9,1},... | collective-permute-start | bytes 393224 | tf_op jit(solution)/shard_map/ppermute | solution.py:213
  64.0 9.7 %collective-permute-start.16 = (bf16[256,256]{1,0:T(8,128)(2,1)S(1)}, bf16[256,256]{1,0:T(8,128)(2,1)S(1)}, u32[]{:S(2)}, u32[]{:S(2)}) collective-permute-start(bf16[256,256]{1,0:T(8,128)(2,1)S(1)} %get-tuple-element.59.pixel_ref.refs_15_), channel_id=1, source_target_pairs={{0,12},{1,13},{2,14},{3,15},{4,8},{5,9},{6,10},{7,11},{8,4},{9,5},... | collective-permute-start | bytes 393224 | tf_op jit(solution)/shard_map/ppermute | solution.py:213
  65.8 12.5 %collective-permute-start.19 = (bf16[256,256]{1,0:T(8,128)(2,1)S(1)}, bf16[256,256]{1,0:T(8,128)(2,1)S(1)}, u32[]{:S(2)}, u32[]{:S(2)}) collective-permute-start(bf16[256,256]{1,0:T(8,128)(2,1)S(1)} %fusion.dates_ref), channel_id=1, source_target_pairs={{0,1},{1,0},{2,3},{3,2},{4,5},{5,4},{6,7},{7,6},{8,9},{9,8},{10,11... | collective-permute-start | bytes 393224 | tf_op jit(solution)/shard_map/ppermute | solution.py:213
  73.7 6.4 %collective-permute-start.20 = (bf16[256,256]{1,0:T(8,128)(2,1)S(1)}, bf16[256,256]{1,0:T(8,128)(2,1)S(1)}, u32[]{:S(2)}, u32[]{:S(2)}) collective-permute-start(bf16[256,256]{1,0:T(8,128)(2,1)S(1)} %collective-permute-done.16.pixel_ref.refs_9_), channel_id=1, source_target_pairs={{0,2},{1,3},{2,0},{3,1},{4,6},{5,7},{6,4},{7,5},{8,10},{9,11},{10,... | collective-permute-start | bytes 393224 | tf_op jit(solution)/shard_map/ppermute | solution.py:213
  75.5 7.4 %collective-permute-start.24 = (bf16[256,256]{1,0:T(8,128)(2,1)S(1)}, bf16[256,256]{1,0:T(8,128)(2,1)S(1)}, u32[]{:S(2)}, u32[]{:S(2)}) collective-permute-start(bf16[256,256]{1,0:T(8,128)(2,1)S(1)} %collective-permute-done.23.pixel_ref.refs_11_), channel_id=1, source_target_pairs={{0,2},{1,3},{2,0},{3,1},{4,6},{5,7},{6,4},{7,5},{8,10},{9,11},{10,... | collective-permute-start | bytes 393224 | tf_op jit(solution)/shard_map/ppermute | solution.py:213
  76.3 9.5 %collective-permute-start.28 = (bf16[256,256]{1,0:T(8,128)(2,1)S(1)}, bf16[256,256]{1,0:T(8,128)(2,1)S(1)}, u32[]{:S(2)}, u32[]{:S(2)}) collective-permute-start(bf16[256,256]{1,0:T(8,128)(2,1)S(1)} %collective-permute-done.27.pixel_ref.refs_13_), channel_id=1, source_target_pairs={{0,2},{1,3},{2,0},{3,1},{4,6},{5,7},{6,4},{7,5},{8,10},{9,11},{10,... | collective-permute-start | bytes 393224 | tf_op jit(solution)/shard_map/ppermute | solution.py:213
  77.6 11.0 %collective-permute-start.31 = (bf16[256,256]{1,0:T(8,128)(2,1)S(1)}, bf16[256,256]{1,0:T(8,128)(2,1)S(1)}, u32[]{:S(2)}, u32[]{:S(2)}) collective-permute-start(bf16[256,256]{1,0:T(8,128)(2,1)S(1)} %get-tuple-element.59.pixel_ref.refs_15_), channel_id=1, source_target_pairs={{0,2},{1,3},{2,0},{3,1},{4,6},{5,7},{6,4},{7,5},{8,10},{9,11},{10,... | collective-permute-start | bytes 393224 | tf_op jit(solution)/shard_map/ppermute | solution.py:213
  80.8 10.6 %collective-permute-start.21 = (bf16[256,256]{1,0:T(8,128)(2,1)S(1)}, bf16[256,256]{1,0:T(8,128)(2,1)S(1)}, u32[]{:S(2)}, u32[]{:S(2)}) collective-permute-start(bf16[256,256]{1,0:T(8,128)(2,1)S(1)} %get-tuple-element.70), channel_id=1, source_target_pairs={{0,2},{1,3},{2,0},{3,1},{4,6},{5,7},{6,4},{7,5},{8,10},{9,11},{10,... | collective-permute-start | bytes 393224 | tf_op jit(solution)/shard_map/ppermute | solution.py:213
  83.6 10.5 %collective-permute-start.25 = (bf16[256,256]{1,0:T(8,128)(2,1)S(1)}, bf16[256,256]{1,0:T(8,128)(2,1)S(1)}, u32[]{:S(2)}, u32[]{:S(2)}) collective-permute-start(bf16[256,256]{1,0:T(8,128)(2,1)S(1)} %get-tuple-element.72), channel_id=1, source_target_pairs={{0,2},{1,3},{2,0},{3,1},{4,6},{5,7},{6,4},{7,5},{8,10},{9,11},{10,... | collective-permute-start | bytes 393224 | tf_op jit(solution)/shard_map/ppermute | solution.py:213
  86.4 9.1 %collective-permute-start.29 = (bf16[256,256]{1,0:T(8,128)(2,1)S(1)}, bf16[256,256]{1,0:T(8,128)(2,1)S(1)}, u32[]{:S(2)}, u32[]{:S(2)}) collective-permute-start(bf16[256,256]{1,0:T(8,128)(2,1)S(1)} %get-tuple-element.74), channel_id=1, source_target_pairs={{0,2},{1,3},{2,0},{3,1},{4,6},{5,7},{6,4},{7,5},{8,10},{9,11},{10,... | collective-permute-start | bytes 393224 | tf_op jit(solution)/shard_map/ppermute | solution.py:213
  89.2 7.7 %collective-permute-start.32 = (bf16[256,256]{1,0:T(8,128)(2,1)S(1)}, bf16[256,256]{1,0:T(8,128)(2,1)S(1)}, u32[]{:S(2)}, u32[]{:S(2)}) collective-permute-start(bf16[256,256]{1,0:T(8,128)(2,1)S(1)} %get-tuple-element.76), channel_id=1, source_target_pairs={{0,2},{1,3},{2,0},{3,1},{4,6},{5,7},{6,4},{7,5},{8,10},{9,11},{10,... | collective-permute-start | bytes 393224 | tf_op jit(solution)/shard_map/ppermute | solution.py:213
  98.4 7.8 %collective-permute-start.22 = (bf16[256,256]{1,0:T(8,128)(2,1)S(1)}, bf16[256,256]{1,0:T(8,128)(2,1)S(1)}, u32[]{:S(2)}, u32[]{:S(2)}) collective-permute-start(bf16[256,256]{1,0:T(8,128)(2,1)S(1)} %get-tuple-element.71), channel_id=1, source_target_pairs={{0,12},{1,13},{2,14},{3,15},{4,8},{5,9},{6,10},{7,11},{8,4},{9,5},... | collective-permute-start | bytes 393224 | tf_op jit(solution)/shard_map/ppermute | solution.py:213
  100.2 14.3 %collective-permute-start.26 = (bf16[256,256]{1,0:T(8,128)(2,1)S(1)}, bf16[256,256]{1,0:T(8,128)(2,1)S(1)}, u32[]{:S(2)}, u32[]{:S(2)}) collective-permute-start(bf16[256,256]{1,0:T(8,128)(2,1)S(1)} %get-tuple-element.73), channel_id=1, source_target_pairs={{0,8},{1,9},{2,10},{3,11},{4,12},{5,13},{6,14},{7,15},{8,0},{9,1},... | collective-permute-start | bytes 393224 | tf_op jit(solution)/shard_map/ppermute | solution.py:213
  104.5 10.0 %collective-permute-start.30 = (bf16[256,256]{1,0:T(8,128)(2,1)S(1)}, bf16[256,256]{1,0:T(8,128)(2,1)S(1)}, u32[]{:S(2)}, u32[]{:S(2)}) collective-permute-start(bf16[256,256]{1,0:T(8,128)(2,1)S(1)} %get-tuple-element.75), channel_id=1, source_target_pairs={{0,4},{1,5},{2,6},{3,7},{4,0},{5,1},{6,2},{7,3},{8,12},{9,13},{10,... | collective-permute-start | bytes 393224 | tf_op jit(solution)/shard_map/ppermute | solution.py:213
  104.5 10.8 %collective-permute-start.34 = (bf16[256,256]{1,0:T(8,128)(2,1)S(1)}, bf16[256,256]{1,0:T(8,128)(2,1)S(1)}, u32[]{:S(2)}, u32[]{:S(2)}) collective-permute-start(bf16[256,256]{1,0:T(8,128)(2,1)S(1)} %add_convert_fusion), channel_id=1, source_target_pairs={{0,16},{16,0},{1,17},{17,1},{2,18},{18,2},{3,19},{19,3},{4,20},{20... | collective-permute-start | bytes 393224 | tf_op jit(solution)/shard_map/ppermute | solution.py:213
  (8 other events, 36.1 us)

commit v2 on v1

v2 whole, which is shorter than its diff:
```python
import functools

import jax
import jax.numpy as jnp
from jax import lax
from jax.experimental import pallas as pl
from jax.experimental.pallas import tpu as pltpu
from jax.sharding import PartitionSpec as P

STEPS = 2
DECAY = 0.05
STEP_SCALE = 48.0
BLOCK_ROWS = 128
BLOCK_DATES = 64
LANES = 128
GROUP = 16
F32 = jnp.float32
BF16 = jnp.bfloat16
VMEM = pl.BlockSpec(memory_space=pltpu.VMEM)
HBM = pl.BlockSpec(memory_space=pltpu.HBM)
ANY = pl.BlockSpec(memory_space=pl.ANY)
SMEM = pl.BlockSpec(memory_space=pltpu.SMEM)


def params(mib):
    return pltpu.CompilerParams(vmem_limit_bytes=mib << 20)


def cost(flops, bytes_accessed):
    return pl.CostEstimate(flops=flops, bytes_accessed=bytes_accessed, transcendentals=0)


def row_pieces(rows):
    half = BLOCK_ROWS // 2
    for block in range(rows // BLOCK_ROWS):
        for odd in range(2):
            yield block * BLOCK_ROWS + odd * half, pl.ds(block * BLOCK_ROWS + odd, half, stride=2), half


def prepare_kernel(pixel_ref, date_ref, pixel_now_ref, pixel_bf_ref, date_bf_ref, slab):
    rows, rank = pixel_ref.shape
    for lane in range(0, rank, LANES):
        slab[lane // LANES] = pixel_ref[:, lane : lane + LANES]
    for to, source, half in row_pieces(rows):
        for lane in range(0, rank, LANES):
            piece = slab[lane // LANES, source, :]
            pixel_now_ref[to : to + half, lane : lane + LANES] = piece
            pixel_bf_ref[to : to + half, lane : lane + LANES] = piece.astype(BF16)
    date_bf_ref[...] = date_ref[...].astype(BF16)


def place_kernel(chip_blocks, place_ref, *refs):
    ids_refs, count_refs, block_refs = refs[0:2], refs[2:4], (refs[4:6], refs[6:8])
    panel_ref, raw, flat, sems = refs[-4:]
    slots, size = block_refs[0][0].shape
    tiles = size // LANES
    core_blocks = chip_blocks // 2
    chip, core = place_ref[0], place_ref[1]
    spare = panel_ref.shape[1] - tiles
    width = panel_ref.shape[2] // 2

    def load(k, g, which):
        rows = pl.ds(pl.multiple_of(g * GROUP, GROUP), GROUP)
        return pltpu.make_async_copy(block_refs[k][which].at[rows], raw.at[k, which, rows], sems.at[k, which, g])

    for k in range(2):
        for g in range(slots // GROUP):
            for which in range(2):
                load(k, g, which).start()
    panel_ref[...] = jnp.zeros_like(panel_ref)

    for k in range(2):
        count = count_refs[k][0, 0]

        def group(g, carry, k=k, count=count):
            first = pl.multiple_of(g * GROUP, GROUP)
            for which in range(2):
                load(k, g, which).wait()

            @pl.when(first < count)
            def _():
                for which in range(2):
                    for t in range(tiles):
                        flat[which, t * GROUP : (t + 1) * GROUP, :] = raw[
                            k, which, pl.ds(first, GROUP), t * LANES : (t + 1) * LANES
                        ].astype(F32)
                for s in range(GROUP):
                    row_block, date_block = ids_refs[k][0, first + s], ids_refs[k][1, first + s]
                    target = lax.bitwise_xor(lax.div(row_block, chip_blocks), chip)
                    inside = lax.rem(row_block, chip_blocks)
                    wanted = jnp.logical_and(lax.div(inside, core_blocks) == core, first + s < count)
                    row = (target * core_blocks + lax.rem(inside, core_blocks)) * tiles
                    row = pl.multiple_of(jnp.where(wanted, row, spare), tiles)
                    lane = pl.multiple_of(k * width + date_block * LANES, LANES)
                    for which in range(2):
                        tile = flat[which, pl.ds(s, tiles, stride=GROUP), :]
                        panel_ref[which, pl.ds(row, tiles), pl.ds(lane, LANES)] = tile.astype(BF16)

            return carry

        lax.fori_loop(0, slots // GROUP, group, 0)


def apart(ref, which, first, rows, lane, width):
    low = lax.broadcasted_iota(jnp.int32, (rows, LANES), 1) < BLOCK_DATES
    even, odd = [], []
    for at in range(lane, lane + width, 2 * LANES):
        a = ref[which, first : first + rows, at : at + LANES].astype(F32)
        b = ref[which, first : first + rows, at + LANES : at + 2 * LANES].astype(F32)
        even.append(jnp.where(low, a, pltpu.roll(b, BLOCK_DATES, 1)))
        odd.append(jnp.where(low, pltpu.roll(a, BLOCK_DATES, 1), b))
    return jnp.concatenate([jnp.concatenate(even, axis=1), jnp.concatenate(odd, axis=1)], axis=0)


def chunk_kernel(n, n_recv, n_after, *refs):
    pixel_refs, (dates_ref, dates_other_ref, panel_ref) = refs[:n], refs[n : n + 3]
    recv_refs, (term_ref, errors_ref) = refs[n + 3 : n + 3 + n_recv], refs[-2:]
    width = panel_ref.shape[2] // 2
    half = BLOCK_ROWS // 2
    local = dates_ref.shape[0]
    blocks = pixel_refs[0].shape[0] // BLOCK_ROWS
    for block in range(n * blocks):
        inside = slice(block % blocks * BLOCK_ROWS, (block % blocks + 1) * BLOCK_ROWS)
        rows = slice(block * BLOCK_ROWS, (block + 1) * BLOCK_ROWS)
        total = None
        for k, dates in enumerate((dates_ref, dates_other_ref)):
            predicted = lax.dot_general(
                pixel_refs[block // blocks][inside, :], dates[...],
                (((1,), (1,)), ((), ())), preferred_element_type=F32,
            )
            observed = apart(panel_ref, 0, block * half, half, k * width, width)
            weights = apart(panel_ref, 1, block * half, half, k * width, width)
            errors = (weights * (predicted - observed)).astype(BF16)
            errors_ref[rows, k * local : (k + 1) * local] = errors
            term = jnp.dot(errors, dates[...], preferred_element_type=F32)
            total = term if total is None else total + term
        for ref in recv_refs:
            total = total + ref[rows, :].astype(F32)
        term_ref[rows, :] = total.astype(term_ref.dtype)


def chunk(pixels, dates_bf, dates_other, panel, at, recv, kind, after):
    rows, rank = pixels[0].shape
    local = dates_bf.shape[0]
    n = len(pixels)
    whole = lambda a: pl.BlockSpec(a.shape, lambda i: (0,) * a.ndim)
    block = lambda at: pl.BlockSpec((rows, rank), lambda i: (at, 0))
    return pl.pallas_call(
        functools.partial(chunk_kernel, n, len(recv), len(after)),
        grid=(1,),
        out_shape=(
            jax.ShapeDtypeStruct((n * rows, rank), kind),
            jax.ShapeDtypeStruct((n * rows, 2 * local), BF16),
        ),
        in_specs=[whole(p) for p in pixels] + [whole(dates_bf), whole(dates_other), pl.BlockSpec((2, n * rows // 2, panel.shape[2]), lambda i: (0, at, 0))]
        + [block(at) for _, at in recv] + [ANY] * len(after),
        out_specs=(block(0) if n == 1 else pl.BlockSpec((n * rows, rank), lambda i: (0, 0)),
                   pl.BlockSpec((n * rows, 2 * local), lambda i: (0, 0))),
        compiler_params=params(24),
        cost_estimate=cost(8 * n * rows * rank * local, n * 1200000),
    )(*pixels, dates_bf, dates_other, panel, *[r for r, _ in recv], *after)


def hold_kernel(x_ref, after_ref, out_ref):
    out_ref[...] = x_ref[...]


def hold(x, after):
    return pl.pallas_call(
        hold_kernel,
        out_shape=jax.ShapeDtypeStruct(x.shape, x.dtype),
        in_specs=[VMEM, ANY],
        out_specs=VMEM,
        compiler_params=params(16),
        cost_estimate=cost(x.size, 4 * x.size),
    )(x, after)


def date_kernel(starts, *refs):
    n = len(starts)
    pixel_refs, errors_refs, (own_ref, other_ref) = refs[:n], refs[n:-2], refs[-2:]
    local = own_ref.shape[0]
    for k, out in enumerate((own_ref, other_ref)):
        total = None
        for (which, start), pixels in zip(starts, pixel_refs):
            errors = errors_refs[which][start : start + pixels.shape[0], k * local : (k + 1) * local]
            term = lax.dot_general(errors, pixels[...], (((0,), (0,)), ((), ())), preferred_element_type=F32)
            total = term if total is None else total + term
        out[...] = total.astype(out.dtype)


def date_gradient(errors, pixels, starts, local, after):
    rank = pixels[0].shape[1]
    n = len(pixels)
    return pl.pallas_call(
        functools.partial(date_kernel, starts),
        out_shape=(jax.ShapeDtypeStruct((local, rank), BF16),) * 2,
        in_specs=[VMEM] * (n + len(errors)) + [ANY] * len(after),
        out_specs=(VMEM, VMEM),
        compiler_params=params(32),
        cost_estimate=cost(4 * n * pixels[0].shape[0] * rank * local, n * 400000),
    )(*pixels, *errors, *after)


def sum_kernel(*refs):
    parts, out_ref = refs[:-1], refs[-1]
    total = parts[0][...].astype(F32)
    for part in parts[1:]:
        total = total + part[...].astype(F32)
    out_ref[...] = total


def pixel_kernel(scale, last, now_ref, *rest):
    parts, outs = rest[:-2], rest[-2:]
    rows, rank = now_ref.shape
    for start, target, half in row_pieces(rows):
        for lane in range(0, rank, LANES):
            at = (slice(start, start + half), slice(lane, lane + LANES))
            grad = parts[0][at].astype(F32)
            for part in parts[1:]:
                grad = grad + part[at].astype(F32)
            new = (1.0 - DECAY) * now_ref[at] - scale * grad
            if last:
                outs[1][lane // LANES, target, :] = new
            else:
                outs[0][at] = new
                outs[1][at] = new.astype(BF16)
    if last:
        for lane in range(0, rank, LANES):
            outs[0][:, lane : lane + LANES] = outs[1][lane // LANES]


def pixel_update(scale, last, now, parts):
    full = jax.ShapeDtypeStruct(now.shape, F32)
    first = pl.BlockSpec(now.shape, lambda i: (0, 0))
    early = pl.pallas_call(
        sum_kernel,
        grid=(1,),
        out_shape=full,
        in_specs=[first] * (len(parts) - 1),
        out_specs=first,
        compiler_params=params(16),
        cost_estimate=cost(4 * now.size, 8 * now.size),
    )(*parts[:-1])
    return pl.pallas_call(
        functools.partial(pixel_kernel, scale, last),
        out_shape=(full,) if last else (full, jax.ShapeDtypeStruct(now.shape, BF16)),
        in_specs=[VMEM] * 3,
        out_specs=(VMEM,) if last else (VMEM, VMEM),
        scratch_shapes=[pltpu.VMEM((now.shape[1] // LANES, now.shape[0], LANES), F32)] if last else [],
        compiler_params=params(16),
        cost_estimate=cost(10 * now.size, 8 * now.size),
    )(now, early, parts[-1])


def date_update_kernel(scale, now_ref, *refs):
    parts, (after_ref, new_ref, bf_ref) = refs[:-3], refs[-3:]
    halves = [None, None]
    for i, part in enumerate(parts):
        side = 2 * i // len(parts)
        value = part[...].astype(F32)
        halves[side] = value if halves[side] is None else halves[side] + value
    new = (1.0 - DECAY) * now_ref[...] - scale * (halves[0] + halves[1])
    new_ref[...] = new
    bf_ref[...] = new.astype(BF16)


def date_update(scale, now, parts, after):
    return pl.pallas_call(
        functools.partial(date_update_kernel, scale),
        out_shape=(jax.ShapeDtypeStruct(now.shape, F32), jax.ShapeDtypeStruct(now.shape, BF16)),
        in_specs=[VMEM] * (1 + len(parts)) + [ANY],
        out_specs=(VMEM, VMEM),
        compiler_params=params(16),
        cost_estimate=cost(8 * now.size, 8 * now.size),
    )(now, *parts, after)


def shards(pixel_factors, date_factors, block_ids, block_counts, block_values, block_weights):
    loop_size, groups = lax.axis_size("date"), lax.axis_size("pix")
    own_rows, rank = pixel_factors.shape
    local = date_factors.shape[0]
    chips = loop_size // 2
    high = 4
    low = chips // high
    all_pixels = own_rows * loop_size * groups
    all_dates = local * loop_size
    slots, flat = block_values.shape[2:]
    me = lax.axis_index("date")
    tiles = flat // LANES
    core_blocks = own_rows // BLOCK_ROWS

    def swap(x, mask, axis="date"):
        return lax.ppermute(x, axis, [(i, i ^ mask) for i in range(lax.axis_size(axis))])

    shape = jax.ShapeDtypeStruct
    pixel_now, pixel_bf, dates_bf = pl.pallas_call(
        prepare_kernel,
        out_shape=(shape((own_rows, rank), F32), shape((own_rows, rank), BF16), shape((local, rank), BF16)),
        in_specs=[VMEM, VMEM],
        out_specs=(VMEM, VMEM, VMEM),
        scratch_shapes=[pltpu.VMEM((rank // LANES, own_rows, LANES), F32)],
        compiler_params=params(16),
        cost_estimate=cost(own_rows * rank, own_rows * rank * 16),
    )(pixel_factors, date_factors)
    dates_now = date_factors
    dates_other = swap(dates_bf, 1)

    rows, width = chips * core_blocks * tiles, local // BLOCK_DATES * LANES
    ids, values, weights = (
        block_ids.reshape(2, slots), block_values.reshape(slots, flat), block_weights.reshape(slots, flat)
    )
    panel = pl.pallas_call(
        functools.partial(place_kernel, 2 * core_blocks),
        out_shape=shape((2, rows + tiles, 2 * width), BF16),
        in_specs=[SMEM] * 5 + [HBM] * 4,
        out_specs=VMEM,
        scratch_shapes=[
            pltpu.VMEM((2, 2, slots, flat), BF16),
            pltpu.VMEM((2, tiles * GROUP, LANES), F32),
            pltpu.SemaphoreType.DMA((2, 2, slots // GROUP)),
        ],
        compiler_params=params(36),
        cost_estimate=cost(slots * flat * 8, slots * flat * 8),
    )(
        jnp.stack([me // 2, me % 2]).astype(jnp.int32),
        ids, swap(ids, 1), block_counts, swap(block_counts, 1),
        values, weights, swap(values, 1), swap(weights, 1),
    )

    for step in range(STEPS):
        last = step == STEPS - 1
        far = range(1, low)
        along = [2 * low * hi for hi in range(high)]
        pixels = {(0, 0): pixel_bf}
        pixels[3, 0] = swap(pixel_bf, along[3])
        for lo in far:
            pixels[0, lo] = swap(pixel_bf, 2 * lo)
        pixels[1, 0] = swap(pixel_bf, along[1])
        pixels[2, 0] = swap(hold(pixel_bf, pixels[0, 1]), along[2])
        for lo in far:
            pixels[1, lo] = swap(pixels[1, 0], 2 * lo)
            pixels[3, lo] = swap(pixels[3, 0], 2 * lo)
            pixels[2, lo] = swap(pixels[2, 0], 2 * lo)
        errors, starts, ordered, after = [], [], [], []

        def terms(keys, recv, kind, errors=errors, starts=starts, ordered=ordered, dates_bf=dates_bf,
                  dates_other=dates_other, pixels=pixels):
            nonlocal after
            hi, lo = keys[0]
            n = len(keys)
            term, error = chunk(
                [pixels[k] for k in keys], dates_bf, dates_other, panel, (hi * low + lo) // n, recv, kind, after,
            )
            starts += [(len(errors), i * own_rows) for i in range(n)]
            errors.append(error)
            ordered += [pixels[k] for k in keys]
            after = [term]
            return term

        pair = swap(terms([(1, lo) for lo in range(low)], [], BF16), along[1])
        parts = [terms([(0, 0)], [], F32), pair]
        recv3 = [swap(terms([(3, lo)], [], BF16), 2 * lo) for lo in far]
        recv2 = [swap(terms([(2, lo)], [], BF16), 2 * lo) for lo in far]
        part3 = swap(terms([(3, 0)], [(r, 0) for r in recv3], BF16), along[3])
        parts += [swap(terms([(0, lo)], [(pair, lo)], BF16), 2 * lo) for lo in far]
        parts += [part3, swap(terms([(2, 0)], [(r, 0) for r in recv2], BF16), along[2])]
        own, partner = date_gradient(errors, ordered, tuple(starts), local, [])
        scale = STEP_SCALE / all_dates
        if last:
            (pixel_now,) = pixel_update(scale, True, pixel_now, parts)
        else:
            pixel_now, pixel_bf = pixel_update(scale, False, pixel_now, parts)
        sums = [own, swap(partner, 1)]
        if groups > 1:
            count = groups * loop_size
            across = [(i, i ^ (loop_size + 1)) for i in range(count)]
            sums += [swap(own, 1, "pix"), lax.ppermute(partner, ("pix", "date"), across)]
        mask = 2
        while mask < groups:
            left, right = sums[: len(sums) // 2], sums[len(sums) // 2 :]
            total = sum(x.astype(F32) for x in left) + sum(x.astype(F32) for x in right)
            sums = [total.astype(BF16)]
            sums.append(swap(sums[0], mask, "pix"))
            mask *= 2
        dates_now, dates_bf = date_update(
            STEP_SCALE / all_pixels, dates_now, sums, pixel_now if last else pixel_bf
        )
        if not last:
            dates_other = swap(dates_bf, 1)
    return (pixel_now, dates_now)


def solution(mesh):
    placed = (
        P(("pix", "date"), None),
        P("date", None),
        P("pix", "date", None, None),
        P("pix", "date"),
        P("pix", "date", None, None),
        P("pix", "date", None, None),
    )
    return jax.shard_map(
        shards,
        mesh=mesh,
        in_specs=placed,
        out_specs=(P(("pix", "date"), None), P("date", None)),
        check_vma=False,
    )
```

time: 116 us -> 96.6 us (0.83)
  waiting for transfers between devices: 54.5 us -> 31.4 us
  local copies, waits for them, and re-layouts: 3.32 us -> 6.87 us
  Pallas kernels: 15.7 us -> 18.7 us
  starting transfers between devices: 40 us -> 37.2 us
    ppermute x35 -> x36, waiting for transfers between devices: 54.5 us -> 29.9 us  [swap(): lax.ppermute(x, axis, [(i, i ^ mask) for i in range(lax.axis_size(axis))])]
    unnamed x10 -> x18, local copies, waits for them, and re-layouts: 3.32 us -> 6.87 us
    ppermute x35 -> x36, starting transfers between devices: 40 us -> 37.2 us  [swap(): lax.ppermute(x, axis, [(i, i ^ mask) for i in range(lax.axis_size(axis))])]
    pallas_call x1, Pallas kernels: 3.18 us -> 5.39 us  [shards(): pl.pallas_call(functools.partial(place_kernel, 2 * core_blocks), out_shap...]
    ppermute x0 -> x2, waiting for transfers between devices: none -> 1.52 us  [shards(): lax.ppermute(partner, ('pix', 'date'), across)]
    pallas_call x18 -> x22, Pallas kernels: 11.6 us -> 12.4 us  [the longest x14 9.86 us: chunk(): pl.pallas_call(functools.partial(chunk_kernel, n, len(recv), len(after)),...]
  transfers between devices with their start and end apart: 35 -> 38, of which waited for: 22 -> 13; matrix products, arithmetic and copies ran while one was open for 0% -> 0% of each run, Pallas kernels for 8% -> 19%
where the time goes in v2:
time: 96.6 us; the launch traced here: 95.8 us
  starting transfers between devices  37.2 us (39%)
  waiting for transfers between devices  31.4 us (33%)
  Pallas kernels  18.7 us (19%)
  local copies, waits for them, and re-layouts  6.87 us (7%)
  between operations  1.62 us (2%)
    ppermute x36, starting transfers between devices, swap(): lax.ppermute(x, axis, [(i, i ^ mask) for i in range(lax.axis_size(axis))])  37.2 us
    ppermute x36, waiting for transfers between devices, swap(): lax.ppermute(x, axis, [(i, i ^ mask) for i in range(lax.axis_size(axis))])  29.9 us
    pallas_call x14, Pallas kernels, chunk(): pl.pallas_call(functools.partial(chunk_kernel, n, len(recv), len(after)),...  9.86 us
    unnamed x18, local copies, waits for them, and re-layouts  6.87 us
    pallas_call x1, Pallas kernels, shards(): pl.pallas_call(functools.partial(place_kernel, 2 * core_blocks), out_shap...  5.39 us
  transfers between devices with their start and end apart: 38, of which 13 were waited for; matrix products, arithmetic and copies ran while one was open for 0% of the time, Pallas kernels for 19%

profile of v2, /device:TPU:0, one launch (start us, length us, event | category | flops | bytes accessed | tf_op | source)
XLA Modules:
  0.0 95.8 jit_solution(2346043108781344054)
XLA Ops:
  3.9 2.9 %collective-permute-start.8 = (bf16[256,256]{1,0:T(8,128)(2,1)S(1)}, bf16[256,256]{1,0:T(8,128)(2,1)S(1)}, u32[]{:S(2)}, u32[]{:S(2)}) collective-permute-start(bf16[256,256]{1,0:T(8,128)(2,1)S(1)} %get-tuple-element.43.refs_0_.x_ref.refs_2_), channel_id=1, source_target_pairs={{0,2},{1,3},{2,0},{3,1},{4,6},{5,7},{6,4},{7,5},{8,10},{9,11},{10,... | collective-permute-start | bytes 393224 | tf_op jit(solution)/shard_map/ppermute | solution.py:294
  6.8 1.6 %collective-permute-start.5 = (bf16[256,256]{1,0:T(8,128)(2,1)S(1)}, bf16[256,256]{1,0:T(8,128)(2,1)S(1)}, u32[]{:S(2)}, u32[]{:S(2)}) collective-permute-start(bf16[256,256]{1,0:T(8,128)(2,1)S(1)} %get-tuple-element.43.refs_0_.x_ref.refs_2_), channel_id=1, source_target_pairs={{0,4},{1,5},{2,6},{3,7},{4,0},{5,1},{6,2},{7,3},{8,12},{9,13},{10,... | collective-permute-start | bytes 393224 | tf_op jit(solution)/shard_map/ppermute | solution.py:294
  8.4 1.2 %collective-permute-done.2.refs_3_ = s32[1,1]{1,0:T(1,128)} collective-permute-done((s32[1,1]{1,0:T(1,128)}, s32[1,1]{1,0:T(1,128)}, u32[]{:S(2)}, u32[]{:S(2)}) %collective-permute-start.2) | collective-permute-done | bytes 36 | tf_op jit(solution)/shard_map/ppermute | solution.py:294
  9.9 1.1 %collective-permute-done.1.refs_1_ = s32[2,80]{1,0:T(2,128)S(1)} collective-permute-done((s32[2,80]{1,0:T(2,128)}, s32[2,80]{1,0:T(2,128)S(1)}, u32[]{:S(2)}, u32[]{:S(2)}) %collective-permute-start.1) | collective-permute-done | bytes 672 | tf_op jit(solution)/shard_map/ppermute | solution.py:294
  11.0 2.5 %collective-permute-start.9 = (bf16[256,256]{1,0:T(8,128)(2,1)S(1)}, bf16[256,256]{1,0:T(8,128)(2,1)S(1)}, u32[]{:S(2)}, u32[]{:S(2)}) collective-permute-start(bf16[256,256]{1,0:T(8,128)(2,1)S(1)} %get-tuple-element.43.refs_0_.x_ref.refs_2_), channel_id=1, source_target_pairs={{0,12},{1,13},{2,14},{3,15},{4,8},{5,9},{6,10},{7,11},{8,4},{9,5},... | collective-permute-start | bytes 393224 | tf_op jit(solution)/shard_map/ppermute | solution.py:294
  14.7 3.8 %collective-permute-done.9.refs_0_.refs_5_ = bf16[256,256]{1,0:T(8,128)(2,1)S(1)} collective-permute-done((bf16[256,256]{1,0:T(8,128)(2,1)S(1)}, bf16[256,256]{1,0:T(8,128)(2,1)S(1)}, u32[]{:S(2)}, u32[]{:S(2)}) %collective-permute-start.9) | collective-permute-done | bytes 131104 | tf_op jit(solution)/shard_map/ppermute | solution.py:294
  18.5 3.5 %collective-permute-start.12 = (bf16[256,256]{1,0:T(8,128)(2,1)S(1)}, bf16[256,256]{1,0:T(8,128)(2,1)S(1)}, u32[]{:S(2)}, u32[]{:S(2)}) collective-permute-start(bf16[256,256]{1,0:T(8,128)(2,1)S(1)} %shard_map.82), channel_id=1, source_target_pairs={{0,8},{1,9},{2,10},{3,11},{4,12},{5,13},{6,14},{7,15},{8,0},{9,1},... | collective-permute-start | bytes 393224 | tf_op jit(solution)/shard_map/ppermute | solution.py:294
  22.6 1.3 %copy-done = bf16[1,1,80,8192]{3,2,1,0:T(8,128)(2,1)S(1)} copy-done((bf16[1,1,80,8192]{3,2,1,0:T(8,128)(2,1)S(1)}, bf16[1,1,80,8192]{3,2,1,0:T(8,128)(2,1)}, u32[]{:S(2)}) %copy-start) | copy-done | bytes 1310744
  23.9 1.3 %copy-done.1 = bf16[1,1,80,8192]{3,2,1,0:T(8,128)(2,1)S(1)} copy-done((bf16[1,1,80,8192]{3,2,1,0:T(8,128)(2,1)S(1)}, bf16[1,1,80,8192]{3,2,1,0:T(8,128)(2,1)}, u32[]{:S(2)}) %copy-start.1) | copy-done | bytes 1310744
  25.9 5.4 %shard_map.78.refs_4_.refs_3_ = bf16[2,1088,1024]{2,1,0:T(8,128)(2,1)S(1)} custom-call(s32[2]{0:T(128)S(1)} %pad_add_fusion.place_ref, s32[2,80]{1,0:T(2,128)S(1)} %bitcast.10, s32[2,80]{1,0:T(2,128)S(1)} %collective-permute-done.1.refs_1_, s32[1,1]{1,0:T(1,128)S(6)} %copy.8.refs_2_, s32[1,1]{1,0:T(1,128)} %collective-permute-done.2.refs_3_, ...), custom_call_target="tpu_custom_call" | custom-call | flops 5242880 | bytes 5242880 | tf_op jit(solution)/shard_map/pallas_call | solution.py:313
  31.4 1.1 %shard_map.79 = (bf16[512,256]{1,0:T(8,128)(2,1)S(1)}, bf16[512,512]{1,0:T(8,128)(2,1)S(1)}) custom-call(bf16[256,256]{1,0:T(8,128)(2,1)S(1)} %collective-permute-done.5.refs_0_, bf16[256,256]{1,0:T(8,128)(2,1)S(1)} %collective-permute-done.6.refs_1_, bf16[256,256]{1,0:T(8,128)(2,1)S(1)} %get-tuple-element.44.refs_2_.refs_1_, ...), custom_call_target="tpu_custom_call" | custom-call | flops 268435456 | bytes 2400000 | tf_op jit(solution)/shard_map/pallas_call | solution.py:148
  32.6 2.0 %collective-permute-start.13 = (bf16[256,256]{1,0:T(8,128)(2,1)S(1)}, bf16[256,256]{1,0:T(8,128)(2,1)S(1)}, u32[]{:S(2)}, u32[]{:S(2)}) collective-permute-start(bf16[256,256]{1,0:T(8,128)(2,1)S(1)} %collective-permute-done.12.refs_0_.refs_7_), channel_id=1, source_target_pairs={{0,2},{1,3},{2,0},{3,1},{4,6},{5,7},{6,4},{7,5},{8,10},{9,11},{10,... | collective-permute-start | bytes 393224 | tf_op jit(solution)/shard_map/ppermute | solution.py:294
  36.0 2.1 %collective-permute-done.13.refs_0_.refs_4_ = bf16[256,256]{1,0:T(8,128)(2,1)S(1)} collective-permute-done((bf16[256,256]{1,0:T(8,128)(2,1)S(1)}, bf16[256,256]{1,0:T(8,128)(2,1)S(1)}, u32[]{:S(2)}, u32[]{:S(2)}) %collective-permute-start.13) | collective-permute-done | bytes 131104 | tf_op jit(solution)/shard_map/ppermute | solution.py:294
  38.8 2.2 %collective-permute-start.16 = (bf16[256,256]{1,0:T(8,128)(2,1)S(1)}, bf16[256,256]{1,0:T(8,128)(2,1)S(1)}, u32[]{:S(2)}, u32[]{:S(2)}) collective-permute-start(bf16[256,256]{1,0:T(8,128)(2,1)S(1)} %get-tuple-element.48.refs_5_), channel_id=1, source_target_pairs={{0,2},{1,3},{2,0},{3,1},{4,6},{5,7},{6,4},{7,5},{8,10},{9,11},{10,... | collective-permute-start | bytes 393224 | tf_op jit(solution)/shard_map/ppermute | solution.py:294
  42.5 1.6 %collective-permute-start.15 = (bf16[256,256]{1,0:T(8,128)(2,1)S(1)}, bf16[256,256]{1,0:T(8,128)(2,1)S(1)}, u32[]{:S(2)}, u32[]{:S(2)}) collective-permute-start(bf16[256,256]{1,0:T(8,128)(2,1)S(1)} %get-tuple-element.49.refs_5_), channel_id=1, source_target_pairs={{0,12},{1,13},{2,14},{3,15},{4,8},{5,9},{6,10},{7,11},{8,4},{9,5},... | collective-permute-start | bytes 393224 | tf_op jit(solution)/shard_map/ppermute | solution.py:294
  44.7 1.4 %collective-permute-start.14 = (bf16[256,256]{1,0:T(8,128)(2,1)S(1)}, bf16[256,256]{1,0:T(8,128)(2,1)S(1)}, u32[]{:S(2)}, u32[]{:S(2)}) collective-permute-start(bf16[256,256]{1,0:T(8,128)(2,1)S(1)} %get-tuple-element.50.refs_5_), channel_id=1, source_target_pairs={{0,2},{1,3},{2,0},{3,1},{4,6},{5,7},{6,4},{7,5},{8,10},{9,11},{10,... | collective-permute-start | bytes 393224 | tf_op jit(solution)/shard_map/ppermute | solution.py:294
  48.4 1.6 %collective-permute-start.19 = (bf16[256,256]{1,0:T(8,128)(2,1)S(1)}, bf16[256,256]{1,0:T(8,128)(2,1)S(1)}, u32[]{:S(2)}, u32[]{:S(2)}) collective-permute-start(bf16[256,256]{1,0:T(8,128)(2,1)S(1)} %get-tuple-element.61.refs_0_), channel_id=1, source_target_pairs={{0,16},{16,0},{1,17},{17,1},{2,18},{18,2},{3,19},{19,3},{4,20},{20... | collective-permute-start | bytes 393224 | tf_op jit(solution)/shard_map/ppermute | solution.py:294
  50.7 4.7 %collective-permute-done.17.rest_1_ = bf16[256,256]{1,0:T(8,128)(2,1)S(1)} collective-permute-done((bf16[256,256]{1,0:T(8,128)(2,1)S(1)}, bf16[256,256]{1,0:T(8,128)(2,1)S(1)}, u32[]{:S(2)}, u32[]{:S(2)}) %collective-permute-start.17) | collective-permute-done | bytes 131104 | tf_op jit(solution)/shard_map/ppermute | solution.py:294
  56.4 2.0 %collective-permute-start.26 = (bf16[256,256]{1,0:T(8,128)(2,1)S(1)}, bf16[256,256]{1,0:T(8,128)(2,1)S(1)}, u32[]{:S(2)}, u32[]{:S(2)}) collective-permute-start(bf16[256,256]{1,0:T(8,128)(2,1)S(1)} %get-tuple-element.53.refs_4_.refs_0_.x_ref.refs_2_), channel_id=1, source_target_pairs={{0,12},{1,13},{2,14},{3,15},{4,8},{5,9},{6,10},{7,11},{8,4},{9,5},... | collective-permute-start | bytes 393224 | tf_op jit(solution)/shard_map/ppermute | solution.py:294
  58.6 4.9 %collective-permute-done.22.refs_0_ = bf16[256,256]{1,0:T(8,128)(2,1)S(1)} collective-permute-done((bf16[256,256]{1,0:T(8,128)(2,1)S(1)}, bf16[256,256]{1,0:T(8,128)(2,1)S(1)}, u32[]{:S(2)}, u32[]{:S(2)}) %collective-permute-start.22) | collective-permute-done | bytes 131104 | tf_op jit(solution)/shard_map/ppermute | solution.py:294
  63.5 2.1 %collective-permute-start.27 = (bf16[256,256]{1,0:T(8,128)(2,1)S(1)}, bf16[256,256]{1,0:T(8,128)(2,1)S(1)}, u32[]{:S(2)}, u32[]{:S(2)}) collective-permute-start(bf16[256,256]{1,0:T(8,128)(2,1)S(1)} %collective-permute-done.26.refs_0_.refs_5_), channel_id=1, source_target_pairs={{0,2},{1,3},{2,0},{3,1},{4,6},{5,7},{6,4},{7,5},{8,10},{9,11},{10,... | collective-permute-start | bytes 393224 | tf_op jit(solution)/shard_map/ppermute | solution.py:294
  65.6 2.8 %collective-permute-done.23.refs_1_ = bf16[256,256]{1,0:T(8,128)(2,1)S(1)} collective-permute-done((bf16[256,256]{1,0:T(8,128)(2,1)S(1)}, bf16[256,256]{1,0:T(8,128)(2,1)S(1)}, u32[]{:S(2)}, u32[]{:S(2)}) %collective-permute-start.23) | collective-permute-done | bytes 131104 | tf_op jit(solution)/shard_map/ppermute | solution.py:294
  68.4 1.1 %shard_map.91 = (bf16[512,256]{1,0:T(8,128)(2,1)S(1)}, bf16[512,512]{1,0:T(8,128)(2,1)S(1)}) custom-call(bf16[256,256]{1,0:T(8,128)(2,1)S(1)} %collective-permute-done.22.refs_0_, bf16[256,256]{1,0:T(8,128)(2,1)S(1)} %collective-permute-done.23.refs_1_, bf16[256,256]{1,0:T(8,128)(2,1)S(1)} %get-tuple-element.63.refs_2_.refs_1_, ...), custom_call_target="tpu_custom_call" | custom-call | flops 268435456 | bytes 2400000 | tf_op jit(solution)/shard_map/pallas_call | solution.py:148
  69.6 1.1 %collective-permute-done.29.refs_0_.refs_7_ = bf16[256,256]{1,0:T(8,128)(2,1)S(1)} collective-permute-done((bf16[256,256]{1,0:T(8,128)(2,1)S(1)}, bf16[256,256]{1,0:T(8,128)(2,1)S(1)}, u32[]{:S(2)}, u32[]{:S(2)}) %collective-permute-start.29) | collective-permute-done | bytes 131104 | tf_op jit(solution)/shard_map/ppermute | solution.py:294
  72.7 1.3 %collective-permute-start.28 = (bf16[256,256]{1,0:T(8,128)(2,1)S(1)}, bf16[256,256]{1,0:T(8,128)(2,1)S(1)}, u32[]{:S(2)}, u32[]{:S(2)}) collective-permute-start(bf16[256,256]{1,0:T(8,128)(2,1)S(1)} %get-tuple-element.66.refs_4_), channel_id=1, source_target_pairs={{0,2},{1,3},{2,0},{3,1},{4,6},{5,7},{6,4},{7,5},{8,10},{9,11},{10,... | collective-permute-start | bytes 393224 | tf_op jit(solution)/shard_map/ppermute | solution.py:294
  74.0 2.8 %collective-permute-done.30.refs_0_.refs_4_ = bf16[256,256]{1,0:T(8,128)(2,1)S(1)} collective-permute-done((bf16[256,256]{1,0:T(8,128)(2,1)S(1)}, bf16[256,256]{1,0:T(8,128)(2,1)S(1)}, u32[]{:S(2)}, u32[]{:S(2)}) %collective-permute-start.30) | collective-permute-done | bytes 131104 | tf_op jit(solution)/shard_map/ppermute | solution.py:294
  77.6 1.3 %collective-permute-done.28.refs_4_ = bf16[256,256]{1,0:T(8,128)(2,1)S(1)} collective-permute-done((bf16[256,256]{1,0:T(8,128)(2,1)S(1)}, bf16[256,256]{1,0:T(8,128)(2,1)S(1)}, u32[]{:S(2)}, u32[]{:S(2)}) %collective-permute-start.28) | collective-permute-done | bytes 131104 | tf_op jit(solution)/shard_map/ppermute | solution.py:294
  79.5 2.5 %collective-permute-start.32 = (bf16[256,256]{1,0:T(8,128)(2,1)S(1)}, bf16[256,256]{1,0:T(8,128)(2,1)S(1)}, u32[]{:S(2)}, u32[]{:S(2)}) collective-permute-start(bf16[256,256]{1,0:T(8,128)(2,1)S(1)} %get-tuple-element.68.refs_5_), channel_id=1, source_target_pairs={{0,12},{1,13},{2,14},{3,15},{4,8},{5,9},{6,10},{7,11},{8,4},{9,5},... | collective-permute-start | bytes 393224 | tf_op jit(solution)/shard_map/ppermute | solution.py:294
  82.6 1.2 %collective-permute-start.31 = (bf16[256,256]{1,0:T(8,128)(2,1)S(1)}, bf16[256,256]{1,0:T(8,128)(2,1)S(1)}, u32[]{:S(2)}, u32[]{:S(2)}) collective-permute-start(bf16[256,256]{1,0:T(8,128)(2,1)S(1)} %get-tuple-element.69.refs_5_), channel_id=1, source_target_pairs={{0,2},{1,3},{2,0},{3,1},{4,6},{5,7},{6,4},{7,5},{8,10},{9,11},{10,... | collective-permute-start | bytes 393224 | tf_op jit(solution)/shard_map/ppermute | solution.py:294
  85.9 2.4 %collective-permute-start.36 = (bf16[256,256]{1,0:T(8,128)(2,1)S(1)}, bf16[256,256]{1,0:T(8,128)(2,1)S(1)}, u32[]{:S(2)}, u32[]{:S(2)}) collective-permute-start(bf16[256,256]{1,0:T(8,128)(2,1)S(1)} %get-tuple-element.79.refs_0_), channel_id=1, source_target_pairs={{0,16},{16,0},{1,17},{17,1},{2,18},{18,2},{3,19},{19,3},{4,20},{20... | collective-permute-start | bytes 393224 | tf_op jit(solution)/shard_map/ppermute | solution.py:294
  88.6 3.2 %collective-permute-done.34.rest_1_ = bf16[256,256]{1,0:T(8,128)(2,1)S(1)} collective-permute-done((bf16[256,256]{1,0:T(8,128)(2,1)S(1)}, bf16[256,256]{1,0:T(8,128)(2,1)S(1)}, u32[]{:S(2)}, u32[]{:S(2)}) %collective-permute-start.34) | collective-permute-done | bytes 131104 | tf_op jit(solution)/shard_map/ppermute | solution.py:294
  92.5 1.5 %collective-permute-done.37.refs_3_ = bf16[256,256]{1,0:T(8,128)(2,1)S(1)} collective-permute-done((bf16[256,256]{1,0:T(8,128)(2,1)S(1)}, bf16[256,256]{1,0:T(8,128)(2,1)S(1)}, u32[]{:S(2)}, u32[]{:S(2)}) %collective-permute-start.37) | collective-permute-done | bytes 131104 | tf_op jit(solution)/shard_map/ppermute | solution.py:378
  (89 shorter events, 22.9 us)
Async XLA Ops:
  0.6 21.5 %collective-permute-start.3 = (bf16[80,8192]{1,0:T(8,128)(2,1)}, bf16[80,8192]{1,0:T(8,128)(2,1)S(1)}, u32[]{:S(2)}, u32[]{:S(2)}) collective-permute-start(bf16[80,8192]{1,0:T(8,128)(2,1)} %bitcast.5), channel_id=1, source_target_pairs={{0,1},{1,0},{2,3},{3,2},{4,5},{5,4},{6,7},{7,6},{8,9},{9,8},{10,11... | collective-permute-start | bytes 3932168 | tf_op jit(solution)/shard_map/ppermute | solution.py:294
  1.1 21.5 %collective-permute-start.4 = (bf16[80,8192]{1,0:T(8,128)(2,1)}, bf16[80,8192]{1,0:T(8,128)(2,1)S(1)}, u32[]{:S(2)}, u32[]{:S(2)}) collective-permute-start(bf16[80,8192]{1,0:T(8,128)(2,1)} %bitcast.7), channel_id=1, source_target_pairs={{0,1},{1,0},{2,3},{3,2},{4,5},{5,4},{6,7},{7,6},{8,9},{9,8},{10,11... | collective-permute-start | bytes 3932168 | tf_op jit(solution)/shard_map/ppermute | solution.py:294
  3.9 9.6 %collective-permute-start.8 = (bf16[256,256]{1,0:T(8,128)(2,1)S(1)}, bf16[256,256]{1,0:T(8,128)(2,1)S(1)}, u32[]{:S(2)}, u32[]{:S(2)}) collective-permute-start(bf16[256,256]{1,0:T(8,128)(2,1)S(1)} %get-tuple-element.43.refs_0_.x_ref.refs_2_), channel_id=1, source_target_pairs={{0,2},{1,3},{2,0},{3,1},{4,6},{5,7},{6,4},{7,5},{8,10},{9,11},{10,... | collective-permute-start | bytes 393224 | tf_op jit(solution)/shard_map/ppermute | solution.py:294
  6.8 6.6 %collective-permute-start.5 = (bf16[256,256]{1,0:T(8,128)(2,1)S(1)}, bf16[256,256]{1,0:T(8,128)(2,1)S(1)}, u32[]{:S(2)}, u32[]{:S(2)}) collective-permute-start(bf16[256,256]{1,0:T(8,128)(2,1)S(1)} %get-tuple-element.43.refs_0_.x_ref.refs_2_), channel_id=1, source_target_pairs={{0,4},{1,5},{2,6},{3,7},{4,0},{5,1},{6,2},{7,3},{8,12},{9,13},{10,... | collective-permute-start | bytes 393224 | tf_op jit(solution)/shard_map/ppermute | solution.py:294
  11.0 7.5 %collective-permute-start.9 = (bf16[256,256]{1,0:T(8,128)(2,1)S(1)}, bf16[256,256]{1,0:T(8,128)(2,1)S(1)}, u32[]{:S(2)}, u32[]{:S(2)}) collective-permute-start(bf16[256,256]{1,0:T(8,128)(2,1)S(1)} %get-tuple-element.43.refs_0_.x_ref.refs_2_), channel_id=1, source_target_pairs={{0,12},{1,13},{2,14},{3,15},{4,8},{5,9},{6,10},{7,11},{8,4},{9,5},... | collective-permute-start | bytes 393224 | tf_op jit(solution)/shard_map/ppermute | solution.py:294
  13.5 17.9 %collective-permute-start = (bf16[256,256]{1,0:T(8,128)(2,1)S(1)}, bf16[256,256]{1,0:T(8,128)(2,1)S(1)}, u32[]{:S(2)}, u32[]{:S(2)}) collective-permute-start(bf16[256,256]{1,0:T(8,128)(2,1)S(1)} %get-tuple-element.44.refs_2_.refs_1_), channel_id=1, source_target_pairs={{0,1},{1,0},{2,3},{3,2},{4,5},{5,4},{6,7},{7,6},{8,9},{9,8},{10,11... | collective-permute-start | bytes 393224 | tf_op jit(solution)/shard_map/ppermute | solution.py:294
  13.5 17.9 %collective-permute-start.6 = (bf16[256,256]{1,0:T(8,128)(2,1)S(1)}, bf16[256,256]{1,0:T(8,128)(2,1)S(1)}, u32[]{:S(2)}, u32[]{:S(2)}) collective-permute-start(bf16[256,256]{1,0:T(8,128)(2,1)S(1)} %collective-permute-done.5.refs_0_), channel_id=1, source_target_pairs={{0,2},{1,3},{2,0},{3,1},{4,6},{5,7},{6,4},{7,5},{8,10},{9,11},{10,... | collective-permute-start | bytes 393224 | tf_op jit(solution)/shard_map/ppermute | solution.py:294
  18.5 14.1 %collective-permute-start.12 = (bf16[256,256]{1,0:T(8,128)(2,1)S(1)}, bf16[256,256]{1,0:T(8,128)(2,1)S(1)}, u32[]{:S(2)}, u32[]{:S(2)}) collective-permute-start(bf16[256,256]{1,0:T(8,128)(2,1)S(1)} %shard_map.82), channel_id=1, source_target_pairs={{0,8},{1,9},{2,10},{3,11},{4,12},{5,13},{6,14},{7,15},{8,0},{9,1},... | collective-permute-start | bytes 393224 | tf_op jit(solution)/shard_map/ppermute | solution.py:294
  22.1 13.1 %collective-permute-start.10 = (bf16[256,256]{1,0:T(8,128)(2,1)S(1)}, bf16[256,256]{1,0:T(8,128)(2,1)S(1)}, u32[]{:S(2)}, u32[]{:S(2)}) collective-permute-start(bf16[256,256]{1,0:T(8,128)(2,1)S(1)} %collective-permute-done.9.refs_0_.refs_5_), channel_id=1, source_target_pairs={{0,2},{1,3},{2,0},{3,1},{4,6},{5,7},{6,4},{7,5},{8,10},{9,11},{10,... | collective-permute-start | bytes 393224 | tf_op jit(solution)/shard_map/ppermute | solution.py:294
  32.5 11.5 %collective-permute-start.7 = (bf16[512,256]{1,0:T(8,128)(2,1)S(1)}, bf16[512,256]{1,0:T(8,128)(2,1)S(1)}, u32[]{:S(2)}, u32[]{:S(2)}) collective-permute-start(bf16[512,256]{1,0:T(8,128)(2,1)S(1)} %get-tuple-element.45.refs_4_), channel_id=1, source_target_pairs={{0,4},{1,5},{2,6},{3,7},{4,0},{5,1},{6,2},{7,3},{8,12},{9,13},{10,... | collective-permute-start | bytes 786440 | tf_op jit(solution)/shard_map/ppermute | solution.py:294
  35.9 6.0 %collective-permute-start.11 = (bf16[256,256]{1,0:T(8,128)(2,1)S(1)}, bf16[256,256]{1,0:T(8,128)(2,1)S(1)}, u32[]{:S(2)}, u32[]{:S(2)}) collective-permute-start(bf16[256,256]{1,0:T(8,128)(2,1)S(1)} %get-tuple-element.47.refs_4_), channel_id=1, source_target_pairs={{0,2},{1,3},{2,0},{3,1},{4,6},{5,7},{6,4},{7,5},{8,10},{9,11},{10,... | collective-permute-start | bytes 393224 | tf_op jit(solution)/shard_map/ppermute | solution.py:294
  38.8 7.3 %collective-permute-start.16 = (bf16[256,256]{1,0:T(8,128)(2,1)S(1)}, bf16[256,256]{1,0:T(8,128)(2,1)S(1)}, u32[]{:S(2)}, u32[]{:S(2)}) collective-permute-start(bf16[256,256]{1,0:T(8,128)(2,1)S(1)} %get-tuple-element.48.refs_5_), channel_id=1, source_target_pairs={{0,2},{1,3},{2,0},{3,1},{4,6},{5,7},{6,4},{7,5},{8,10},{9,11},{10,... | collective-permute-start | bytes 393224 | tf_op jit(solution)/shard_map/ppermute | solution.py:294
  42.5 7.5 %collective-permute-start.15 = (bf16[256,256]{1,0:T(8,128)(2,1)S(1)}, bf16[256,256]{1,0:T(8,128)(2,1)S(1)}, u32[]{:S(2)}, u32[]{:S(2)}) collective-permute-start(bf16[256,256]{1,0:T(8,128)(2,1)S(1)} %get-tuple-element.49.refs_5_), channel_id=1, source_target_pairs={{0,12},{1,13},{2,14},{3,15},{4,8},{5,9},{6,10},{7,11},{8,4},{9,5},... | collective-permute-start | bytes 393224 | tf_op jit(solution)/shard_map/ppermute | solution.py:294
  44.7 5.9 %collective-permute-start.14 = (bf16[256,256]{1,0:T(8,128)(2,1)S(1)}, bf16[256,256]{1,0:T(8,128)(2,1)S(1)}, u32[]{:S(2)}, u32[]{:S(2)}) collective-permute-start(bf16[256,256]{1,0:T(8,128)(2,1)S(1)} %get-tuple-element.50.refs_5_), channel_id=1, source_target_pairs={{0,2},{1,3},{2,0},{3,1},{4,6},{5,7},{6,4},{7,5},{8,10},{9,11},{10,... | collective-permute-start | bytes 393224 | tf_op jit(solution)/shard_map/ppermute | solution.py:294
  46.7 8.7 %collective-permute-start.17 = (bf16[256,256]{1,0:T(8,128)(2,1)S(1)}, bf16[256,256]{1,0:T(8,128)(2,1)S(1)}, u32[]{:S(2)}, u32[]{:S(2)}) collective-permute-start(bf16[256,256]{1,0:T(8,128)(2,1)S(1)} %get-tuple-element.51), channel_id=1, source_target_pairs={{0,8},{1,9},{2,10},{3,11},{4,12},{5,13},{6,14},{7,15},{8,0},{9,1},... | collective-permute-start | bytes 393224 | tf_op jit(solution)/shard_map/ppermute | solution.py:294
  48.4 8.0 %collective-permute-start.19 = (bf16[256,256]{1,0:T(8,128)(2,1)S(1)}, bf16[256,256]{1,0:T(8,128)(2,1)S(1)}, u32[]{:S(2)}, u32[]{:S(2)}) collective-permute-start(bf16[256,256]{1,0:T(8,128)(2,1)S(1)} %get-tuple-element.61.refs_0_), channel_id=1, source_target_pairs={{0,16},{16,0},{1,17},{17,1},{2,18},{18,2},{3,19},{19,3},{4,20},{20... | collective-permute-start | bytes 393224 | tf_op jit(solution)/shard_map/ppermute | solution.py:294
  50.0 8.4 %collective-permute-start.20 = (bf16[256,256]{1,0:T(8,128)(2,1)S(1)}, bf16[256,256]{1,0:T(8,128)(2,1)S(1)}, u32[]{:S(2)}, u32[]{:S(2)}) collective-permute-start(bf16[256,256]{1,0:T(8,128)(2,1)S(1)} %get-tuple-element.62), channel_id=1, source_target_pairs={{0,17},{1,16},{2,19},{3,18},{4,21},{5,20},{6,23},{7,22},{8,25},{9,... | collective-permute-start | bytes 393224 | tf_op jit(solution)/shard_map/ppermute | solution.py:378
  50.0 8.4 %collective-permute-start.18 = (bf16[256,256]{1,0:T(8,128)(2,1)S(1)}, bf16[256,256]{1,0:T(8,128)(2,1)S(1)}, u32[]{:S(2)}, u32[]{:S(2)}) collective-permute-start(bf16[256,256]{1,0:T(8,128)(2,1)S(1)} %get-tuple-element.62), channel_id=1, source_target_pairs={{0,1},{1,0},{2,3},{3,2},{4,5},{5,4},{6,7},{7,6},{8,9},{9,8},{10,11... | collective-permute-start | bytes 393224 | tf_op jit(solution)/shard_map/ppermute | solution.py:294
  55.5 8.0 %collective-permute-start.22 = (bf16[256,256]{1,0:T(8,128)(2,1)S(1)}, bf16[256,256]{1,0:T(8,128)(2,1)S(1)}, u32[]{:S(2)}, u32[]{:S(2)}) collective-permute-start(bf16[256,256]{1,0:T(8,128)(2,1)S(1)} %get-tuple-element.53.refs_4_.refs_0_.x_ref.refs_2_), channel_id=1, source_target_pairs={{0,4},{1,5},{2,6},{3,7},{4,0},{5,1},{6,2},{7,3},{8,12},{9,13},{10,... | collective-permute-start | bytes 393224 | tf_op jit(solution)/shard_map/ppermute | solution.py:294
  55.5 7.9 %collective-permute-start.25 = (bf16[256,256]{1,0:T(8,128)(2,1)S(1)}, bf16[256,256]{1,0:T(8,128)(2,1)S(1)}, u32[]{:S(2)}, u32[]{:S(2)}) collective-permute-start(bf16[256,256]{1,0:T(8,128)(2,1)S(1)} %get-tuple-element.53.refs_4_.refs_0_.x_ref.refs_2_), channel_id=1, source_target_pairs={{0,2},{1,3},{2,0},{3,1},{4,6},{5,7},{6,4},{7,5},{8,10},{9,11},{10,... | collective-permute-start | bytes 393224 | tf_op jit(solution)/shard_map/ppermute | solution.py:294
  56.4 7.1 %collective-permute-start.26 = (bf16[256,256]{1,0:T(8,128)(2,1)S(1)}, bf16[256,256]{1,0:T(8,128)(2,1)S(1)}, u32[]{:S(2)}, u32[]{:S(2)}) collective-permute-start(bf16[256,256]{1,0:T(8,128)(2,1)S(1)} %get-tuple-element.53.refs_4_.refs_0_.x_ref.refs_2_), channel_id=1, source_target_pairs={{0,12},{1,13},{2,14},{3,15},{4,8},{5,9},{6,10},{7,11},{8,4},{9,5},... | collective-permute-start | bytes 393224 | tf_op jit(solution)/shard_map/ppermute | solution.py:294
  58.5 7.1 %collective-permute-start.21 = (bf16[256,256]{1,0:T(8,128)(2,1)S(1)}, bf16[256,256]{1,0:T(8,128)(2,1)S(1)}, u32[]{:S(2)}, u32[]{:S(2)}) collective-permute-start(bf16[256,256]{1,0:T(8,128)(2,1)S(1)} %get-tuple-element.63.refs_2_.refs_1_), channel_id=1, source_target_pairs={{0,1},{1,0},{2,3},{3,2},{4,5},{5,4},{6,7},{7,6},{8,9},{9,8},{10,11... | collective-permute-start | bytes 393224 | tf_op jit(solution)/shard_map/ppermute | solution.py:294
  63.4 7.2 %collective-permute-start.29 = (bf16[256,256]{1,0:T(8,128)(2,1)S(1)}, bf16[256,256]{1,0:T(8,128)(2,1)S(1)}, u32[]{:S(2)}, u32[]{:S(2)}) collective-permute-start(bf16[256,256]{1,0:T(8,128)(2,1)S(1)} %shard_map.94), channel_id=1, source_target_pairs={{0,8},{1,9},{2,10},{3,11},{4,12},{5,13},{6,14},{7,15},{8,0},{9,1},... | collective-permute-start | bytes 393224 | tf_op jit(solution)/shard_map/ppermute | solution.py:294
  63.5 8.6 %collective-permute-start.27 = (bf16[256,256]{1,0:T(8,128)(2,1)S(1)}, bf16[256,256]{1,0:T(8,128)(2,1)S(1)}, u32[]{:S(2)}, u32[]{:S(2)}) collective-permute-start(bf16[256,256]{1,0:T(8,128)(2,1)S(1)} %collective-permute-done.26.refs_0_.refs_5_), channel_id=1, source_target_pairs={{0,2},{1,3},{2,0},{3,1},{4,6},{5,7},{6,4},{7,5},{8,10},{9,11},{10,... | collective-permute-start | bytes 393224 | tf_op jit(solution)/shard_map/ppermute | solution.py:294
  69.5 12.5 %collective-permute-start.24 = (bf16[512,256]{1,0:T(8,128)(2,1)S(1)}, bf16[512,256]{1,0:T(8,128)(2,1)S(1)}, u32[]{:S(2)}, u32[]{:S(2)}) collective-permute-start(bf16[512,256]{1,0:T(8,128)(2,1)S(1)} %get-tuple-element.64.refs_4_), channel_id=1, source_target_pairs={{0,4},{1,5},{2,6},{3,7},{4,0},{5,1},{6,2},{7,3},{8,12},{9,13},{10,... | collective-permute-start | bytes 786440 | tf_op jit(solution)/shard_map/ppermute | solution.py:294
  70.7 6.2 %collective-permute-start.30 = (bf16[256,256]{1,0:T(8,128)(2,1)S(1)}, bf16[256,256]{1,0:T(8,128)(2,1)S(1)}, u32[]{:S(2)}, u32[]{:S(2)}) collective-permute-start(bf16[256,256]{1,0:T(8,128)(2,1)S(1)} %collective-permute-done.29.refs_0_.refs_7_), channel_id=1, source_target_pairs={{0,2},{1,3},{2,0},{3,1},{4,6},{5,7},{6,4},{7,5},{8,10},{9,11},{10,... | collective-permute-start | bytes 393224 | tf_op jit(solution)/shard_map/ppermute | solution.py:294
  72.7 6.1 %collective-permute-start.28 = (bf16[256,256]{1,0:T(8,128)(2,1)S(1)}, bf16[256,256]{1,0:T(8,128)(2,1)S(1)}, u32[]{:S(2)}, u32[]{:S(2)}) collective-permute-start(bf16[256,256]{1,0:T(8,128)(2,1)S(1)} %get-tuple-element.66.refs_4_), channel_id=1, source_target_pairs={{0,2},{1,3},{2,0},{3,1},{4,6},{5,7},{6,4},{7,5},{8,10},{9,11},{10,... | collective-permute-start | bytes 393224 | tf_op jit(solution)/shard_map/ppermute | solution.py:294
  77.5 6.3 %collective-permute-start.33 = (bf16[256,256]{1,0:T(8,128)(2,1)S(1)}, bf16[256,256]{1,0:T(8,128)(2,1)S(1)}, u32[]{:S(2)}, u32[]{:S(2)}) collective-permute-start(bf16[256,256]{1,0:T(8,128)(2,1)S(1)} %get-tuple-element.67.refs_5_), channel_id=1, source_target_pairs={{0,2},{1,3},{2,0},{3,1},{4,6},{5,7},{6,4},{7,5},{8,10},{9,11},{10,... | collective-permute-start | bytes 393224 | tf_op jit(solution)/shard_map/ppermute | solution.py:294
  79.5 8.8 %collective-permute-start.32 = (bf16[256,256]{1,0:T(8,128)(2,1)S(1)}, bf16[256,256]{1,0:T(8,128)(2,1)S(1)}, u32[]{:S(2)}, u32[]{:S(2)}) collective-permute-start(bf16[256,256]{1,0:T(8,128)(2,1)S(1)} %get-tuple-element.68.refs_5_), channel_id=1, source_target_pairs={{0,12},{1,13},{2,14},{3,15},{4,8},{5,9},{6,10},{7,11},{8,4},{9,5},... | collective-permute-start | bytes 393224 | tf_op jit(solution)/shard_map/ppermute | solution.py:294
  82.6 5.9 %collective-permute-start.31 = (bf16[256,256]{1,0:T(8,128)(2,1)S(1)}, bf16[256,256]{1,0:T(8,128)(2,1)S(1)}, u32[]{:S(2)}, u32[]{:S(2)}) collective-permute-start(bf16[256,256]{1,0:T(8,128)(2,1)S(1)} %get-tuple-element.69.refs_5_), channel_id=1, source_target_pairs={{0,2},{1,3},{2,0},{3,1},{4,6},{5,7},{6,4},{7,5},{8,10},{9,11},{10,... | collective-permute-start | bytes 393224 | tf_op jit(solution)/shard_map/ppermute | solution.py:294
  84.4 7.3 %collective-permute-start.34 = (bf16[256,256]{1,0:T(8,128)(2,1)S(1)}, bf16[256,256]{1,0:T(8,128)(2,1)S(1)}, u32[]{:S(2)}, u32[]{:S(2)}) collective-permute-start(bf16[256,256]{1,0:T(8,128)(2,1)S(1)} %get-tuple-element.70), channel_id=1, source_target_pairs={{0,8},{1,9},{2,10},{3,11},{4,12},{5,13},{6,14},{7,15},{8,0},{9,1},... | collective-permute-start | bytes 393224 | tf_op jit(solution)/shard_map/ppermute | solution.py:294
  85.9 6.6 %collective-permute-start.36 = (bf16[256,256]{1,0:T(8,128)(2,1)S(1)}, bf16[256,256]{1,0:T(8,128)(2,1)S(1)}, u32[]{:S(2)}, u32[]{:S(2)}) collective-permute-start(bf16[256,256]{1,0:T(8,128)(2,1)S(1)} %get-tuple-element.79.refs_0_), channel_id=1, source_target_pairs={{0,16},{16,0},{1,17},{17,1},{2,18},{18,2},{3,19},{19,3},{4,20},{20... | collective-permute-start | bytes 393224 | tf_op jit(solution)/shard_map/ppermute | solution.py:294
  (15 other events, 49.2 us)

commit v3 on v2

v3 whole, which is shorter than its diff:
```python
import functools

import jax
import jax.numpy as jnp
from jax import lax
from jax.experimental import pallas as pl
from jax.experimental.pallas import tpu as pltpu
from jax.sharding import PartitionSpec as P

STEPS = 2
DECAY = 0.05
STEP_SCALE = 48.0
BLOCK_ROWS = 128
BLOCK_DATES = 64
LANES = 128
GROUP = 16
F32 = jnp.float32
BF16 = jnp.bfloat16
VMEM = pl.BlockSpec(memory_space=pltpu.VMEM)
HBM = pl.BlockSpec(memory_space=pltpu.HBM)
ANY = pl.BlockSpec(memory_space=pl.ANY)
SMEM = pl.BlockSpec(memory_space=pltpu.SMEM)


def params(mib):
    return pltpu.CompilerParams(vmem_limit_bytes=mib << 20)


def cost(flops, bytes_accessed):
    return pl.CostEstimate(flops=flops, bytes_accessed=bytes_accessed, transcendentals=0)


def row_pieces(rows):
    half = BLOCK_ROWS // 2
    for block in range(rows // BLOCK_ROWS):
        for odd in range(2):
            yield block * BLOCK_ROWS + odd * half, pl.ds(block * BLOCK_ROWS + odd, half, stride=2), half


def prepare_kernel(pixel_ref, pixel_now_ref, pixel_bf_ref, slab):
    rows, rank = pixel_ref.shape
    for lane in range(0, rank, LANES):
        slab[lane // LANES] = pixel_ref[:, lane : lane + LANES]
    for to, source, half in row_pieces(rows):
        for lane in range(0, rank, LANES):
            piece = slab[lane // LANES, source, :]
            pixel_now_ref[to : to + half, lane : lane + LANES] = piece
            pixel_bf_ref[to : to + half, lane : lane + LANES] = piece.astype(BF16)


def place_kernel(copies, chip_blocks, place_ref, ids_ref, values_ref, weights_ref, panel_ref, flat, *scratch):
    slots, size = values_ref.shape
    tiles = size // LANES
    core_blocks = chip_blocks // 2
    chip, core, count = place_ref[0], place_ref[1], ids_ref[2, 0]
    spare = panel_ref.shape[1] - tiles
    refs = (values_ref, weights_ref)

    def load(g, which):
        raw, sems = scratch
        rows = pl.ds(pl.multiple_of(g * GROUP, GROUP), GROUP)
        return pltpu.make_async_copy(refs[which].at[rows], raw.at[which, rows], sems.at[which, g])

    if copies:
        for g in range(slots // GROUP):
            for which in range(2):
                load(g, which).start()
    panel_ref[...] = jnp.zeros_like(panel_ref)

    def group(g, carry):
        first = pl.multiple_of(g * GROUP, GROUP)
        if copies:
            for which in range(2):
                load(g, which).wait()

        @pl.when(first < count)
        def _():
            for which in range(2):
                source = scratch[0].at[which] if copies else refs[which]
                for t in range(tiles):
                    flat[which, t * GROUP : (t + 1) * GROUP, :] = source[
                        pl.ds(first, GROUP), t * LANES : (t + 1) * LANES
                    ].astype(F32)
            for s in range(GROUP):
                row_block, date_block = ids_ref[0, first + s], ids_ref[1, first + s]
                target = lax.bitwise_xor(lax.div(row_block, chip_blocks), chip)
                inside = lax.rem(row_block, chip_blocks)
                wanted = jnp.logical_and(lax.div(inside, core_blocks) == core, first + s < count)
                row = (target * core_blocks + lax.rem(inside, core_blocks)) * tiles
                row = pl.multiple_of(jnp.where(wanted, row, spare), tiles)
                lane = pl.multiple_of(date_block * LANES, LANES)
                for which in range(2):
                    tile = flat[which, pl.ds(s, tiles, stride=GROUP), :]
                    panel_ref[which, pl.ds(row, tiles), pl.ds(lane, LANES)] = tile.astype(BF16)

        return carry

    lax.fori_loop(0, slots // GROUP, group, 0)


def place_blocks(copies, core_blocks, place, ids, values, weights, rows, width, mib):
    slots, size = values.shape
    tiles = size // LANES
    scratch = [pltpu.VMEM((2, slots, size), BF16), pltpu.SemaphoreType.DMA((2, slots // GROUP))] if copies else []
    return pl.pallas_call(
        functools.partial(place_kernel, copies, 2 * core_blocks),
        out_shape=jax.ShapeDtypeStruct((2, rows + tiles, width), BF16),
        in_specs=[SMEM, SMEM] + [HBM if copies else VMEM] * 2,
        out_specs=VMEM,
        scratch_shapes=[pltpu.VMEM((2, tiles * GROUP, LANES), F32)] + scratch,
        compiler_params=params(mib),
        cost_estimate=cost(slots * size * 8, slots * size * 8),
    )(place, ids, values, weights)


def pack_kernel(count_ref, date_ref, ids_ref, out_ref):
    local, rank = date_ref.shape
    slots = ids_ref.shape[1]
    out_ref[:local, :] = date_ref[...].astype(BF16)
    row = lax.broadcasted_iota(jnp.int32, (GROUP, slots), 0)
    ids = jnp.where(row == 0, ids_ref[0:1, :], jnp.where(row == 1, ids_ref[1:2, :], count_ref[0, 0]))
    out_ref[local:, :] = jnp.zeros((GROUP, rank), BF16)
    out_ref[local:, :slots] = ids.astype(F32).astype(BF16)


def apart(ref, which, first, rows):
    low = lax.broadcasted_iota(jnp.int32, (rows, LANES), 1) < BLOCK_DATES
    even, odd = [], []
    for at in range(0, ref.shape[2], 2 * LANES):
        a = ref[which, first : first + rows, at : at + LANES].astype(F32)
        b = ref[which, first : first + rows, at + LANES : at + 2 * LANES].astype(F32)
        even.append(jnp.where(low, a, pltpu.roll(b, BLOCK_DATES, 1)))
        odd.append(jnp.where(low, pltpu.roll(a, BLOCK_DATES, 1), b))
    return jnp.concatenate([jnp.concatenate(even, axis=1), jnp.concatenate(odd, axis=1)], axis=0)


def chunk_kernel(n, *refs):
    pixel_refs, (dates_ref, dates_other_ref, mine_ref, other_ref) = refs[:n], refs[n : n + 4]
    term_ref, errors_ref = refs[-2:]
    half = BLOCK_ROWS // 2
    local = dates_ref.shape[0]
    blocks = pixel_refs[0].shape[0] // BLOCK_ROWS
    for block in range(n * blocks):
        inside = slice(block % blocks * BLOCK_ROWS, (block % blocks + 1) * BLOCK_ROWS)
        rows = slice(block * BLOCK_ROWS, (block + 1) * BLOCK_ROWS)
        total = None
        for k, (panel, dates) in enumerate(((mine_ref, dates_ref), (other_ref, dates_other_ref))):
            predicted = lax.dot_general(
                pixel_refs[block // blocks][inside, :], dates[...],
                (((1,), (1,)), ((), ())), preferred_element_type=F32,
            )
            observed = apart(panel, 0, block * half, half)
            weights = apart(panel, 1, block * half, half)
            errors = (weights * (predicted - observed)).astype(BF16)
            errors_ref[rows, k * local : (k + 1) * local] = errors
            term = jnp.dot(errors, dates[...], preferred_element_type=F32)
            total = term if total is None else total + term
        term_ref[rows, :] = total.astype(term_ref.dtype)


def chunk(pixels, dates_bf, dates_other, panels, at, kind, after):
    rows, rank = pixels[0].shape
    local = panels[0].shape[2] // 2
    n = len(pixels)
    whole = lambda a: pl.BlockSpec(a.shape, lambda i: (0,) * a.ndim)
    dates = pl.BlockSpec((local, rank), lambda i: (0, 0))
    panel = pl.BlockSpec((2, n * rows // 2, panels[0].shape[2]), lambda i: (0, at, 0))
    return pl.pallas_call(
        functools.partial(chunk_kernel, n),
        grid=(1,),
        out_shape=(
            jax.ShapeDtypeStruct((n * rows, rank), kind),
            jax.ShapeDtypeStruct((n * rows, 2 * local), BF16),
        ),
        in_specs=[whole(p) for p in pixels] + [dates, dates, panel, panel]
        + [ANY] * len(after),
        out_specs=(pl.BlockSpec((n * rows, rank), lambda i: (0, 0)),
                   pl.BlockSpec((n * rows, 2 * local), lambda i: (0, 0))),
        compiler_params=params(24),
        cost_estimate=cost(8 * n * rows * rank * local, n * 1200000),
    )(*pixels, dates_bf, dates_other, *panels, *after)


def hold_kernel(x_ref, *refs):
    refs[-1][...] = x_ref[...]


def hold(x, *after):
    return pl.pallas_call(
        hold_kernel,
        out_shape=jax.ShapeDtypeStruct(x.shape, x.dtype),
        in_specs=[VMEM] + [ANY] * len(after),
        out_specs=VMEM,
        compiler_params=params(16),
        cost_estimate=cost(x.size, 4 * x.size),
    )(x, *after)


def date_kernel(starts, *refs):
    n = len(starts)
    pixel_refs, errors_refs, (own_ref, other_ref) = refs[:n], refs[n:-2], refs[-2:]
    local = own_ref.shape[0]
    for k, out in enumerate((own_ref, other_ref)):
        total = None
        for (which, start), pixels in zip(starts, pixel_refs):
            errors = errors_refs[which][start : start + pixels.shape[0], k * local : (k + 1) * local]
            term = lax.dot_general(errors, pixels[...], (((0,), (0,)), ((), ())), preferred_element_type=F32)
            total = term if total is None else total + term
        out[...] = total.astype(out.dtype)


def date_gradient(errors, pixels, starts, local, after):
    rank = pixels[0].shape[1]
    n = len(pixels)
    return pl.pallas_call(
        functools.partial(date_kernel, starts),
        out_shape=(jax.ShapeDtypeStruct((local, rank), BF16),) * 2,
        in_specs=[VMEM] * (n + len(errors)) + [ANY] * len(after),
        out_specs=(VMEM, VMEM),
        compiler_params=params(32),
        cost_estimate=cost(4 * n * pixels[0].shape[0] * rank * local, n * 400000),
    )(*pixels, *errors, *after)


def sum_kernel(*refs):
    parts, out_ref = refs[:-1], refs[-1]
    total = parts[0][...].astype(F32)
    for part in parts[1:]:
        total = total + part[...].astype(F32)
    out_ref[...] = total.astype(out_ref.dtype)


def add(parts, kind):
    rows, rank = parts[0][0].shape
    block = lambda at: pl.BlockSpec((rows, rank), lambda i: (at, 0))
    return pl.pallas_call(
        sum_kernel,
        grid=(1,),
        out_shape=jax.ShapeDtypeStruct((rows, rank), kind),
        in_specs=[block(at) for _, at in parts],
        out_specs=block(0),
        compiler_params=params(16),
        cost_estimate=cost(4 * rows * rank, 8 * rows * rank),
    )(*[x for x, _ in parts])


def pixel_kernel(scale, last, now_ref, *rest):
    parts, outs = rest[:-2], rest[-2:]
    rows, rank = now_ref.shape
    for start, target, half in row_pieces(rows):
        for lane in range(0, rank, LANES):
            at = (slice(start, start + half), slice(lane, lane + LANES))
            grad = parts[0][at].astype(F32)
            for part in parts[1:]:
                grad = grad + part[at].astype(F32)
            new = (1.0 - DECAY) * now_ref[at] - scale * grad
            if last:
                outs[1][lane // LANES, target, :] = new
            else:
                outs[0][at] = new
                outs[1][at] = new.astype(BF16)
    if last:
        for lane in range(0, rank, LANES):
            outs[0][:, lane : lane + LANES] = outs[1][lane // LANES]


def pixel_update(scale, last, now, parts):
    full = jax.ShapeDtypeStruct(now.shape, F32)
    early = add([(part, 0) for part in parts[:-1]], F32)
    return pl.pallas_call(
        functools.partial(pixel_kernel, scale, last),
        out_shape=(full,) if last else (full, jax.ShapeDtypeStruct(now.shape, BF16)),
        in_specs=[VMEM] * 3,
        out_specs=(VMEM,) if last else (VMEM, VMEM),
        scratch_shapes=[pltpu.VMEM((now.shape[1] // LANES, now.shape[0], LANES), F32)] if last else [],
        compiler_params=params(16),
        cost_estimate=cost(10 * now.size, 8 * now.size),
    )(now, early, parts[-1])


def date_update_kernel(scale, now_ref, *refs):
    parts, (after_ref, new_ref, bf_ref) = refs[:-3], refs[-3:]
    halves = [None, None]
    for i, part in enumerate(parts):
        side = 2 * i // len(parts)
        value = part[...].astype(F32)
        halves[side] = value if halves[side] is None else halves[side] + value
    new = (1.0 - DECAY) * now_ref[...] - scale * (halves[0] + halves[1])
    new_ref[...] = new
    bf_ref[...] = new.astype(BF16)


def date_update(scale, now, parts, after):
    return pl.pallas_call(
        functools.partial(date_update_kernel, scale),
        out_shape=(jax.ShapeDtypeStruct(now.shape, F32), jax.ShapeDtypeStruct(now.shape, BF16)),
        in_specs=[VMEM] * (1 + len(parts)) + [ANY],
        out_specs=(VMEM, VMEM),
        compiler_params=params(16),
        cost_estimate=cost(8 * now.size, 8 * now.size),
    )(now, *parts, after)


def shards(pixel_factors, date_factors, block_ids, block_counts, block_values, block_weights):
    loop_size, groups = lax.axis_size("date"), lax.axis_size("pix")
    own_rows, rank = pixel_factors.shape
    local = date_factors.shape[0]
    chips = loop_size // 2
    high = 4
    low = chips // high
    all_pixels = own_rows * loop_size * groups
    all_dates = local * loop_size
    slots, flat = block_values.shape[2:]
    me = lax.axis_index("date")
    tiles = flat // LANES
    core_blocks = own_rows // BLOCK_ROWS

    def swap(x, mask, axis="date"):
        return lax.ppermute(x, axis, [(i, i ^ mask) for i in range(lax.axis_size(axis))])

    shape = jax.ShapeDtypeStruct
    pixel_now, pixel_bf = pl.pallas_call(
        prepare_kernel,
        out_shape=(shape((own_rows, rank), F32), shape((own_rows, rank), BF16)),
        in_specs=[VMEM],
        out_specs=(VMEM, VMEM),
        scratch_shapes=[pltpu.VMEM((rank // LANES, own_rows, LANES), F32)],
        compiler_params=params(16),
        cost_estimate=cost(own_rows * rank, own_rows * rank * 16),
    )(pixel_factors)
    dates_now = date_factors
    block_lists = block_ids.reshape(2, slots)
    dates_bf = pl.pallas_call(
        pack_kernel,
        out_shape=shape((local + GROUP, rank), BF16),
        in_specs=[SMEM, VMEM, VMEM],
        out_specs=VMEM,
        compiler_params=params(16),
        cost_estimate=cost(local * rank, 6 * local * rank),
    )(block_counts, date_factors, block_lists)
    dates_other = swap(dates_bf, 1)

    def lists(packed):
        return packed[local : local + 3, :slots].astype(jnp.int32)

    rows, width = chips * core_blocks * tiles, local // BLOCK_DATES * LANES
    values, weights = block_values.reshape(slots, flat), block_weights.reshape(slots, flat)
    place = jnp.stack([me // 2, me % 2]).astype(jnp.int32)
    mine = place_blocks(True, core_blocks, place, lists(dates_bf), values, weights, rows, width, 36)
    other = place_blocks(
        False, core_blocks, place, lists(dates_other), swap(values, 1), swap(weights, 1), rows, width, 30
    )
    panels = (mine, other)

    for step in range(STEPS):
        last = step == STEPS - 1
        far = range(1, low)
        along = [2 * low * hi for hi in range(high)]
        pixels = {(0, 0): pixel_bf}
        pixels[3, 0] = swap(pixel_bf, along[3])
        for lo in far:
            pixels[0, lo] = swap(pixel_bf, 2 * lo)
        pixels[1, 0] = swap(pixel_bf, along[1])
        pixels[2, 0] = swap(hold(pixel_bf, pixels[0, 1], *([] if step else [mine])), along[2])
        for lo in far:
            pixels[1, lo] = swap(pixels[1, 0], 2 * lo)
            pixels[3, lo] = swap(pixels[3, 0], 2 * lo)
            pixels[2, lo] = swap(pixels[2, 0] if step else hold(pixels[2, 0], other), 2 * lo)
        errors, starts, ordered, after = [], [], [], []

        def terms(keys, kind, errors=errors, starts=starts, ordered=ordered, dates_bf=dates_bf,
                  dates_other=dates_other, pixels=pixels):
            nonlocal after
            hi, lo = keys[0]
            n = len(keys)
            term, error = chunk(
                [pixels[k] for k in keys], dates_bf, dates_other, panels, (hi * low + lo) // n, kind, after,
            )
            starts += [(len(errors), i * own_rows) for i in range(n)]
            errors.append(error)
            ordered += [pixels[k] for k in keys]
            after = [term]
            return term

        pair = swap(terms([(1, lo) for lo in range(low)], BF16), along[1])
        recv3 = [(swap(terms([(3, lo)], BF16), 2 * lo), 0) for lo in far]
        near3 = terms([(3, 0)], F32)
        near2 = terms([(2, 0)], F32)
        near0 = terms([(0, 0)], F32)
        row0 = [terms([(0, lo)], F32) for lo in far]
        recv2 = [(swap(terms([(2, lo)], BF16), 2 * lo), 0) for lo in far]
        part3 = swap(add([(near3, 0)] + recv3, BF16), along[3])
        part0 = [swap(add([(row0[lo - 1], 0), (pair, lo)], BF16), 2 * lo) for lo in far]
        part2 = swap(add([(near2, 0)] + recv2, BF16), along[2])
        parts = [near0, pair] + part0 + [part3, part2]
        own, partner = date_gradient(errors, ordered, tuple(starts), local, [])
        scale = STEP_SCALE / all_dates
        if last:
            (pixel_now,) = pixel_update(scale, True, pixel_now, parts)
        else:
            pixel_now, pixel_bf = pixel_update(scale, False, pixel_now, parts)
        sums = [own, swap(partner, 1)]
        if groups > 1:
            count = groups * loop_size
            across = [(i, i ^ (loop_size + 1)) for i in range(count)]
            sums += [swap(own, 1, "pix"), lax.ppermute(partner, ("pix", "date"), across)]
        mask = 2
        while mask < groups:
            left, right = sums[: len(sums) // 2], sums[len(sums) // 2 :]
            total = sum(x.astype(F32) for x in left) + sum(x.astype(F32) for x in right)
            sums = [total.astype(BF16)]
            sums.append(swap(sums[0], mask, "pix"))
            mask *= 2
        dates_now, dates_bf = date_update(
            STEP_SCALE / all_pixels, dates_now, sums, pixel_now if last else pixel_bf
        )
        if not last:
            dates_other = swap(dates_bf, 1)
    return (pixel_now, dates_now)


def solution(mesh):
    placed = (
        P(("pix", "date"), None),
        P("date", None),
        P("pix", "date", None, None),
        P("pix", "date"),
        P("pix", "date", None, None),
        P("pix", "date", None, None),
    )
    return jax.shard_map(
        shards,
        mesh=mesh,
        in_specs=placed,
        out_specs=(P(("pix", "date"), None), P("date", None)),
        check_vma=False,
    )
```

time: 96.6 us -> 89.6 us (0.928)
  waiting for transfers between devices: 31.4 us -> 22.7 us
  starting transfers between devices: 37.2 us -> 40 us
  Pallas kernels: 18.7 us -> 17.7 us
    ppermute x36 -> x34, waiting for transfers between devices: 29.9 us -> 22.7 us  [swap(): lax.ppermute(x, axis, [(i, i ^ mask) for i in range(lax.axis_size(axis))])]
    ppermute x36 -> x34, starting transfers between devices: 37.2 us -> 40 us  [swap(): lax.ppermute(x, axis, [(i, i ^ mask) for i in range(lax.axis_size(axis))])]
    ppermute x2, waiting for transfers between devices: 1.52 us -> 0.01 us  [shards(): lax.ppermute(partner, ('pix', 'date'), across)]
    pallas_call x17 -> x25, Pallas kernels: 15.4 us -> 14.4 us  [the longest x14 9.88 us: chunk(): pl.pallas_call(functools.partial(chunk_kernel, n), grid=(1,), out_shape=(...]
  transfers between devices with their start and end apart: 38 -> 36, of which waited for: 13 -> 10; matrix products, arithmetic and copies ran while one was open for 0% -> 0% of each run, Pallas kernels for 19% -> 19%
where the time goes in v3:
time: 89.6 us; the launch traced here: 89 us
  starting transfers between devices  40 us (45%)
  waiting for transfers between devices  22.7 us (25%)
  Pallas kernels  17.7 us (20%)
  local copies, waits for them, and re-layouts  6.86 us (8%)
  between operations  1.66 us (2%)
    ppermute x34, starting transfers between devices, swap(): lax.ppermute(x, axis, [(i, i ^ mask) for i in range(lax.axis_size(axis))])  40 us
    ppermute x34, waiting for transfers between devices, swap(): lax.ppermute(x, axis, [(i, i ^ mask) for i in range(lax.axis_size(axis))])  22.7 us
    pallas_call x14, Pallas kernels, chunk(): pl.pallas_call(functools.partial(chunk_kernel, n), grid=(1,), out_shape=(...  9.88 us
    unnamed x18, local copies, waits for them, and re-layouts  6.86 us
    pallas_call x2, Pallas kernels, place_blocks(): pl.pallas_call(functools.partial(place_kernel, copies, 2 * core_blocks),...  4.18 us
  transfers between devices with their start and end apart: 36, of which 10 were waited for; matrix products, arithmetic and copies ran while one was open for 0% of the time, Pallas kernels for 19%

profile of v3, /device:TPU:0, one launch (start us, length us, event | category | flops | bytes accessed | tf_op | source)
XLA Modules:
  0.0 89.0 jit_solution(3157516150732533520)
XLA Ops:
  1.2 0.9 %copy-done.5 = f32[256,256]{1,0:T(8,128)S(1)} copy-done((f32[256,256]{1,0:T(8,128)S(1)}, f32[256,256]{1,0:T(8,128)}, u32[]{:S(2)}) %copy-start.5) | copy-done | bytes 262168
  2.9 2.9 %collective-permute-start.3 = (bf16[256,256]{1,0:T(8,128)(2,1)S(1)}, bf16[256,256]{1,0:T(8,128)(2,1)S(1)}, u32[]{:S(2)}, u32[]{:S(2)}) collective-permute-start(bf16[256,256]{1,0:T(8,128)(2,1)S(1)} %get-tuple-element.42.x_ref.refs_0_.refs_5_), channel_id=1, source_target_pairs={{0,2},{1,3},{2,0},{3,1},{4,6},{5,7},{6,4},{7,5},{8,10},{9,11},{10,... | collective-permute-start | bytes 393224 | tf_op jit(solution)/shard_map/ppermute | solution.py:319
  5.9 1.6 %collective-permute-start.7 = (bf16[256,256]{1,0:T(8,128)(2,1)S(1)}, bf16[256,256]{1,0:T(8,128)(2,1)S(1)}, u32[]{:S(2)}, u32[]{:S(2)}) collective-permute-start(bf16[256,256]{1,0:T(8,128)(2,1)S(1)} %get-tuple-element.42.x_ref.refs_0_.refs_5_), channel_id=1, source_target_pairs={{0,4},{1,5},{2,6},{3,7},{4,0},{5,1},{6,2},{7,3},{8,12},{9,13},{10,... | collective-permute-start | bytes 393224 | tf_op jit(solution)/shard_map/ppermute | solution.py:319
  7.4 2.5 %collective-permute-start.5 = (bf16[256,256]{1,0:T(8,128)(2,1)S(1)}, bf16[256,256]{1,0:T(8,128)(2,1)S(1)}, u32[]{:S(2)}, u32[]{:S(2)}) collective-permute-start(bf16[256,256]{1,0:T(8,128)(2,1)S(1)} %get-tuple-element.42.x_ref.refs_0_.refs_5_), channel_id=1, source_target_pairs={{0,12},{1,13},{2,14},{3,15},{4,8},{5,9},{6,10},{7,11},{8,4},{9,5},... | collective-permute-start | bytes 393224 | tf_op jit(solution)/shard_map/ppermute | solution.py:319
  12.4 1.3 %copy-done = bf16[1,1,80,8192]{3,2,1,0:T(8,128)(2,1)S(1)} copy-done((bf16[1,1,80,8192]{3,2,1,0:T(8,128)(2,1)S(1)}, bf16[1,1,80,8192]{3,2,1,0:T(8,128)(2,1)}, u32[]{:S(2)}) %copy-start) | copy-done | bytes 1310744
  13.7 1.3 %copy-done.1 = bf16[1,1,80,8192]{3,2,1,0:T(8,128)(2,1)S(1)} copy-done((bf16[1,1,80,8192]{3,2,1,0:T(8,128)(2,1)S(1)}, bf16[1,1,80,8192]{3,2,1,0:T(8,128)(2,1)}, u32[]{:S(2)}) %copy-start.1) | copy-done | bytes 1310744
  15.0 2.3 %shard_map.79.refs_1_.refs_4_.refs_3_ = bf16[2,1088,512]{2,1,0:T(8,128)(2,1)S(1)} custom-call(s32[2]{0:T(128)S(1)} %pad_add_fusion.place_ref, s32[3,80]{1,0:T(4,128)S(1)} %slice_convert_fusion.1.ids_ref, bf16[80,8192]{1,0:T(8,128)(2,1)S(1)} %bitcast.6, bf16[80,8192]{1,0:T(8,128)(2,1)S(1)} %bitcast.8), custom_call_target="tpu_custom_call" | custom-call | flops 5242880 | bytes 5242880 | tf_op jit(solution)/shard_map/pallas_call | solution.py:105
  17.4 1.1 %collective-permute-start.4 = (bf16[256,256]{1,0:T(8,128)(2,1)S(1)}, bf16[256,256]{1,0:T(8,128)(2,1)S(1)}, u32[]{:S(2)}, u32[]{:S(2)}) collective-permute-start(bf16[256,256]{1,0:T(8,128)(2,1)S(1)} %shard_map.81), channel_id=1, source_target_pairs={{0,8},{1,9},{2,10},{3,11},{4,12},{5,13},{6,14},{7,15},{8,0},{9,1},... | collective-permute-start | bytes 393224 | tf_op jit(solution)/shard_map/ppermute | solution.py:319
  19.1 1.4 %collective-permute-start.6 = (bf16[256,256]{1,0:T(8,128)(2,1)S(1)}, bf16[256,256]{1,0:T(8,128)(2,1)S(1)}, u32[]{:S(2)}, u32[]{:S(2)}) collective-permute-start(bf16[256,256]{1,0:T(8,128)(2,1)S(1)} %collective-permute-done.5.refs_0_.refs_3_), channel_id=1, source_target_pairs={{0,2},{1,3},{2,0},{3,1},{4,6},{5,7},{6,4},{7,5},{8,10},{9,11},{10,... | collective-permute-start | bytes 393224 | tf_op jit(solution)/shard_map/ppermute | solution.py:319
  20.5 1.8 %shard_map.80.refs_5_.refs_4_.refs_0_ = bf16[2,1088,512]{2,1,0:T(8,128)(2,1)S(1)} custom-call(s32[2]{0:T(128)S(1)} %pad_add_fusion.place_ref, s32[3,80]{1,0:T(4,128)S(1)} %slice_convert_fusion.ids_ref, bf16[80,8192]{1,0:T(8,128)(2,1)S(1)} %collective-permute-done.1.values_ref, bf16[80,8192]{1,0:T(8,128)(2,1)S(1)} %collective-permute-done.2.weights_ref), custom_call_target="tpu_custom_call" | custom-call | flops 5242880 | bytes 5242880 | tf_op jit(solution)/shard_map/pallas_call | solution.py:105
  22.4 4.3 %collective-permute-done.4.refs_0_.x_ref.refs_4_ = bf16[256,256]{1,0:T(8,128)(2,1)S(1)} collective-permute-done((bf16[256,256]{1,0:T(8,128)(2,1)S(1)}, bf16[256,256]{1,0:T(8,128)(2,1)S(1)}, u32[]{:S(2)}, u32[]{:S(2)}) %collective-permute-start.4) | collective-permute-done | bytes 131104 | tf_op jit(solution)/shard_map/ppermute | solution.py:319
  26.7 1.3 %collective-permute-start.13 = (bf16[256,256]{1,0:T(8,128)(2,1)S(1)}, bf16[256,256]{1,0:T(8,128)(2,1)S(1)}, u32[]{:S(2)}, u32[]{:S(2)}) collective-permute-start(bf16[256,256]{1,0:T(8,128)(2,1)S(1)} %shard_map.91), channel_id=1, source_target_pairs={{0,2},{1,3},{2,0},{3,1},{4,6},{5,7},{6,4},{7,5},{8,10},{9,11},{10,... | collective-permute-start | bytes 393224 | tf_op jit(solution)/shard_map/ppermute | solution.py:319
  27.9 1.1 %shard_map.82 = (bf16[512,256]{1,0:T(8,128)(2,1)S(1)}, bf16[512,512]{1,0:T(8,128)(2,1)S(1)}) custom-call(bf16[256,256]{1,0:T(8,128)(2,1)S(1)} %collective-permute-done.7.refs_0_, bf16[256,256]{1,0:T(8,128)(2,1)S(1)} %collective-permute-done.8.refs_1_, bf16[272,256]{1,0:T(8,128)(2,1)S(1)} %shard_map.78.refs_2_.refs_1_, ...), custom_call_target="tpu_custom_call" | custom-call | flops 268435456 | bytes 2400000 | tf_op jit(solution)/shard_map/pallas_call | solution.py:168
  33.9 1.3 %collective-permute-start.14 = (bf16[256,256]{1,0:T(8,128)(2,1)S(1)}, bf16[256,256]{1,0:T(8,128)(2,1)S(1)}, u32[]{:S(2)}, u32[]{:S(2)}) collective-permute-start(bf16[256,256]{1,0:T(8,128)(2,1)S(1)} %get-tuple-element.49), channel_id=1, source_target_pairs={{0,2},{1,3},{2,0},{3,1},{4,6},{5,7},{6,4},{7,5},{8,10},{9,11},{10,... | collective-permute-start | bytes 393224 | tf_op jit(solution)/shard_map/ppermute | solution.py:319
  35.2 2.2 %collective-permute-start.12 = (bf16[256,256]{1,0:T(8,128)(2,1)S(1)}, bf16[256,256]{1,0:T(8,128)(2,1)S(1)}, u32[]{:S(2)}, u32[]{:S(2)}) collective-permute-start(bf16[256,256]{1,0:T(8,128)(2,1)S(1)} %shard_map.89), channel_id=1, source_target_pairs={{0,12},{1,13},{2,14},{3,15},{4,8},{5,9},{6,10},{7,11},{8,4},{9,5},... | collective-permute-start | bytes 393224 | tf_op jit(solution)/shard_map/ppermute | solution.py:319
  37.4 1.5 %collective-permute-done.14.refs_1_ = bf16[256,256]{1,0:T(8,128)(2,1)S(1)} collective-permute-done((bf16[256,256]{1,0:T(8,128)(2,1)S(1)}, bf16[256,256]{1,0:T(8,128)(2,1)S(1)}, u32[]{:S(2)}, u32[]{:S(2)}) %collective-permute-start.14) | collective-permute-done | bytes 131104 | tf_op jit(solution)/shard_map/ppermute | solution.py:319
  39.0 3.0 %collective-permute-start.15 = (bf16[256,256]{1,0:T(8,128)(2,1)S(1)}, bf16[256,256]{1,0:T(8,128)(2,1)S(1)}, u32[]{:S(2)}, u32[]{:S(2)}) collective-permute-start(bf16[256,256]{1,0:T(8,128)(2,1)S(1)} %shard_map.93), channel_id=1, source_target_pairs={{0,8},{1,9},{2,10},{3,11},{4,12},{5,13},{6,14},{7,15},{8,0},{9,1},... | collective-permute-start | bytes 393224 | tf_op jit(solution)/shard_map/ppermute | solution.py:319
  43.2 1.8 %collective-permute-start.17 = (bf16[256,256]{1,0:T(8,128)(2,1)S(1)}, bf16[256,256]{1,0:T(8,128)(2,1)S(1)}, u32[]{:S(2)}, u32[]{:S(2)}) collective-permute-start(bf16[256,256]{1,0:T(8,128)(2,1)S(1)} %get-tuple-element.59.refs_0_), channel_id=1, source_target_pairs={{0,16},{16,0},{1,17},{17,1},{2,18},{18,2},{3,19},{19,3},{4,20},{20... | collective-permute-start | bytes 393224 | tf_op jit(solution)/shard_map/ppermute | solution.py:319
  45.4 1.6 %collective-permute-done.10.refs_2_ = bf16[256,256]{1,0:T(8,128)(2,1)S(1)} collective-permute-done((bf16[256,256]{1,0:T(8,128)(2,1)S(1)}, bf16[256,256]{1,0:T(8,128)(2,1)S(1)}, u32[]{:S(2)}, u32[]{:S(2)}) %collective-permute-start.10) | collective-permute-done | bytes 131104 | tf_op jit(solution)/shard_map/ppermute | solution.py:319
  47.1 2.5 %collective-permute-done.15.rest_1_ = bf16[256,256]{1,0:T(8,128)(2,1)S(1)} collective-permute-done((bf16[256,256]{1,0:T(8,128)(2,1)S(1)}, bf16[256,256]{1,0:T(8,128)(2,1)S(1)}, u32[]{:S(2)}, u32[]{:S(2)}) %collective-permute-start.15) | collective-permute-done | bytes 131104 | tf_op jit(solution)/shard_map/ppermute | solution.py:319
  50.2 2.6 %collective-permute-start.22 = (bf16[256,256]{1,0:T(8,128)(2,1)S(1)}, bf16[256,256]{1,0:T(8,128)(2,1)S(1)}, u32[]{:S(2)}, u32[]{:S(2)}) collective-permute-start(bf16[256,256]{1,0:T(8,128)(2,1)S(1)} %get-tuple-element.51.refs_4_.x_ref.refs_0_.refs_5_), channel_id=1, source_target_pairs={{0,12},{1,13},{2,14},{3,15},{4,8},{5,9},{6,10},{7,11},{8,4},{9,5},... | collective-permute-start | bytes 393224 | tf_op jit(solution)/shard_map/ppermute | solution.py:319
  53.0 1.7 %collective-permute-done.20.refs_0_.refs_6_ = bf16[256,256]{1,0:T(8,128)(2,1)S(1)} collective-permute-done((bf16[256,256]{1,0:T(8,128)(2,1)S(1)}, bf16[256,256]{1,0:T(8,128)(2,1)S(1)}, u32[]{:S(2)}, u32[]{:S(2)}) %collective-permute-start.20) | collective-permute-done | bytes 131104 | tf_op jit(solution)/shard_map/ppermute | solution.py:319
  55.0 1.6 %collective-permute-done.24.refs_0_ = bf16[256,256]{1,0:T(8,128)(2,1)S(1)} collective-permute-done((bf16[256,256]{1,0:T(8,128)(2,1)S(1)}, bf16[256,256]{1,0:T(8,128)(2,1)S(1)}, u32[]{:S(2)}, u32[]{:S(2)}) %collective-permute-start.24) | collective-permute-done | bytes 131104 | tf_op jit(solution)/shard_map/ppermute | solution.py:319
  56.6 2.4 %collective-permute-start.25 = (bf16[256,256]{1,0:T(8,128)(2,1)S(1)}, bf16[256,256]{1,0:T(8,128)(2,1)S(1)}, u32[]{:S(2)}, u32[]{:S(2)}) collective-permute-start(bf16[256,256]{1,0:T(8,128)(2,1)S(1)} %collective-permute-done.24.refs_0_), channel_id=1, source_target_pairs={{0,2},{1,3},{2,0},{3,1},{4,6},{5,7},{6,4},{7,5},{8,10},{9,11},{10,... | collective-permute-start | bytes 393224 | tf_op jit(solution)/shard_map/ppermute | solution.py:319
  60.4 4.0 %collective-permute-done.21.refs_0_.refs_4_ = bf16[256,256]{1,0:T(8,128)(2,1)S(1)} collective-permute-done((bf16[256,256]{1,0:T(8,128)(2,1)S(1)}, bf16[256,256]{1,0:T(8,128)(2,1)S(1)}, u32[]{:S(2)}, u32[]{:S(2)}) %collective-permute-start.21) | collective-permute-done | bytes 131104 | tf_op jit(solution)/shard_map/ppermute | solution.py:319
  64.3 1.4 %collective-permute-start.30 = (bf16[256,256]{1,0:T(8,128)(2,1)S(1)}, bf16[256,256]{1,0:T(8,128)(2,1)S(1)}, u32[]{:S(2)}, u32[]{:S(2)}) collective-permute-start(bf16[256,256]{1,0:T(8,128)(2,1)S(1)} %collective-permute-done.21.refs_0_.refs_4_), channel_id=1, source_target_pairs={{0,2},{1,3},{2,0},{3,1},{4,6},{5,7},{6,4},{7,5},{8,10},{9,11},{10,... | collective-permute-start | bytes 393224 | tf_op jit(solution)/shard_map/ppermute | solution.py:319
  65.8 1.1 %shard_map.98 = (bf16[512,256]{1,0:T(8,128)(2,1)S(1)}, bf16[512,512]{1,0:T(8,128)(2,1)S(1)}) custom-call(bf16[256,256]{1,0:T(8,128)(2,1)S(1)} %collective-permute-done.24.refs_0_, bf16[256,256]{1,0:T(8,128)(2,1)S(1)} %collective-permute-done.25.refs_1_, bf16[256,256]{1,0:T(8,128)(2,1)S(1)} %get-tuple-element.61.refs_2_.refs_1_, ...), custom_call_target="tpu_custom_call" | custom-call | flops 268435456 | bytes 2400000 | tf_op jit(solution)/shard_map/pallas_call | solution.py:168
  67.6 1.2 %collective-permute-start.28 = (bf16[256,256]{1,0:T(8,128)(2,1)S(1)}, bf16[256,256]{1,0:T(8,128)(2,1)S(1)}, u32[]{:S(2)}, u32[]{:S(2)}) collective-permute-start(bf16[256,256]{1,0:T(8,128)(2,1)S(1)} %get-tuple-element.63.refs_5_), channel_id=1, source_target_pairs={{0,2},{1,3},{2,0},{3,1},{4,6},{5,7},{6,4},{7,5},{8,10},{9,11},{10,... | collective-permute-start | bytes 393224 | tf_op jit(solution)/shard_map/ppermute | solution.py:319
  73.0 2.3 %collective-permute-start.29 = (bf16[256,256]{1,0:T(8,128)(2,1)S(1)}, bf16[256,256]{1,0:T(8,128)(2,1)S(1)}, u32[]{:S(2)}, u32[]{:S(2)}) collective-permute-start(bf16[256,256]{1,0:T(8,128)(2,1)S(1)} %shard_map.105), channel_id=1, source_target_pairs={{0,12},{1,13},{2,14},{3,15},{4,8},{5,9},{6,10},{7,11},{8,4},{9,5},... | collective-permute-start | bytes 393224 | tf_op jit(solution)/shard_map/ppermute | solution.py:319
  77.6 2.3 %collective-permute-start.32 = (bf16[256,256]{1,0:T(8,128)(2,1)S(1)}, bf16[256,256]{1,0:T(8,128)(2,1)S(1)}, u32[]{:S(2)}, u32[]{:S(2)}) collective-permute-start(bf16[256,256]{1,0:T(8,128)(2,1)S(1)} %shard_map.108), channel_id=1, source_target_pairs={{0,8},{1,9},{2,10},{3,11},{4,12},{5,13},{6,14},{7,15},{8,0},{9,1},... | collective-permute-start | bytes 393224 | tf_op jit(solution)/shard_map/ppermute | solution.py:319
  79.9 1.4 %collective-permute-start.34 = (bf16[256,256]{1,0:T(8,128)(2,1)S(1)}, bf16[256,256]{1,0:T(8,128)(2,1)S(1)}, u32[]{:S(2)}, u32[]{:S(2)}) collective-permute-start(bf16[256,256]{1,0:T(8,128)(2,1)S(1)} %get-tuple-element.77.refs_0_), channel_id=1, source_target_pairs={{0,16},{16,0},{1,17},{17,1},{2,18},{18,2},{3,19},{19,3},{4,20},{20... | collective-permute-start | bytes 393224 | tf_op jit(solution)/shard_map/ppermute | solution.py:319
  82.1 4.4 %collective-permute-done.32.rest_1_ = bf16[256,256]{1,0:T(8,128)(2,1)S(1)} collective-permute-done((bf16[256,256]{1,0:T(8,128)(2,1)S(1)}, bf16[256,256]{1,0:T(8,128)(2,1)S(1)}, u32[]{:S(2)}, u32[]{:S(2)}) %collective-permute-start.32) | collective-permute-done | bytes 131104 | tf_op jit(solution)/shard_map/ppermute | solution.py:319
  (96 shorter events, 23.1 us)
Async XLA Ops:
  0.6 19.9 %collective-permute-start.1 = (bf16[80,8192]{1,0:T(8,128)(2,1)}, bf16[80,8192]{1,0:T(8,128)(2,1)S(1)}, u32[]{:S(2)}, u32[]{:S(2)}) collective-permute-start(bf16[80,8192]{1,0:T(8,128)(2,1)} %bitcast.5), channel_id=1, source_target_pairs={{0,1},{1,0},{2,3},{3,2},{4,5},{5,4},{6,7},{7,6},{8,9},{9,8},{10,11... | collective-permute-start | bytes 3932168 | tf_op jit(solution)/shard_map/ppermute | solution.py:319
  1.1 19.4 %collective-permute-start.2 = (bf16[80,8192]{1,0:T(8,128)(2,1)}, bf16[80,8192]{1,0:T(8,128)(2,1)S(1)}, u32[]{:S(2)}, u32[]{:S(2)}) collective-permute-start(bf16[80,8192]{1,0:T(8,128)(2,1)} %bitcast.7), channel_id=1, source_target_pairs={{0,1},{1,0},{2,3},{3,2},{4,5},{5,4},{6,7},{7,6},{8,9},{9,8},{10,11... | collective-permute-start | bytes 3932168 | tf_op jit(solution)/shard_map/ppermute | solution.py:319
  2.9 9.3 %collective-permute-start.3 = (bf16[256,256]{1,0:T(8,128)(2,1)S(1)}, bf16[256,256]{1,0:T(8,128)(2,1)S(1)}, u32[]{:S(2)}, u32[]{:S(2)}) collective-permute-start(bf16[256,256]{1,0:T(8,128)(2,1)S(1)} %get-tuple-element.42.x_ref.refs_0_.refs_5_), channel_id=1, source_target_pairs={{0,2},{1,3},{2,0},{3,1},{4,6},{5,7},{6,4},{7,5},{8,10},{9,11},{10,... | collective-permute-start | bytes 393224 | tf_op jit(solution)/shard_map/ppermute | solution.py:319
  5.9 11.6 %collective-permute-start.7 = (bf16[256,256]{1,0:T(8,128)(2,1)S(1)}, bf16[256,256]{1,0:T(8,128)(2,1)S(1)}, u32[]{:S(2)}, u32[]{:S(2)}) collective-permute-start(bf16[256,256]{1,0:T(8,128)(2,1)S(1)} %get-tuple-element.42.x_ref.refs_0_.refs_5_), channel_id=1, source_target_pairs={{0,4},{1,5},{2,6},{3,7},{4,0},{5,1},{6,2},{7,3},{8,12},{9,13},{10,... | collective-permute-start | bytes 393224 | tf_op jit(solution)/shard_map/ppermute | solution.py:319
  7.4 11.1 %collective-permute-start.5 = (bf16[256,256]{1,0:T(8,128)(2,1)S(1)}, bf16[256,256]{1,0:T(8,128)(2,1)S(1)}, u32[]{:S(2)}, u32[]{:S(2)}) collective-permute-start(bf16[256,256]{1,0:T(8,128)(2,1)S(1)} %get-tuple-element.42.x_ref.refs_0_.refs_5_), channel_id=1, source_target_pairs={{0,12},{1,13},{2,14},{3,15},{4,8},{5,9},{6,10},{7,11},{8,4},{9,5},... | collective-permute-start | bytes 393224 | tf_op jit(solution)/shard_map/ppermute | solution.py:319
  12.2 6.9 %collective-permute-start = (bf16[272,256]{1,0:T(8,128)(2,1)S(1)}, bf16[272,256]{1,0:T(8,128)(2,1)S(1)}, u32[]{:S(2)}, u32[]{:S(2)}) collective-permute-start(bf16[272,256]{1,0:T(8,128)(2,1)S(1)} %shard_map.78.refs_2_.refs_1_), channel_id=1, source_target_pairs={{0,1},{1,0},{2,3},{3,2},{4,5},{5,4},{6,7},{7,6},{8,9},{9,8},{10,11... | collective-permute-start | bytes 417800 | tf_op jit(solution)/shard_map/ppermute | solution.py:319
  17.4 9.2 %collective-permute-start.4 = (bf16[256,256]{1,0:T(8,128)(2,1)S(1)}, bf16[256,256]{1,0:T(8,128)(2,1)S(1)}, u32[]{:S(2)}, u32[]{:S(2)}) collective-permute-start(bf16[256,256]{1,0:T(8,128)(2,1)S(1)} %shard_map.81), channel_id=1, source_target_pairs={{0,8},{1,9},{2,10},{3,11},{4,12},{5,13},{6,14},{7,15},{8,0},{9,1},... | collective-permute-start | bytes 393224 | tf_op jit(solution)/shard_map/ppermute | solution.py:319
  18.5 9.4 %collective-permute-start.8 = (bf16[256,256]{1,0:T(8,128)(2,1)S(1)}, bf16[256,256]{1,0:T(8,128)(2,1)S(1)}, u32[]{:S(2)}, u32[]{:S(2)}) collective-permute-start(bf16[256,256]{1,0:T(8,128)(2,1)S(1)} %collective-permute-done.7.refs_0_), channel_id=1, source_target_pairs={{0,2},{1,3},{2,0},{3,1},{4,6},{5,7},{6,4},{7,5},{8,10},{9,11},{10,... | collective-permute-start | bytes 393224 | tf_op jit(solution)/shard_map/ppermute | solution.py:319
  19.1 10.0 %collective-permute-start.6 = (bf16[256,256]{1,0:T(8,128)(2,1)S(1)}, bf16[256,256]{1,0:T(8,128)(2,1)S(1)}, u32[]{:S(2)}, u32[]{:S(2)}) collective-permute-start(bf16[256,256]{1,0:T(8,128)(2,1)S(1)} %collective-permute-done.5.refs_0_.refs_3_), channel_id=1, source_target_pairs={{0,2},{1,3},{2,0},{3,1},{4,6},{5,7},{6,4},{7,5},{8,10},{9,11},{10,... | collective-permute-start | bytes 393224 | tf_op jit(solution)/shard_map/ppermute | solution.py:319
  26.7 6.6 %collective-permute-start.13 = (bf16[256,256]{1,0:T(8,128)(2,1)S(1)}, bf16[256,256]{1,0:T(8,128)(2,1)S(1)}, u32[]{:S(2)}, u32[]{:S(2)}) collective-permute-start(bf16[256,256]{1,0:T(8,128)(2,1)S(1)} %shard_map.91), channel_id=1, source_target_pairs={{0,2},{1,3},{2,0},{3,1},{4,6},{5,7},{6,4},{7,5},{8,10},{9,11},{10,... | collective-permute-start | bytes 393224 | tf_op jit(solution)/shard_map/ppermute | solution.py:319
  29.1 12.9 %collective-permute-start.9 = (bf16[512,256]{1,0:T(8,128)(2,1)S(1)}, bf16[512,256]{1,0:T(8,128)(2,1)S(1)}, u32[]{:S(2)}, u32[]{:S(2)}) collective-permute-start(bf16[512,256]{1,0:T(8,128)(2,1)S(1)} %get-tuple-element.43.refs_5_), channel_id=1, source_target_pairs={{0,4},{1,5},{2,6},{3,7},{4,0},{5,1},{6,2},{7,3},{8,12},{9,13},{10,... | collective-permute-start | bytes 786440 | tf_op jit(solution)/shard_map/ppermute | solution.py:319
  29.8 5.4 %collective-permute-start.11 = (bf16[256,256]{1,0:T(8,128)(2,1)S(1)}, bf16[256,256]{1,0:T(8,128)(2,1)S(1)}, u32[]{:S(2)}, u32[]{:S(2)}) collective-permute-start(bf16[256,256]{1,0:T(8,128)(2,1)S(1)} %get-tuple-element.44.refs_5_), channel_id=1, source_target_pairs={{0,2},{1,3},{2,0},{3,1},{4,6},{5,7},{6,4},{7,5},{8,10},{9,11},{10,... | collective-permute-start | bytes 393224 | tf_op jit(solution)/shard_map/ppermute | solution.py:319
  35.2 9.8 %collective-permute-start.12 = (bf16[256,256]{1,0:T(8,128)(2,1)S(1)}, bf16[256,256]{1,0:T(8,128)(2,1)S(1)}, u32[]{:S(2)}, u32[]{:S(2)}) collective-permute-start(bf16[256,256]{1,0:T(8,128)(2,1)S(1)} %shard_map.89), channel_id=1, source_target_pairs={{0,12},{1,13},{2,14},{3,15},{4,8},{5,9},{6,10},{7,11},{8,4},{9,5},... | collective-permute-start | bytes 393224 | tf_op jit(solution)/shard_map/ppermute | solution.py:319
  39.0 10.6 %collective-permute-start.15 = (bf16[256,256]{1,0:T(8,128)(2,1)S(1)}, bf16[256,256]{1,0:T(8,128)(2,1)S(1)}, u32[]{:S(2)}, u32[]{:S(2)}) collective-permute-start(bf16[256,256]{1,0:T(8,128)(2,1)S(1)} %shard_map.93), channel_id=1, source_target_pairs={{0,8},{1,9},{2,10},{3,11},{4,12},{5,13},{6,14},{7,15},{8,0},{9,1},... | collective-permute-start | bytes 393224 | tf_op jit(solution)/shard_map/ppermute | solution.py:319
  43.2 7.0 %collective-permute-start.17 = (bf16[256,256]{1,0:T(8,128)(2,1)S(1)}, bf16[256,256]{1,0:T(8,128)(2,1)S(1)}, u32[]{:S(2)}, u32[]{:S(2)}) collective-permute-start(bf16[256,256]{1,0:T(8,128)(2,1)S(1)} %get-tuple-element.59.refs_0_), channel_id=1, source_target_pairs={{0,16},{16,0},{1,17},{17,1},{2,18},{18,2},{3,19},{19,3},{4,20},{20... | collective-permute-start | bytes 393224 | tf_op jit(solution)/shard_map/ppermute | solution.py:319
  45.1 7.8 %collective-permute-start.18 = (bf16[256,256]{1,0:T(8,128)(2,1)S(1)}, bf16[256,256]{1,0:T(8,128)(2,1)S(1)}, u32[]{:S(2)}, u32[]{:S(2)}) collective-permute-start(bf16[256,256]{1,0:T(8,128)(2,1)S(1)} %get-tuple-element.60), channel_id=1, source_target_pairs={{0,17},{1,16},{2,19},{3,18},{4,21},{5,20},{6,23},{7,22},{8,25},{9,... | collective-permute-start | bytes 393224 | tf_op jit(solution)/shard_map/ppermute | solution.py:406
  45.1 7.8 %collective-permute-start.16 = (bf16[256,256]{1,0:T(8,128)(2,1)S(1)}, bf16[256,256]{1,0:T(8,128)(2,1)S(1)}, u32[]{:S(2)}, u32[]{:S(2)}) collective-permute-start(bf16[256,256]{1,0:T(8,128)(2,1)S(1)} %get-tuple-element.60), channel_id=1, source_target_pairs={{0,1},{1,0},{2,3},{3,2},{4,5},{5,4},{6,7},{7,6},{8,9},{9,8},{10,11... | collective-permute-start | bytes 393224 | tf_op jit(solution)/shard_map/ppermute | solution.py:319
  50.2 6.4 %collective-permute-start.24 = (bf16[256,256]{1,0:T(8,128)(2,1)S(1)}, bf16[256,256]{1,0:T(8,128)(2,1)S(1)}, u32[]{:S(2)}, u32[]{:S(2)}) collective-permute-start(bf16[256,256]{1,0:T(8,128)(2,1)S(1)} %get-tuple-element.51.refs_4_.x_ref.refs_0_.refs_5_), channel_id=1, source_target_pairs={{0,4},{1,5},{2,6},{3,7},{4,0},{5,1},{6,2},{7,3},{8,12},{9,13},{10,... | collective-permute-start | bytes 393224 | tf_op jit(solution)/shard_map/ppermute | solution.py:319
  50.2 9.5 %collective-permute-start.22 = (bf16[256,256]{1,0:T(8,128)(2,1)S(1)}, bf16[256,256]{1,0:T(8,128)(2,1)S(1)}, u32[]{:S(2)}, u32[]{:S(2)}) collective-permute-start(bf16[256,256]{1,0:T(8,128)(2,1)S(1)} %get-tuple-element.51.refs_4_.x_ref.refs_0_.refs_5_), channel_id=1, source_target_pairs={{0,12},{1,13},{2,14},{3,15},{4,8},{5,9},{6,10},{7,11},{8,4},{9,5},... | collective-permute-start | bytes 393224 | tf_op jit(solution)/shard_map/ppermute | solution.py:319
  54.7 9.7 %collective-permute-start.21 = (bf16[256,256]{1,0:T(8,128)(2,1)S(1)}, bf16[256,256]{1,0:T(8,128)(2,1)S(1)}, u32[]{:S(2)}, u32[]{:S(2)}) collective-permute-start(bf16[256,256]{1,0:T(8,128)(2,1)S(1)} %shard_map.97), channel_id=1, source_target_pairs={{0,8},{1,9},{2,10},{3,11},{4,12},{5,13},{6,14},{7,15},{8,0},{9,1},... | collective-permute-start | bytes 393224 | tf_op jit(solution)/shard_map/ppermute | solution.py:319
  55.0 10.8 %collective-permute-start.19 = (bf16[256,256]{1,0:T(8,128)(2,1)S(1)}, bf16[256,256]{1,0:T(8,128)(2,1)S(1)}, u32[]{:S(2)}, u32[]{:S(2)}) collective-permute-start(bf16[256,256]{1,0:T(8,128)(2,1)S(1)} %get-tuple-element.61.refs_2_.refs_1_), channel_id=1, source_target_pairs={{0,1},{1,0},{2,3},{3,2},{4,5},{5,4},{6,7},{7,6},{8,9},{9,8},{10,11... | collective-permute-start | bytes 393224 | tf_op jit(solution)/shard_map/ppermute | solution.py:319
  56.6 9.2 %collective-permute-start.25 = (bf16[256,256]{1,0:T(8,128)(2,1)S(1)}, bf16[256,256]{1,0:T(8,128)(2,1)S(1)}, u32[]{:S(2)}, u32[]{:S(2)}) collective-permute-start(bf16[256,256]{1,0:T(8,128)(2,1)S(1)} %collective-permute-done.24.refs_0_), channel_id=1, source_target_pairs={{0,2},{1,3},{2,0},{3,1},{4,6},{5,7},{6,4},{7,5},{8,10},{9,11},{10,... | collective-permute-start | bytes 393224 | tf_op jit(solution)/shard_map/ppermute | solution.py:319
  59.7 7.3 %collective-permute-start.23 = (bf16[256,256]{1,0:T(8,128)(2,1)S(1)}, bf16[256,256]{1,0:T(8,128)(2,1)S(1)}, u32[]{:S(2)}, u32[]{:S(2)}) collective-permute-start(bf16[256,256]{1,0:T(8,128)(2,1)S(1)} %collective-permute-done.22.refs_0_.refs_3_), channel_id=1, source_target_pairs={{0,2},{1,3},{2,0},{3,1},{4,6},{5,7},{6,4},{7,5},{8,10},{9,11},{10,... | collective-permute-start | bytes 393224 | tf_op jit(solution)/shard_map/ppermute | solution.py:319
  64.3 7.1 %collective-permute-start.30 = (bf16[256,256]{1,0:T(8,128)(2,1)S(1)}, bf16[256,256]{1,0:T(8,128)(2,1)S(1)}, u32[]{:S(2)}, u32[]{:S(2)}) collective-permute-start(bf16[256,256]{1,0:T(8,128)(2,1)S(1)} %collective-permute-done.21.refs_0_.refs_4_), channel_id=1, source_target_pairs={{0,2},{1,3},{2,0},{3,1},{4,6},{5,7},{6,4},{7,5},{8,10},{9,11},{10,... | collective-permute-start | bytes 393224 | tf_op jit(solution)/shard_map/ppermute | solution.py:319
  66.9 9.2 %collective-permute-start.26 = (bf16[512,256]{1,0:T(8,128)(2,1)S(1)}, bf16[512,256]{1,0:T(8,128)(2,1)S(1)}, u32[]{:S(2)}, u32[]{:S(2)}) collective-permute-start(bf16[512,256]{1,0:T(8,128)(2,1)S(1)} %get-tuple-element.62.refs_5_), channel_id=1, source_target_pairs={{0,4},{1,5},{2,6},{3,7},{4,0},{5,1},{6,2},{7,3},{8,12},{9,13},{10,... | collective-permute-start | bytes 786440 | tf_op jit(solution)/shard_map/ppermute | solution.py:319
  72.1 5.5 %collective-permute-start.31 = (bf16[256,256]{1,0:T(8,128)(2,1)S(1)}, bf16[256,256]{1,0:T(8,128)(2,1)S(1)}, u32[]{:S(2)}, u32[]{:S(2)}) collective-permute-start(bf16[256,256]{1,0:T(8,128)(2,1)S(1)} %get-tuple-element.68), channel_id=1, source_target_pairs={{0,2},{1,3},{2,0},{3,1},{4,6},{5,7},{6,4},{7,5},{8,10},{9,11},{10,... | collective-permute-start | bytes 393224 | tf_op jit(solution)/shard_map/ppermute | solution.py:319
  73.0 8.3 %collective-permute-start.29 = (bf16[256,256]{1,0:T(8,128)(2,1)S(1)}, bf16[256,256]{1,0:T(8,128)(2,1)S(1)}, u32[]{:S(2)}, u32[]{:S(2)}) collective-permute-start(bf16[256,256]{1,0:T(8,128)(2,1)S(1)} %shard_map.105), channel_id=1, source_target_pairs={{0,12},{1,13},{2,14},{3,15},{4,8},{5,9},{6,10},{7,11},{8,4},{9,5},... | collective-permute-start | bytes 393224 | tf_op jit(solution)/shard_map/ppermute | solution.py:319
  76.2 5.8 %collective-permute-start.27 = (bf16[256,256]{1,0:T(8,128)(2,1)S(1)}, bf16[256,256]{1,0:T(8,128)(2,1)S(1)}, u32[]{:S(2)}, u32[]{:S(2)}) collective-permute-start(bf16[256,256]{1,0:T(8,128)(2,1)S(1)} %shard_map.104), channel_id=1, source_target_pairs={{0,2},{1,3},{2,0},{3,1},{4,6},{5,7},{6,4},{7,5},{8,10},{9,11},{10,... | collective-permute-start | bytes 393224 | tf_op jit(solution)/shard_map/ppermute | solution.py:319
  77.6 8.9 %collective-permute-start.32 = (bf16[256,256]{1,0:T(8,128)(2,1)S(1)}, bf16[256,256]{1,0:T(8,128)(2,1)S(1)}, u32[]{:S(2)}, u32[]{:S(2)}) collective-permute-start(bf16[256,256]{1,0:T(8,128)(2,1)S(1)} %shard_map.108), channel_id=1, source_target_pairs={{0,8},{1,9},{2,10},{3,11},{4,12},{5,13},{6,14},{7,15},{8,0},{9,1},... | collective-permute-start | bytes 393224 | tf_op jit(solution)/shard_map/ppermute | solution.py:319
  79.9 7.4 %collective-permute-start.34 = (bf16[256,256]{1,0:T(8,128)(2,1)S(1)}, bf16[256,256]{1,0:T(8,128)(2,1)S(1)}, u32[]{:S(2)}, u32[]{:S(2)}) collective-permute-start(bf16[256,256]{1,0:T(8,128)(2,1)S(1)} %get-tuple-element.77.refs_0_), channel_id=1, source_target_pairs={{0,16},{16,0},{1,17},{17,1},{2,18},{18,2},{3,19},{19,3},{4,20},{20... | collective-permute-start | bytes 393224 | tf_op jit(solution)/shard_map/ppermute | solution.py:319
  81.3 5.9 %collective-permute-start.35 = (bf16[256,256]{1,0:T(8,128)(2,1)S(1)}, bf16[256,256]{1,0:T(8,128)(2,1)S(1)}, u32[]{:S(2)}, u32[]{:S(2)}) collective-permute-start(bf16[256,256]{1,0:T(8,128)(2,1)S(1)} %get-tuple-element.78), channel_id=1, source_target_pairs={{0,17},{1,16},{2,19},{3,18},{4,21},{5,20},{6,23},{7,22},{8,25},{9,... | collective-permute-start | bytes 393224 | tf_op jit(solution)/shard_map/ppermute | solution.py:406
  81.3 5.9 %collective-permute-start.33 = (bf16[256,256]{1,0:T(8,128)(2,1)S(1)}, bf16[256,256]{1,0:T(8,128)(2,1)S(1)}, u32[]{:S(2)}, u32[]{:S(2)}) collective-permute-start(bf16[256,256]{1,0:T(8,128)(2,1)S(1)} %get-tuple-element.78), channel_id=1, source_target_pairs={{0,1},{1,0},{2,3},{3,2},{4,5},{5,4},{6,7},{7,6},{8,9},{9,8},{10,11... | collective-permute-start | bytes 393224 | tf_op jit(solution)/shard_map/ppermute | solution.py:319
  (13 other events, 44.1 us)

commit v4 on v3

--- a/solution.py
+++ b/solution.py
@@ -196,9 +196,10 @@
     )(x, *after)
 
 
-def date_kernel(starts, *refs):
+def date_kernel(starts, now_ref, *refs):
     n = len(starts)
-    pixel_refs, errors_refs, (own_ref, other_ref) = refs[:n], refs[n:-2], refs[-2:]
+    pixel_refs, errors_refs, (own_ref, other_ref, rest_ref) = refs[:n], refs[n:-3], refs[-3:]
+    rest_ref[...] = (1.0 - DECAY) * now_ref[...]
     local = own_ref.shape[0]
     for k, out in enumerate((own_ref, other_ref)):
         total = None
@@ -209,17 +210,17 @@
         out[...] = total.astype(out.dtype)
 
 
-def date_gradient(errors, pixels, starts, local, after):
-    rank = pixels[0].shape[1]
+def date_gradient(now, errors, pixels, starts):
+    local, rank = now.shape
     n = len(pixels)
     return pl.pallas_call(
         functools.partial(date_kernel, starts),
-        out_shape=(jax.ShapeDtypeStruct((local, rank), BF16),) * 2,
-        in_specs=[VMEM] * (n + len(errors)) + [ANY] * len(after),
-        out_specs=(VMEM, VMEM),
+        out_shape=(jax.ShapeDtypeStruct((local, rank), BF16),) * 2 + (jax.ShapeDtypeStruct((local, rank), F32),),
+        in_specs=[VMEM] * (1 + n + len(errors)),
+        out_specs=(VMEM, VMEM, VMEM),
         compiler_params=params(32),
         cost_estimate=cost(4 * n * pixels[0].shape[0] * rank * local, n * 400000),
-    )(*pixels, *errors, *after)
+    )(now, *pixels, *errors)
 
 
 def sum_kernel(*refs):
@@ -244,48 +245,47 @@
     )(*[x for x, _ in parts])
 
 
-def pixel_kernel(scale, last, now_ref, *rest):
-    parts, outs = rest[:-2], rest[-2:]
+def pixel_kernel(scale, last, now_ref, *refs):
+    parts, out_ref, other_ref = refs[:2], refs[2], refs[3]
     rows, rank = now_ref.shape
     for start, target, half in row_pieces(rows):
         for lane in range(0, rank, LANES):
             at = (slice(start, start + half), slice(lane, lane + LANES))
-            grad = parts[0][at].astype(F32)
-            for part in parts[1:]:
-                grad = grad + part[at].astype(F32)
-            new = (1.0 - DECAY) * now_ref[at] - scale * grad
+            new = (1.0 - DECAY) * now_ref[at] - scale * (parts[0][at].astype(F32) + parts[1][at].astype(F32))
             if last:
-                outs[1][lane // LANES, target, :] = new
+                refs[4][lane // LANES, target, :] = new
             else:
-                outs[0][at] = new
-                outs[1][at] = new.astype(BF16)
+                out_ref[at] = new
+                other_ref[at] = new.astype(BF16)
     if last:
         for lane in range(0, rank, LANES):
-            outs[0][:, lane : lane + LANES] = outs[1][lane // LANES]
+            out_ref[:, lane : lane + LANES] = refs[4][lane // LANES]
+        other_ref[...] = jnp.zeros_like(other_ref)
 
 
 def pixel_update(scale, last, now, parts):
     full = jax.ShapeDtypeStruct(now.shape, F32)
     early = add([(part, 0) for part in parts[:-1]], F32)
+    other = jax.ShapeDtypeStruct((8, LANES), F32) if last else jax.ShapeDtypeStruct(now.shape, BF16)
     return pl.pallas_call(
         functools.partial(pixel_kernel, scale, last),
-        out_shape=(full,) if last else (full, jax.ShapeDtypeStruct(now.shape, BF16)),
+        out_shape=(full, other),
         in_specs=[VMEM] * 3,
-        out_specs=(VMEM,) if last else (VMEM, VMEM),
+        out_specs=(VMEM, VMEM),
         scratch_shapes=[pltpu.VMEM((now.shape[1] // LANES, now.shape[0], LANES), F32)] if last else [],
         compiler_params=params(16),
         cost_estimate=cost(10 * now.size, 8 * now.size),
     )(now, early, parts[-1])
 
 
-def date_update_kernel(scale, now_ref, *refs):
+def date_update_kernel(scale, rest_ref, *refs):
     parts, (after_ref, new_ref, bf_ref) = refs[:-3], refs[-3:]
     halves = [None, None]
     for i, part in enumerate(parts):
         side = 2 * i // len(parts)
         value = part[...].astype(F32)
         halves[side] = value if halves[side] is None else halves[side] + value
-    new = (1.0 - DECAY) * now_ref[...] - scale * (halves[0] + halves[1])
+    new = rest_ref[...] - scale * (halves[0] + halves[1])
     new_ref[...] = new
     bf_ref[...] = new.astype(BF16)
 
@@ -361,11 +361,10 @@
         for lo in far:
             pixels[0, lo] = swap(pixel_bf, 2 * lo)
         pixels[1, 0] = swap(pixel_bf, along[1])
-        pixels[2, 0] = swap(hold(pixel_bf, pixels[0, 1], *([] if step else [mine])), along[2])
+        pixels[2, 0] = swap(hold(pixel_bf, pixels[1, 0] if step else pixels[0, 1], *([] if step else [mine])), along[2])
         for lo in far:
             pixels[1, lo] = swap(pixels[1, 0], 2 * lo)
             pixels[3, lo] = swap(pixels[3, 0], 2 * lo)
-            pixels[2, lo] = swap(pixels[2, 0] if step else hold(pixels[2, 0], other), 2 * lo)
         errors, starts, ordered, after = [], [], [], []
 
         def terms(keys, kind, errors=errors, starts=starts, ordered=ordered, dates_bf=dates_bf,
@@ -382,7 +381,10 @@
             after = [term]
             return term
 
-        pair = swap(terms([(1, lo) for lo in range(low)], BF16), along[1])
+        pair = terms([(1, lo) for lo in range(low)], BF16)
+        for lo in far:
+            pixels[2, lo] = swap(hold(pixels[2, 0], pair), 2 * lo)
+        pair = swap(pair, along[1])
         recv3 = [(swap(terms([(3, lo)], BF16), 2 * lo), 0) for lo in far]
         near3 = terms([(3, 0)], F32)
         near2 = terms([(2, 0)], F32)
@@ -393,12 +395,8 @@
         part0 = [swap(add([(row0[lo - 1], 0), (pair, lo)], BF16), 2 * lo) for lo in far]
         part2 = swap(add([(near2, 0)] + recv2, BF16), along[2])
         parts = [near0, pair] + part0 + [part3, part2]
-        own, partner = date_gradient(errors, ordered, tuple(starts), local, [])
-        scale = STEP_SCALE / all_dates
-        if last:
-            (pixel_now,) = pixel_update(scale, True, pixel_now, parts)
-        else:
-            pixel_now, pixel_bf = pixel_update(scale, False, pixel_now, parts)
+        own, partner, dates_rest = date_gradient(dates_now, errors, ordered, tuple(starts))
+        pixel_now, pixel_bf = pixel_update(STEP_SCALE / all_dates, last, pixel_now, parts)
         sums = [own, swap(partner, 1)]
         if groups > 1:
             count = groups * loop_size
@@ -412,7 +410,7 @@
             sums.append(swap(sums[0], mask, "pix"))
             mask *= 2
         dates_now, dates_bf = date_update(
-            STEP_SCALE / all_pixels, dates_now, sums, pixel_now if last else pixel_bf
+            STEP_SCALE / all_pixels, dates_rest, sums, pixel_bf
         )
         if not last:
             dates_other = swap(dates_bf, 1)

time: 89.6 us -> 85.8 us (0.958)
  starting transfers between devices: 40 us -> 37.2 us
  local copies, waits for them, and re-layouts: 6.86 us -> 5.91 us
    ppermute x34, starting transfers between devices: 40 us -> 37.1 us  [swap(): lax.ppermute(x, axis, [(i, i ^ mask) for i in range(lax.axis_size(axis))])]
    unnamed x18 -> x16, local copies, waits for them, and re-layouts: 6.86 us -> 5.91 us
  transfers between devices with their start and end apart: 36 -> 36, of which waited for: 10 -> 14; matrix products, arithmetic and copies ran while one was open for 0% -> 0% of each run, Pallas kernels for 19% -> 19%
where the time goes in v4:
time: 85.8 us; the launch traced here: 84.9 us
  starting transfers between devices  37.2 us (43%)
  waiting for transfers between devices  22.9 us (27%)
  Pallas kernels  17.2 us (20%)
  local copies, waits for them, and re-layouts  5.91 us (7%)
  between operations  1.65 us (2%)
    ppermute x34, starting transfers between devices, swap(): lax.ppermute(x, axis, [(i, i ^ mask) for i in range(lax.axis_size(axis))])  37.1 us
    ppermute x34, waiting for transfers between devices, swap(): lax.ppermute(x, axis, [(i, i ^ mask) for i in range(lax.axis_size(axis))])  22.9 us
    pallas_call x14, Pallas kernels, chunk(): pl.pallas_call(functools.partial(chunk_kernel, n), grid=(1,), out_shape=(...  9.87 us
    unnamed x16, local copies, waits for them, and re-layouts  5.91 us
    pallas_call x2, Pallas kernels, place_blocks(): pl.pallas_call(functools.partial(place_kernel, copies, 2 * core_blocks),...  3.74 us
  transfers between devices with their start and end apart: 36, of which 14 were waited for; matrix products, arithmetic and copies ran while one was open for 0% of the time, Pallas kernels for 19%

profile of v4, /device:TPU:0, one launch (start us, length us, event | category | flops | bytes accessed | tf_op | source)
XLA Modules:
  0.0 84.9 jit_solution(5840275230601387054)
XLA Ops:
  1.2 0.9 %copy-done.4 = f32[256,256]{1,0:T(8,128)S(1)} copy-done((f32[256,256]{1,0:T(8,128)S(1)}, f32[256,256]{1,0:T(8,128)}, u32[]{:S(2)}) %copy-start.4) | copy-done | bytes 262168
  2.9 2.9 %collective-permute-start.3 = (bf16[256,256]{1,0:T(8,128)(2,1)S(1)}, bf16[256,256]{1,0:T(8,128)(2,1)S(1)}, u32[]{:S(2)}, u32[]{:S(2)}) collective-permute-start(bf16[256,256]{1,0:T(8,128)(2,1)S(1)} %get-tuple-element.46.x_ref.refs_0_.refs_5_), channel_id=1, source_target_pairs={{0,2},{1,3},{2,0},{3,1},{4,6},{5,7},{6,4},{7,5},{8,10},{9,11},{10,... | collective-permute-start | bytes 393224 | tf_op jit(solution)/shard_map/ppermute | solution.py:319
  5.9 1.6 %collective-permute-start.7 = (bf16[256,256]{1,0:T(8,128)(2,1)S(1)}, bf16[256,256]{1,0:T(8,128)(2,1)S(1)}, u32[]{:S(2)}, u32[]{:S(2)}) collective-permute-start(bf16[256,256]{1,0:T(8,128)(2,1)S(1)} %get-tuple-element.46.x_ref.refs_0_.refs_5_), channel_id=1, source_target_pairs={{0,4},{1,5},{2,6},{3,7},{4,0},{5,1},{6,2},{7,3},{8,12},{9,13},{10,... | collective-permute-start | bytes 393224 | tf_op jit(solution)/shard_map/ppermute | solution.py:319
  7.4 2.5 %collective-permute-start.5 = (bf16[256,256]{1,0:T(8,128)(2,1)S(1)}, bf16[256,256]{1,0:T(8,128)(2,1)S(1)}, u32[]{:S(2)}, u32[]{:S(2)}) collective-permute-start(bf16[256,256]{1,0:T(8,128)(2,1)S(1)} %get-tuple-element.46.x_ref.refs_0_.refs_5_), channel_id=1, source_target_pairs={{0,12},{1,13},{2,14},{3,15},{4,8},{5,9},{6,10},{7,11},{8,4},{9,5},... | collective-permute-start | bytes 393224 | tf_op jit(solution)/shard_map/ppermute | solution.py:319
  12.4 1.3 %copy-done = bf16[1,1,80,8192]{3,2,1,0:T(8,128)(2,1)S(1)} copy-done((bf16[1,1,80,8192]{3,2,1,0:T(8,128)(2,1)S(1)}, bf16[1,1,80,8192]{3,2,1,0:T(8,128)(2,1)}, u32[]{:S(2)}) %copy-start) | copy-done | bytes 1310744
  13.7 1.3 %copy-done.1 = bf16[1,1,80,8192]{3,2,1,0:T(8,128)(2,1)S(1)} copy-done((bf16[1,1,80,8192]{3,2,1,0:T(8,128)(2,1)S(1)}, bf16[1,1,80,8192]{3,2,1,0:T(8,128)(2,1)}, u32[]{:S(2)}) %copy-start.1) | copy-done | bytes 1310744
  15.0 1.9 %shard_map.79.refs_1_.refs_4_.refs_3_ = bf16[2,1088,512]{2,1,0:T(8,128)(2,1)S(1)} custom-call(s32[2]{0:T(128)S(1)} %pad_add_fusion.place_ref, s32[3,80]{1,0:T(4,128)S(1)} %slice_convert_fusion.1.ids_ref, bf16[80,8192]{1,0:T(8,128)(2,1)S(1)} %bitcast.6, bf16[80,8192]{1,0:T(8,128)(2,1)S(1)} %bitcast.8), custom_call_target="tpu_custom_call" | custom-call | flops 5242880 | bytes 5242880 | tf_op jit(solution)/shard_map/pallas_call | solution.py:105
  17.0 1.5 %collective-permute-start.4 = (bf16[256,256]{1,0:T(8,128)(2,1)S(1)}, bf16[256,256]{1,0:T(8,128)(2,1)S(1)}, u32[]{:S(2)}, u32[]{:S(2)}) collective-permute-start(bf16[256,256]{1,0:T(8,128)(2,1)S(1)} %shard_map.81), channel_id=1, source_target_pairs={{0,8},{1,9},{2,10},{3,11},{4,12},{5,13},{6,14},{7,15},{8,0},{9,1},... | collective-permute-start | bytes 393224 | tf_op jit(solution)/shard_map/ppermute | solution.py:319
  18.7 1.8 %collective-permute-start.6 = (bf16[256,256]{1,0:T(8,128)(2,1)S(1)}, bf16[256,256]{1,0:T(8,128)(2,1)S(1)}, u32[]{:S(2)}, u32[]{:S(2)}) collective-permute-start(bf16[256,256]{1,0:T(8,128)(2,1)S(1)} %collective-permute-done.5.refs_0_.refs_3_), channel_id=1, source_target_pairs={{0,2},{1,3},{2,0},{3,1},{4,6},{5,7},{6,4},{7,5},{8,10},{9,11},{10,... | collective-permute-start | bytes 393224 | tf_op jit(solution)/shard_map/ppermute | solution.py:319
  20.5 1.8 %shard_map.80.refs_5_.refs_4_ = bf16[2,1088,512]{2,1,0:T(8,128)(2,1)S(1)} custom-call(s32[2]{0:T(128)S(1)} %pad_add_fusion.place_ref, s32[3,80]{1,0:T(4,128)S(1)} %slice_convert_fusion.ids_ref, bf16[80,8192]{1,0:T(8,128)(2,1)S(1)} %collective-permute-done.1.values_ref, bf16[80,8192]{1,0:T(8,128)(2,1)S(1)} %collective-permute-done.2.weights_ref), custom_call_target="tpu_custom_call" | custom-call | flops 5242880 | bytes 5242880 | tf_op jit(solution)/shard_map/pallas_call | solution.py:105
  22.4 2.5 %collective-permute-done.8.refs_1_ = bf16[256,256]{1,0:T(8,128)(2,1)S(1)} collective-permute-done((bf16[256,256]{1,0:T(8,128)(2,1)S(1)}, bf16[256,256]{1,0:T(8,128)(2,1)S(1)}, u32[]{:S(2)}, u32[]{:S(2)}) %collective-permute-start.8) | collective-permute-done | bytes 131104 | tf_op jit(solution)/shard_map/ppermute | solution.py:319
  24.9 1.1 %shard_map.82 = (bf16[512,256]{1,0:T(8,128)(2,1)S(1)}, bf16[512,512]{1,0:T(8,128)(2,1)S(1)}) custom-call(bf16[256,256]{1,0:T(8,128)(2,1)S(1)} %collective-permute-done.7.refs_0_, bf16[256,256]{1,0:T(8,128)(2,1)S(1)} %collective-permute-done.8.refs_1_, bf16[272,256]{1,0:T(8,128)(2,1)S(1)} %shard_map.78.refs_2_.refs_1_, ...), custom_call_target="tpu_custom_call" | custom-call | flops 268435456 | bytes 2400000 | tf_op jit(solution)/shard_map/pallas_call | solution.py:168
  26.7 1.6 %collective-permute-start.13 = (bf16[256,256]{1,0:T(8,128)(2,1)S(1)}, bf16[256,256]{1,0:T(8,128)(2,1)S(1)}, u32[]{:S(2)}, u32[]{:S(2)}) collective-permute-start(bf16[256,256]{1,0:T(8,128)(2,1)S(1)} %shard_map.91), channel_id=1, source_target_pairs={{0,2},{1,3},{2,0},{3,1},{4,6},{5,7},{6,4},{7,5},{8,10},{9,11},{10,... | collective-permute-start | bytes 393224 | tf_op jit(solution)/shard_map/ppermute | solution.py:319
  33.3 2.0 %collective-permute-start.14 = (bf16[256,256]{1,0:T(8,128)(2,1)S(1)}, bf16[256,256]{1,0:T(8,128)(2,1)S(1)}, u32[]{:S(2)}, u32[]{:S(2)}) collective-permute-start(bf16[256,256]{1,0:T(8,128)(2,1)S(1)} %get-tuple-element.53), channel_id=1, source_target_pairs={{0,2},{1,3},{2,0},{3,1},{4,6},{5,7},{6,4},{7,5},{8,10},{9,11},{10,... | collective-permute-start | bytes 393224 | tf_op jit(solution)/shard_map/ppermute | solution.py:319
  35.3 1.9 %collective-permute-start.12 = (bf16[256,256]{1,0:T(8,128)(2,1)S(1)}, bf16[256,256]{1,0:T(8,128)(2,1)S(1)}, u32[]{:S(2)}, u32[]{:S(2)}) collective-permute-start(bf16[256,256]{1,0:T(8,128)(2,1)S(1)} %shard_map.89), channel_id=1, source_target_pairs={{0,12},{1,13},{2,14},{3,15},{4,8},{5,9},{6,10},{7,11},{8,4},{9,5},... | collective-permute-start | bytes 393224 | tf_op jit(solution)/shard_map/ppermute | solution.py:319
  37.2 1.0 %collective-permute-start.10 = (bf16[256,256]{1,0:T(8,128)(2,1)S(1)}, bf16[256,256]{1,0:T(8,128)(2,1)S(1)}, u32[]{:S(2)}, u32[]{:S(2)}) collective-permute-start(bf16[256,256]{1,0:T(8,128)(2,1)S(1)} %shard_map.88), channel_id=1, source_target_pairs={{0,2},{1,3},{2,0},{3,1},{4,6},{5,7},{6,4},{7,5},{8,10},{9,11},{10,... | collective-permute-start | bytes 393224 | tf_op jit(solution)/shard_map/ppermute | solution.py:319
  38.3 3.7 %collective-permute-start.15 = (bf16[256,256]{1,0:T(8,128)(2,1)S(1)}, bf16[256,256]{1,0:T(8,128)(2,1)S(1)}, u32[]{:S(2)}, u32[]{:S(2)}) collective-permute-start(bf16[256,256]{1,0:T(8,128)(2,1)S(1)} %shard_map.93), channel_id=1, source_target_pairs={{0,8},{1,9},{2,10},{3,11},{4,12},{5,13},{6,14},{7,15},{8,0},{9,1},... | collective-permute-start | bytes 393224 | tf_op jit(solution)/shard_map/ppermute | solution.py:319
  43.7 1.3 %collective-permute-start.17 = (bf16[256,256]{1,0:T(8,128)(2,1)S(1)}, bf16[256,256]{1,0:T(8,128)(2,1)S(1)}, u32[]{:S(2)}, u32[]{:S(2)}) collective-permute-start(bf16[256,256]{1,0:T(8,128)(2,1)S(1)} %get-tuple-element.64.refs_0_), channel_id=1, source_target_pairs={{0,16},{16,0},{1,17},{17,1},{2,18},{18,2},{3,19},{19,3},{4,20},{20... | collective-permute-start | bytes 393224 | tf_op jit(solution)/shard_map/ppermute | solution.py:319
  45.0 3.6 %collective-permute-done.15.refs_1_ = bf16[256,256]{1,0:T(8,128)(2,1)S(1)} collective-permute-done((bf16[256,256]{1,0:T(8,128)(2,1)S(1)}, bf16[256,256]{1,0:T(8,128)(2,1)S(1)}, u32[]{:S(2)}, u32[]{:S(2)}) %collective-permute-start.15) | collective-permute-done | bytes 131104 | tf_op jit(solution)/shard_map/ppermute | solution.py:319
  48.8 1.5 %collective-permute-start.22 = (bf16[256,256]{1,0:T(8,128)(2,1)S(1)}, bf16[256,256]{1,0:T(8,128)(2,1)S(1)}, u32[]{:S(2)}, u32[]{:S(2)}) collective-permute-start(bf16[256,256]{1,0:T(8,128)(2,1)S(1)} %get-tuple-element.55.refs_4_.x_ref.refs_0_.refs_5_), channel_id=1, source_target_pairs={{0,12},{1,13},{2,14},{3,15},{4,8},{5,9},{6,10},{7,11},{8,4},{9,5},... | collective-permute-start | bytes 393224 | tf_op jit(solution)/shard_map/ppermute | solution.py:319
  50.6 6.2 %collective-permute-done.20.refs_0_ = bf16[256,256]{1,0:T(8,128)(2,1)S(1)} collective-permute-done((bf16[256,256]{1,0:T(8,128)(2,1)S(1)}, bf16[256,256]{1,0:T(8,128)(2,1)S(1)}, u32[]{:S(2)}, u32[]{:S(2)}) %collective-permute-start.20) | collective-permute-done | bytes 131104 | tf_op jit(solution)/shard_map/ppermute | solution.py:319
  57.8 1.2 %collective-permute-start.23 = (bf16[256,256]{1,0:T(8,128)(2,1)S(1)}, bf16[256,256]{1,0:T(8,128)(2,1)S(1)}, u32[]{:S(2)}, u32[]{:S(2)}) collective-permute-start(bf16[256,256]{1,0:T(8,128)(2,1)S(1)} %collective-permute-done.22.refs_0_.refs_3_), channel_id=1, source_target_pairs={{0,2},{1,3},{2,0},{3,1},{4,6},{5,7},{6,4},{7,5},{8,10},{9,11},{10,... | collective-permute-start | bytes 393224 | tf_op jit(solution)/shard_map/ppermute | solution.py:319
  59.9 2.3 %collective-permute-done.24.refs_1_ = bf16[256,256]{1,0:T(8,128)(2,1)S(1)} collective-permute-done((bf16[256,256]{1,0:T(8,128)(2,1)S(1)}, bf16[256,256]{1,0:T(8,128)(2,1)S(1)}, u32[]{:S(2)}, u32[]{:S(2)}) %collective-permute-start.24) | collective-permute-done | bytes 131104 | tf_op jit(solution)/shard_map/ppermute | solution.py:319
  62.3 1.1 %shard_map.98 = (bf16[512,256]{1,0:T(8,128)(2,1)S(1)}, bf16[512,512]{1,0:T(8,128)(2,1)S(1)}) custom-call(bf16[256,256]{1,0:T(8,128)(2,1)S(1)} %collective-permute-done.20.refs_0_, bf16[256,256]{1,0:T(8,128)(2,1)S(1)} %collective-permute-done.24.refs_1_, bf16[256,256]{1,0:T(8,128)(2,1)S(1)} %get-tuple-element.66.refs_2_.refs_1_, ...), custom_call_target="tpu_custom_call" | custom-call | flops 268435456 | bytes 2400000 | tf_op jit(solution)/shard_map/pallas_call | solution.py:168
  64.1 1.1 %collective-permute-start.30 = (bf16[256,256]{1,0:T(8,128)(2,1)S(1)}, bf16[256,256]{1,0:T(8,128)(2,1)S(1)}, u32[]{:S(2)}, u32[]{:S(2)}) collective-permute-start(bf16[256,256]{1,0:T(8,128)(2,1)S(1)} %shard_map.107), channel_id=1, source_target_pairs={{0,2},{1,3},{2,0},{3,1},{4,6},{5,7},{6,4},{7,5},{8,10},{9,11},{10,... | collective-permute-start | bytes 393224 | tf_op jit(solution)/shard_map/ppermute | solution.py:319
  65.8 1.1 %collective-permute-start.28 = (bf16[256,256]{1,0:T(8,128)(2,1)S(1)}, bf16[256,256]{1,0:T(8,128)(2,1)S(1)}, u32[]{:S(2)}, u32[]{:S(2)}) collective-permute-start(bf16[256,256]{1,0:T(8,128)(2,1)S(1)} %get-tuple-element.68.refs_5_), channel_id=1, source_target_pairs={{0,2},{1,3},{2,0},{3,1},{4,6},{5,7},{6,4},{7,5},{8,10},{9,11},{10,... | collective-permute-start | bytes 393224 | tf_op jit(solution)/shard_map/ppermute | solution.py:319
  70.1 1.1 %collective-permute-start.31 = (bf16[256,256]{1,0:T(8,128)(2,1)S(1)}, bf16[256,256]{1,0:T(8,128)(2,1)S(1)}, u32[]{:S(2)}, u32[]{:S(2)}) collective-permute-start(bf16[256,256]{1,0:T(8,128)(2,1)S(1)} %get-tuple-element.73), channel_id=1, source_target_pairs={{0,2},{1,3},{2,0},{3,1},{4,6},{5,7},{6,4},{7,5},{8,10},{9,11},{10,... | collective-permute-start | bytes 393224 | tf_op jit(solution)/shard_map/ppermute | solution.py:319
  71.2 0.9 %collective-permute-done.28.refs_1_ = bf16[256,256]{1,0:T(8,128)(2,1)S(1)} collective-permute-done((bf16[256,256]{1,0:T(8,128)(2,1)S(1)}, bf16[256,256]{1,0:T(8,128)(2,1)S(1)}, u32[]{:S(2)}, u32[]{:S(2)}) %collective-permute-start.28) | collective-permute-done | bytes 131104 | tf_op jit(solution)/shard_map/ppermute | solution.py:319
  72.1 1.8 %collective-permute-start.29 = (bf16[256,256]{1,0:T(8,128)(2,1)S(1)}, bf16[256,256]{1,0:T(8,128)(2,1)S(1)}, u32[]{:S(2)}, u32[]{:S(2)}) collective-permute-start(bf16[256,256]{1,0:T(8,128)(2,1)S(1)} %shard_map.105), channel_id=1, source_target_pairs={{0,12},{1,13},{2,14},{3,15},{4,8},{5,9},{6,10},{7,11},{8,4},{9,5},... | collective-permute-start | bytes 393224 | tf_op jit(solution)/shard_map/ppermute | solution.py:319
  76.0 1.5 %collective-permute-start.32 = (bf16[256,256]{1,0:T(8,128)(2,1)S(1)}, bf16[256,256]{1,0:T(8,128)(2,1)S(1)}, u32[]{:S(2)}, u32[]{:S(2)}) collective-permute-start(bf16[256,256]{1,0:T(8,128)(2,1)S(1)} %shard_map.109), channel_id=1, source_target_pairs={{0,8},{1,9},{2,10},{3,11},{4,12},{5,13},{6,14},{7,15},{8,0},{9,1},... | collective-permute-start | bytes 393224 | tf_op jit(solution)/shard_map/ppermute | solution.py:319
  77.6 1.5 %collective-permute-done.29.refs_3_ = bf16[256,256]{1,0:T(8,128)(2,1)S(1)} collective-permute-done((bf16[256,256]{1,0:T(8,128)(2,1)S(1)}, bf16[256,256]{1,0:T(8,128)(2,1)S(1)}, u32[]{:S(2)}, u32[]{:S(2)}) %collective-permute-start.29) | collective-permute-done | bytes 131104 | tf_op jit(solution)/shard_map/ppermute | solution.py:319
  79.8 3.5 %collective-permute-done.32.refs_1_ = bf16[256,256]{1,0:T(8,128)(2,1)S(1)} collective-permute-done((bf16[256,256]{1,0:T(8,128)(2,1)S(1)}, bf16[256,256]{1,0:T(8,128)(2,1)S(1)}, u32[]{:S(2)}, u32[]{:S(2)}) %collective-permute-start.32) | collective-permute-done | bytes 131104 | tf_op jit(solution)/shard_map/ppermute | solution.py:319
  (95 shorter events, 22.1 us)
Async XLA Ops:
  0.6 19.9 %collective-permute-start.1 = (bf16[80,8192]{1,0:T(8,128)(2,1)}, bf16[80,8192]{1,0:T(8,128)(2,1)S(1)}, u32[]{:S(2)}, u32[]{:S(2)}) collective-permute-start(bf16[80,8192]{1,0:T(8,128)(2,1)} %bitcast.5), channel_id=1, source_target_pairs={{0,1},{1,0},{2,3},{3,2},{4,5},{5,4},{6,7},{7,6},{8,9},{9,8},{10,11... | collective-permute-start | bytes 3932168 | tf_op jit(solution)/shard_map/ppermute | solution.py:319
  1.1 19.4 %collective-permute-start.2 = (bf16[80,8192]{1,0:T(8,128)(2,1)}, bf16[80,8192]{1,0:T(8,128)(2,1)S(1)}, u32[]{:S(2)}, u32[]{:S(2)}) collective-permute-start(bf16[80,8192]{1,0:T(8,128)(2,1)} %bitcast.7), channel_id=1, source_target_pairs={{0,1},{1,0},{2,3},{3,2},{4,5},{5,4},{6,7},{7,6},{8,9},{9,8},{10,11... | collective-permute-start | bytes 3932168 | tf_op jit(solution)/shard_map/ppermute | solution.py:319
  2.9 9.3 %collective-permute-start.3 = (bf16[256,256]{1,0:T(8,128)(2,1)S(1)}, bf16[256,256]{1,0:T(8,128)(2,1)S(1)}, u32[]{:S(2)}, u32[]{:S(2)}) collective-permute-start(bf16[256,256]{1,0:T(8,128)(2,1)S(1)} %get-tuple-element.46.x_ref.refs_0_.refs_5_), channel_id=1, source_target_pairs={{0,2},{1,3},{2,0},{3,1},{4,6},{5,7},{6,4},{7,5},{8,10},{9,11},{10,... | collective-permute-start | bytes 393224 | tf_op jit(solution)/shard_map/ppermute | solution.py:319
  5.9 11.1 %collective-permute-start.7 = (bf16[256,256]{1,0:T(8,128)(2,1)S(1)}, bf16[256,256]{1,0:T(8,128)(2,1)S(1)}, u32[]{:S(2)}, u32[]{:S(2)}) collective-permute-start(bf16[256,256]{1,0:T(8,128)(2,1)S(1)} %get-tuple-element.46.x_ref.refs_0_.refs_5_), channel_id=1, source_target_pairs={{0,4},{1,5},{2,6},{3,7},{4,0},{5,1},{6,2},{7,3},{8,12},{9,13},{10,... | collective-permute-start | bytes 393224 | tf_op jit(solution)/shard_map/ppermute | solution.py:319
  7.4 11.1 %collective-permute-start.5 = (bf16[256,256]{1,0:T(8,128)(2,1)S(1)}, bf16[256,256]{1,0:T(8,128)(2,1)S(1)}, u32[]{:S(2)}, u32[]{:S(2)}) collective-permute-start(bf16[256,256]{1,0:T(8,128)(2,1)S(1)} %get-tuple-element.46.x_ref.refs_0_.refs_5_), channel_id=1, source_target_pairs={{0,12},{1,13},{2,14},{3,15},{4,8},{5,9},{6,10},{7,11},{8,4},{9,5},... | collective-permute-start | bytes 393224 | tf_op jit(solution)/shard_map/ppermute | solution.py:319
  12.2 6.4 %collective-permute-start = (bf16[272,256]{1,0:T(8,128)(2,1)S(1)}, bf16[272,256]{1,0:T(8,128)(2,1)S(1)}, u32[]{:S(2)}, u32[]{:S(2)}) collective-permute-start(bf16[272,256]{1,0:T(8,128)(2,1)S(1)} %shard_map.78.refs_2_.refs_1_), channel_id=1, source_target_pairs={{0,1},{1,0},{2,3},{3,2},{4,5},{5,4},{6,7},{7,6},{8,9},{9,8},{10,11... | collective-permute-start | bytes 417800 | tf_op jit(solution)/shard_map/ppermute | solution.py:319
  17.0 9.6 %collective-permute-start.4 = (bf16[256,256]{1,0:T(8,128)(2,1)S(1)}, bf16[256,256]{1,0:T(8,128)(2,1)S(1)}, u32[]{:S(2)}, u32[]{:S(2)}) collective-permute-start(bf16[256,256]{1,0:T(8,128)(2,1)S(1)} %shard_map.81), channel_id=1, source_target_pairs={{0,8},{1,9},{2,10},{3,11},{4,12},{5,13},{6,14},{7,15},{8,0},{9,1},... | collective-permute-start | bytes 393224 | tf_op jit(solution)/shard_map/ppermute | solution.py:319
  18.5 6.4 %collective-permute-start.8 = (bf16[256,256]{1,0:T(8,128)(2,1)S(1)}, bf16[256,256]{1,0:T(8,128)(2,1)S(1)}, u32[]{:S(2)}, u32[]{:S(2)}) collective-permute-start(bf16[256,256]{1,0:T(8,128)(2,1)S(1)} %collective-permute-done.7.refs_0_), channel_id=1, source_target_pairs={{0,2},{1,3},{2,0},{3,1},{4,6},{5,7},{6,4},{7,5},{8,10},{9,11},{10,... | collective-permute-start | bytes 393224 | tf_op jit(solution)/shard_map/ppermute | solution.py:319
  18.7 10.5 %collective-permute-start.6 = (bf16[256,256]{1,0:T(8,128)(2,1)S(1)}, bf16[256,256]{1,0:T(8,128)(2,1)S(1)}, u32[]{:S(2)}, u32[]{:S(2)}) collective-permute-start(bf16[256,256]{1,0:T(8,128)(2,1)S(1)} %collective-permute-done.5.refs_0_.refs_3_), channel_id=1, source_target_pairs={{0,2},{1,3},{2,0},{3,1},{4,6},{5,7},{6,4},{7,5},{8,10},{9,11},{10,... | collective-permute-start | bytes 393224 | tf_op jit(solution)/shard_map/ppermute | solution.py:319
  26.7 6.0 %collective-permute-start.13 = (bf16[256,256]{1,0:T(8,128)(2,1)S(1)}, bf16[256,256]{1,0:T(8,128)(2,1)S(1)}, u32[]{:S(2)}, u32[]{:S(2)}) collective-permute-start(bf16[256,256]{1,0:T(8,128)(2,1)S(1)} %shard_map.91), channel_id=1, source_target_pairs={{0,2},{1,3},{2,0},{3,1},{4,6},{5,7},{6,4},{7,5},{8,10},{9,11},{10,... | collective-permute-start | bytes 393224 | tf_op jit(solution)/shard_map/ppermute | solution.py:319
  28.2 9.0 %collective-permute-start.9 = (bf16[512,256]{1,0:T(8,128)(2,1)S(1)}, bf16[512,256]{1,0:T(8,128)(2,1)S(1)}, u32[]{:S(2)}, u32[]{:S(2)}) collective-permute-start(bf16[512,256]{1,0:T(8,128)(2,1)S(1)} %get-tuple-element.47.refs_5_.refs_0_), channel_id=1, source_target_pairs={{0,4},{1,5},{2,6},{3,7},{4,0},{5,1},{6,2},{7,3},{8,12},{9,13},{10,... | collective-permute-start | bytes 786440 | tf_op jit(solution)/shard_map/ppermute | solution.py:319
  29.8 5.5 %collective-permute-start.11 = (bf16[256,256]{1,0:T(8,128)(2,1)S(1)}, bf16[256,256]{1,0:T(8,128)(2,1)S(1)}, u32[]{:S(2)}, u32[]{:S(2)}) collective-permute-start(bf16[256,256]{1,0:T(8,128)(2,1)S(1)} %get-tuple-element.48.refs_5_), channel_id=1, source_target_pairs={{0,2},{1,3},{2,0},{3,1},{4,6},{5,7},{6,4},{7,5},{8,10},{9,11},{10,... | collective-permute-start | bytes 393224 | tf_op jit(solution)/shard_map/ppermute | solution.py:319
  35.3 8.3 %collective-permute-start.12 = (bf16[256,256]{1,0:T(8,128)(2,1)S(1)}, bf16[256,256]{1,0:T(8,128)(2,1)S(1)}, u32[]{:S(2)}, u32[]{:S(2)}) collective-permute-start(bf16[256,256]{1,0:T(8,128)(2,1)S(1)} %shard_map.89), channel_id=1, source_target_pairs={{0,12},{1,13},{2,14},{3,15},{4,8},{5,9},{6,10},{7,11},{8,4},{9,5},... | collective-permute-start | bytes 393224 | tf_op jit(solution)/shard_map/ppermute | solution.py:319
  37.2 7.7 %collective-permute-start.10 = (bf16[256,256]{1,0:T(8,128)(2,1)S(1)}, bf16[256,256]{1,0:T(8,128)(2,1)S(1)}, u32[]{:S(2)}, u32[]{:S(2)}) collective-permute-start(bf16[256,256]{1,0:T(8,128)(2,1)S(1)} %shard_map.88), channel_id=1, source_target_pairs={{0,2},{1,3},{2,0},{3,1},{4,6},{5,7},{6,4},{7,5},{8,10},{9,11},{10,... | collective-permute-start | bytes 393224 | tf_op jit(solution)/shard_map/ppermute | solution.py:319
  38.3 10.3 %collective-permute-start.15 = (bf16[256,256]{1,0:T(8,128)(2,1)S(1)}, bf16[256,256]{1,0:T(8,128)(2,1)S(1)}, u32[]{:S(2)}, u32[]{:S(2)}) collective-permute-start(bf16[256,256]{1,0:T(8,128)(2,1)S(1)} %shard_map.93), channel_id=1, source_target_pairs={{0,8},{1,9},{2,10},{3,11},{4,12},{5,13},{6,14},{7,15},{8,0},{9,1},... | collective-permute-start | bytes 393224 | tf_op jit(solution)/shard_map/ppermute | solution.py:319
  42.8 7.6 %collective-permute-start.18 = (bf16[256,256]{1,0:T(8,128)(2,1)S(1)}, bf16[256,256]{1,0:T(8,128)(2,1)S(1)}, u32[]{:S(2)}, u32[]{:S(2)}) collective-permute-start(bf16[256,256]{1,0:T(8,128)(2,1)S(1)} %get-tuple-element.65), channel_id=1, source_target_pairs={{0,17},{1,16},{2,19},{3,18},{4,21},{5,20},{6,23},{7,22},{8,25},{9,... | collective-permute-start | bytes 393224 | tf_op jit(solution)/shard_map/ppermute | solution.py:404
  42.8 7.5 %collective-permute-start.16 = (bf16[256,256]{1,0:T(8,128)(2,1)S(1)}, bf16[256,256]{1,0:T(8,128)(2,1)S(1)}, u32[]{:S(2)}, u32[]{:S(2)}) collective-permute-start(bf16[256,256]{1,0:T(8,128)(2,1)S(1)} %get-tuple-element.65), channel_id=1, source_target_pairs={{0,1},{1,0},{2,3},{3,2},{4,5},{5,4},{6,7},{7,6},{8,9},{9,8},{10,11... | collective-permute-start | bytes 393224 | tf_op jit(solution)/shard_map/ppermute | solution.py:319
  43.7 6.7 %collective-permute-start.17 = (bf16[256,256]{1,0:T(8,128)(2,1)S(1)}, bf16[256,256]{1,0:T(8,128)(2,1)S(1)}, u32[]{:S(2)}, u32[]{:S(2)}) collective-permute-start(bf16[256,256]{1,0:T(8,128)(2,1)S(1)} %get-tuple-element.64.refs_0_), channel_id=1, source_target_pairs={{0,16},{16,0},{1,17},{17,1},{2,18},{18,2},{3,19},{19,3},{4,20},{20... | collective-permute-start | bytes 393224 | tf_op jit(solution)/shard_map/ppermute | solution.py:319
  48.7 8.1 %collective-permute-start.20 = (bf16[256,256]{1,0:T(8,128)(2,1)S(1)}, bf16[256,256]{1,0:T(8,128)(2,1)S(1)}, u32[]{:S(2)}, u32[]{:S(2)}) collective-permute-start(bf16[256,256]{1,0:T(8,128)(2,1)S(1)} %get-tuple-element.55.refs_4_.x_ref.refs_0_.refs_5_), channel_id=1, source_target_pairs={{0,4},{1,5},{2,6},{3,7},{4,0},{5,1},{6,2},{7,3},{8,12},{9,13},{10,... | collective-permute-start | bytes 393224 | tf_op jit(solution)/shard_map/ppermute | solution.py:319
  48.8 9.0 %collective-permute-start.22 = (bf16[256,256]{1,0:T(8,128)(2,1)S(1)}, bf16[256,256]{1,0:T(8,128)(2,1)S(1)}, u32[]{:S(2)}, u32[]{:S(2)}) collective-permute-start(bf16[256,256]{1,0:T(8,128)(2,1)S(1)} %get-tuple-element.55.refs_4_.x_ref.refs_0_.refs_5_), channel_id=1, source_target_pairs={{0,12},{1,13},{2,14},{3,15},{4,8},{5,9},{6,10},{7,11},{8,4},{9,5},... | collective-permute-start | bytes 393224 | tf_op jit(solution)/shard_map/ppermute | solution.py:319
  50.4 9.5 %collective-permute-start.19 = (bf16[256,256]{1,0:T(8,128)(2,1)S(1)}, bf16[256,256]{1,0:T(8,128)(2,1)S(1)}, u32[]{:S(2)}, u32[]{:S(2)}) collective-permute-start(bf16[256,256]{1,0:T(8,128)(2,1)S(1)} %get-tuple-element.66.refs_2_.refs_1_), channel_id=1, source_target_pairs={{0,1},{1,0},{2,3},{3,2},{4,5},{5,4},{6,7},{7,6},{8,9},{9,8},{10,11... | collective-permute-start | bytes 393224 | tf_op jit(solution)/shard_map/ppermute | solution.py:319
  56.8 5.5 %collective-permute-start.24 = (bf16[256,256]{1,0:T(8,128)(2,1)S(1)}, bf16[256,256]{1,0:T(8,128)(2,1)S(1)}, u32[]{:S(2)}, u32[]{:S(2)}) collective-permute-start(bf16[256,256]{1,0:T(8,128)(2,1)S(1)} %collective-permute-done.20.refs_0_), channel_id=1, source_target_pairs={{0,2},{1,3},{2,0},{3,1},{4,6},{5,7},{6,4},{7,5},{8,10},{9,11},{10,... | collective-permute-start | bytes 393224 | tf_op jit(solution)/shard_map/ppermute | solution.py:319
  57.7 6.3 %collective-permute-start.21 = (bf16[256,256]{1,0:T(8,128)(2,1)S(1)}, bf16[256,256]{1,0:T(8,128)(2,1)S(1)}, u32[]{:S(2)}, u32[]{:S(2)}) collective-permute-start(bf16[256,256]{1,0:T(8,128)(2,1)S(1)} %shard_map.97), channel_id=1, source_target_pairs={{0,8},{1,9},{2,10},{3,11},{4,12},{5,13},{6,14},{7,15},{8,0},{9,1},... | collective-permute-start | bytes 393224 | tf_op jit(solution)/shard_map/ppermute | solution.py:319
  57.8 7.3 %collective-permute-start.23 = (bf16[256,256]{1,0:T(8,128)(2,1)S(1)}, bf16[256,256]{1,0:T(8,128)(2,1)S(1)}, u32[]{:S(2)}, u32[]{:S(2)}) collective-permute-start(bf16[256,256]{1,0:T(8,128)(2,1)S(1)} %collective-permute-done.22.refs_0_.refs_3_), channel_id=1, source_target_pairs={{0,2},{1,3},{2,0},{3,1},{4,6},{5,7},{6,4},{7,5},{8,10},{9,11},{10,... | collective-permute-start | bytes 393224 | tf_op jit(solution)/shard_map/ppermute | solution.py:319
  59.0 9.7 %collective-permute-start.26 = (bf16[256,256]{1,0:T(8,128)(2,1)S(1)}, bf16[256,256]{1,0:T(8,128)(2,1)S(1)}, u32[]{:S(2)}, u32[]{:S(2)}) collective-permute-start(bf16[256,256]{1,0:T(8,128)(2,1)S(1)} %get-tuple-element.55.refs_4_.x_ref.refs_0_.refs_5_), channel_id=1, source_target_pairs={{0,2},{1,3},{2,0},{3,1},{4,6},{5,7},{6,4},{7,5},{8,10},{9,11},{10,... | collective-permute-start | bytes 393224 | tf_op jit(solution)/shard_map/ppermute | solution.py:319
  65.2 9.5 %collective-permute-start.25 = (bf16[512,256]{1,0:T(8,128)(2,1)S(1)}, bf16[512,256]{1,0:T(8,128)(2,1)S(1)}, u32[]{:S(2)}, u32[]{:S(2)}) collective-permute-start(bf16[512,256]{1,0:T(8,128)(2,1)S(1)} %get-tuple-element.67.refs_5_.refs_0_), channel_id=1, source_target_pairs={{0,4},{1,5},{2,6},{3,7},{4,0},{5,1},{6,2},{7,3},{8,12},{9,13},{10,... | collective-permute-start | bytes 786440 | tf_op jit(solution)/shard_map/ppermute | solution.py:319
  65.8 6.3 %collective-permute-start.28 = (bf16[256,256]{1,0:T(8,128)(2,1)S(1)}, bf16[256,256]{1,0:T(8,128)(2,1)S(1)}, u32[]{:S(2)}, u32[]{:S(2)}) collective-permute-start(bf16[256,256]{1,0:T(8,128)(2,1)S(1)} %get-tuple-element.68.refs_5_), channel_id=1, source_target_pairs={{0,2},{1,3},{2,0},{3,1},{4,6},{5,7},{6,4},{7,5},{8,10},{9,11},{10,... | collective-permute-start | bytes 393224 | tf_op jit(solution)/shard_map/ppermute | solution.py:319
  70.1 5.8 %collective-permute-start.31 = (bf16[256,256]{1,0:T(8,128)(2,1)S(1)}, bf16[256,256]{1,0:T(8,128)(2,1)S(1)}, u32[]{:S(2)}, u32[]{:S(2)}) collective-permute-start(bf16[256,256]{1,0:T(8,128)(2,1)S(1)} %get-tuple-element.73), channel_id=1, source_target_pairs={{0,2},{1,3},{2,0},{3,1},{4,6},{5,7},{6,4},{7,5},{8,10},{9,11},{10,... | collective-permute-start | bytes 393224 | tf_op jit(solution)/shard_map/ppermute | solution.py:319
  72.1 6.9 %collective-permute-start.29 = (bf16[256,256]{1,0:T(8,128)(2,1)S(1)}, bf16[256,256]{1,0:T(8,128)(2,1)S(1)}, u32[]{:S(2)}, u32[]{:S(2)}) collective-permute-start(bf16[256,256]{1,0:T(8,128)(2,1)S(1)} %shard_map.105), channel_id=1, source_target_pairs={{0,12},{1,13},{2,14},{3,15},{4,8},{5,9},{6,10},{7,11},{8,4},{9,5},... | collective-permute-start | bytes 393224 | tf_op jit(solution)/shard_map/ppermute | solution.py:319
  76.0 7.3 %collective-permute-start.32 = (bf16[256,256]{1,0:T(8,128)(2,1)S(1)}, bf16[256,256]{1,0:T(8,128)(2,1)S(1)}, u32[]{:S(2)}, u32[]{:S(2)}) collective-permute-start(bf16[256,256]{1,0:T(8,128)(2,1)S(1)} %shard_map.109), channel_id=1, source_target_pairs={{0,8},{1,9},{2,10},{3,11},{4,12},{5,13},{6,14},{7,15},{8,0},{9,1},... | collective-permute-start | bytes 393224 | tf_op jit(solution)/shard_map/ppermute | solution.py:319
  77.5 6.6 %collective-permute-start.34 = (bf16[256,256]{1,0:T(8,128)(2,1)S(1)}, bf16[256,256]{1,0:T(8,128)(2,1)S(1)}, u32[]{:S(2)}, u32[]{:S(2)}) collective-permute-start(bf16[256,256]{1,0:T(8,128)(2,1)S(1)} %get-tuple-element.84.refs_0_), channel_id=1, source_target_pairs={{0,16},{16,0},{1,17},{17,1},{2,18},{18,2},{3,19},{19,3},{4,20},{20... | collective-permute-start | bytes 393224 | tf_op jit(solution)/shard_map/ppermute | solution.py:319
  77.6 6.5 %collective-permute-start.35 = (bf16[256,256]{1,0:T(8,128)(2,1)S(1)}, bf16[256,256]{1,0:T(8,128)(2,1)S(1)}, u32[]{:S(2)}, u32[]{:S(2)}) collective-permute-start(bf16[256,256]{1,0:T(8,128)(2,1)S(1)} %get-tuple-element.85), channel_id=1, source_target_pairs={{0,17},{1,16},{2,19},{3,18},{4,21},{5,20},{6,23},{7,22},{8,25},{9,... | collective-permute-start | bytes 393224 | tf_op jit(solution)/shard_map/ppermute | solution.py:404
  (12 other events, 41.8 us)

commit v5 on v4

--- a/solution.py
+++ b/solution.py
@@ -37,15 +37,13 @@
             yield block * BLOCK_ROWS + odd * half, pl.ds(block * BLOCK_ROWS + odd, half, stride=2), half
 
 
-def prepare_kernel(pixel_ref, pixel_now_ref, pixel_bf_ref, slab):
+def prepare_kernel(pixel_ref, pixel_bf_ref, slab):
     rows, rank = pixel_ref.shape
     for lane in range(0, rank, LANES):
         slab[lane // LANES] = pixel_ref[:, lane : lane + LANES]
     for to, source, half in row_pieces(rows):
         for lane in range(0, rank, LANES):
-            piece = slab[lane // LANES, source, :]
-            pixel_now_ref[to : to + half, lane : lane + LANES] = piece
-            pixel_bf_ref[to : to + half, lane : lane + LANES] = piece.astype(BF16)
+            pixel_bf_ref[to : to + half, lane : lane + LANES] = slab[lane // LANES, source, :].astype(BF16)
 
 
 def place_kernel(copies, chip_blocks, place_ref, ids_ref, values_ref, weights_ref, panel_ref, flat, *scratch):
@@ -245,34 +243,38 @@
     )(*[x for x, _ in parts])
 
 
-def pixel_kernel(scale, last, now_ref, *refs):
-    parts, out_ref, other_ref = refs[:2], refs[2], refs[3]
+def pixel_kernel(scale, first, last, now_ref, *refs):
+    parts, out_ref, other_ref, slabs = refs[:2], refs[2], refs[3], refs[4:]
     rows, rank = now_ref.shape
+    if first:
+        for lane in range(0, rank, LANES):
+            slabs[0][lane // LANES] = now_ref[:, lane : lane + LANES]
     for start, target, half in row_pieces(rows):
         for lane in range(0, rank, LANES):
             at = (slice(start, start + half), slice(lane, lane + LANES))
-            new = (1.0 - DECAY) * now_ref[at] - scale * (parts[0][at].astype(F32) + parts[1][at].astype(F32))
+            now = slabs[0][lane // LANES, target, :] if first else now_ref[at]
+            new = (1.0 - DECAY) * now - scale * (parts[0][at].astype(F32) + parts[1][at].astype(F32))
             if last:
-                refs[4][lane // LANES, target, :] = new
+                slabs[-1][lane // LANES, target, :] = new
             else:
                 out_ref[at] = new
                 other_ref[at] = new.astype(BF16)
     if last:
         for lane in range(0, rank, LANES):
-            out_ref[:, lane : lane + LANES] = refs[4][lane // LANES]
+            out_ref[:, lane : lane + LANES] = slabs[-1][lane // LANES]
         other_ref[...] = jnp.zeros_like(other_ref)
 
 
-def pixel_update(scale, last, now, parts):
+def pixel_update(scale, first, last, now, parts):
     full = jax.ShapeDtypeStruct(now.shape, F32)
     early = add([(part, 0) for part in parts[:-1]], F32)
     other = jax.ShapeDtypeStruct((8, LANES), F32) if last else jax.ShapeDtypeStruct(now.shape, BF16)
     return pl.pallas_call(
-        functools.partial(pixel_kernel, scale, last),
+        functools.partial(pixel_kernel, scale, first, last),
         out_shape=(full, other),
         in_specs=[VMEM] * 3,
         out_specs=(VMEM, VMEM),
-        scratch_shapes=[pltpu.VMEM((now.shape[1] // LANES, now.shape[0], LANES), F32)] if last else [],
+        scratch_shapes=[pltpu.VMEM((now.shape[1] // LANES, now.shape[0], LANES), F32)] * (first + last),
         compiler_params=params(16),
         cost_estimate=cost(10 * now.size, 8 * now.size),
     )(now, early, parts[-1])
@@ -319,11 +321,12 @@
         return lax.ppermute(x, axis, [(i, i ^ mask) for i in range(lax.axis_size(axis))])
 
     shape = jax.ShapeDtypeStruct
-    pixel_now, pixel_bf = pl.pallas_call(
+    pixel_now = pixel_factors
+    pixel_bf = pl.pallas_call(
         prepare_kernel,
-        out_shape=(shape((own_rows, rank), F32), shape((own_rows, rank), BF16)),
+        out_shape=shape((own_rows, rank), BF16),
         in_specs=[VMEM],
-        out_specs=(VMEM, VMEM),
+        out_specs=VMEM,
         scratch_shapes=[pltpu.VMEM((rank // LANES, own_rows, LANES), F32)],
         compiler_params=params(16),
         cost_estimate=cost(own_rows * rank, own_rows * rank * 16),
@@ -346,7 +349,7 @@
     rows, width = chips * core_blocks * tiles, local // BLOCK_DATES * LANES
     values, weights = block_values.reshape(slots, flat), block_weights.reshape(slots, flat)
     place = jnp.stack([me // 2, me % 2]).astype(jnp.int32)
-    mine = place_blocks(True, core_blocks, place, lists(dates_bf), values, weights, rows, width, 36)
+    mine = place_blocks(False, core_blocks, place, lists(dates_bf), values, weights, rows, width, 36)
     other = place_blocks(
         False, core_blocks, place, lists(dates_other), swap(values, 1), swap(weights, 1), rows, width, 30
     )
@@ -396,7 +399,7 @@
         part2 = swap(add([(near2, 0)] + recv2, BF16), along[2])
         parts = [near0, pair] + part0 + [part3, part2]
         own, partner, dates_rest = date_gradient(dates_now, errors, ordered, tuple(starts))
-        pixel_now, pixel_bf = pixel_update(STEP_SCALE / all_dates, last, pixel_now, parts)
+        pixel_now, pixel_bf = pixel_update(STEP_SCALE / all_dates, step == 0, last, pixel_now, parts)
         sums = [own, swap(partner, 1)]
         if groups > 1:
             count = groups * loop_size

time: 85.8 us -> 85.4 us (level)
  waiting for transfers between devices: 22.9 us -> 25.5 us
  starting transfers between devices: 37.2 us -> 34.8 us
    ppermute x34, waiting for transfers between devices: 22.9 us -> 25.5 us  [swap(): lax.ppermute(x, axis, [(i, i ^ mask) for i in range(lax.axis_size(axis))])]
    ppermute x34, starting transfers between devices: 37.1 us -> 34.8 us  [swap(): lax.ppermute(x, axis, [(i, i ^ mask) for i in range(lax.axis_size(axis))])]
    unnamed x16 -> x14, local copies, waits for them, and re-layouts: 5.91 us -> 5.22 us
  transfers between devices with their start and end apart: 36 -> 36, of which waited for: 14 -> 13; matrix products, arithmetic and copies ran while one was open for 0% -> 0% of each run, Pallas kernels for 19% -> 19%
where the time goes in v5:
time: 85.4 us; the launch traced here: 84.5 us
  starting transfers between devices  34.8 us (41%)
  waiting for transfers between devices  25.5 us (30%)
  Pallas kernels  17.2 us (20%)
  local copies, waits for them, and re-layouts  5.22 us (6%)
  between operations  1.63 us (2%)
    ppermute x34, starting transfers between devices, swap(): lax.ppermute(x, axis, [(i, i ^ mask) for i in range(lax.axis_size(axis))])  34.8 us
    ppermute x34, waiting for transfers between devices, swap(): lax.ppermute(x, axis, [(i, i ^ mask) for i in range(lax.axis_size(axis))])  25.5 us
    pallas_call x14, Pallas kernels, chunk(): pl.pallas_call(functools.partial(chunk_kernel, n), grid=(1,), out_shape=(...  9.87 us
    unnamed x14, local copies, waits for them, and re-layouts  5.22 us
    pallas_call x2, Pallas kernels, place_blocks(): pl.pallas_call(functools.partial(place_kernel, copies, 2 * core_blocks),...  3.73 us
  transfers between devices with their start and end apart: 36, of which 13 were waited for; matrix products, arithmetic and copies ran while one was open for 0% of the time, Pallas kernels for 19%

profile of v5, /device:TPU:0, one launch (start us, length us, event | category | flops | bytes accessed | tf_op | source)
XLA Modules:
  0.0 84.5 jit_solution(3195134267508493875)
XLA Ops:
  1.2 0.9 %copy-done.2 = f32[256,256]{1,0:T(8,128)S(1)} copy-done((f32[256,256]{1,0:T(8,128)S(1)}, f32[256,256]{1,0:T(8,128)}, u32[]{:S(2)}) %copy-start.2) | copy-done | bytes 262168
  2.2 3.0 %collective-permute-start.3 = (bf16[256,256]{1,0:T(8,128)(2,1)S(1)}, bf16[256,256]{1,0:T(8,128)(2,1)S(1)}, u32[]{:S(2)}, u32[]{:S(2)}) collective-permute-start(bf16[256,256]{1,0:T(8,128)(2,1)S(1)} %shard_map.77.x_ref.refs_0_.refs_5_), channel_id=1, source_target_pairs={{0,2},{1,3},{2,0},{3,1},{4,6},{5,7},{6,4},{7,5},{8,10},{9,11},{10,... | collective-permute-start | bytes 393224 | tf_op jit(solution)/shard_map/ppermute | solution.py:321
  5.2 1.6 %collective-permute-start.7 = (bf16[256,256]{1,0:T(8,128)(2,1)S(1)}, bf16[256,256]{1,0:T(8,128)(2,1)S(1)}, u32[]{:S(2)}, u32[]{:S(2)}) collective-permute-start(bf16[256,256]{1,0:T(8,128)(2,1)S(1)} %shard_map.77.x_ref.refs_0_.refs_5_), channel_id=1, source_target_pairs={{0,4},{1,5},{2,6},{3,7},{4,0},{5,1},{6,2},{7,3},{8,12},{9,13},{10,... | collective-permute-start | bytes 393224 | tf_op jit(solution)/shard_map/ppermute | solution.py:321
  6.8 2.5 %collective-permute-start.5 = (bf16[256,256]{1,0:T(8,128)(2,1)S(1)}, bf16[256,256]{1,0:T(8,128)(2,1)S(1)}, u32[]{:S(2)}, u32[]{:S(2)}) collective-permute-start(bf16[256,256]{1,0:T(8,128)(2,1)S(1)} %shard_map.77.x_ref.refs_0_.refs_5_), channel_id=1, source_target_pairs={{0,12},{1,13},{2,14},{3,15},{4,8},{5,9},{6,10},{7,11},{8,4},{9,5},... | collective-permute-start | bytes 393224 | tf_op jit(solution)/shard_map/ppermute | solution.py:321
  11.8 1.3 %copy-done = bf16[1,1,80,8192]{3,2,1,0:T(8,128)(2,1)S(1)} copy-done((bf16[1,1,80,8192]{3,2,1,0:T(8,128)(2,1)S(1)}, bf16[1,1,80,8192]{3,2,1,0:T(8,128)(2,1)}, u32[]{:S(2)}) %copy-start) | copy-done | bytes 1310744
  13.1 1.3 %copy-done.1 = bf16[1,1,80,8192]{3,2,1,0:T(8,128)(2,1)S(1)} copy-done((bf16[1,1,80,8192]{3,2,1,0:T(8,128)(2,1)S(1)}, bf16[1,1,80,8192]{3,2,1,0:T(8,128)(2,1)}, u32[]{:S(2)}) %copy-start.1) | copy-done | bytes 1310744
  14.4 1.6 %shard_map.79.refs_1_.refs_4_.refs_3_ = bf16[2,1088,512]{2,1,0:T(8,128)(2,1)S(1)} custom-call(s32[2]{0:T(128)S(1)} %pad_add_fusion.place_ref, s32[3,80]{1,0:T(4,128)S(1)} %slice_convert_fusion.1.ids_ref, bf16[80,8192]{1,0:T(8,128)(2,1)S(1)} %bitcast.6, bf16[80,8192]{1,0:T(8,128)(2,1)S(1)} %bitcast.8), custom_call_target="tpu_custom_call" | custom-call | flops 5242880 | bytes 5242880 | tf_op jit(solution)/shard_map/pallas_call | solution.py:103
  16.1 1.5 %collective-permute-start.4 = (bf16[256,256]{1,0:T(8,128)(2,1)S(1)}, bf16[256,256]{1,0:T(8,128)(2,1)S(1)}, u32[]{:S(2)}, u32[]{:S(2)}) collective-permute-start(bf16[256,256]{1,0:T(8,128)(2,1)S(1)} %shard_map.81), channel_id=1, source_target_pairs={{0,8},{1,9},{2,10},{3,11},{4,12},{5,13},{6,14},{7,15},{8,0},{9,1},... | collective-permute-start | bytes 393224 | tf_op jit(solution)/shard_map/ppermute | solution.py:321
  18.2 1.4 %collective-permute-start.6 = (bf16[256,256]{1,0:T(8,128)(2,1)S(1)}, bf16[256,256]{1,0:T(8,128)(2,1)S(1)}, u32[]{:S(2)}, u32[]{:S(2)}) collective-permute-start(bf16[256,256]{1,0:T(8,128)(2,1)S(1)} %collective-permute-done.5.refs_0_.refs_3_), channel_id=1, source_target_pairs={{0,2},{1,3},{2,0},{3,1},{4,6},{5,7},{6,4},{7,5},{8,10},{9,11},{10,... | collective-permute-start | bytes 393224 | tf_op jit(solution)/shard_map/ppermute | solution.py:321
  19.6 2.1 %shard_map.80.refs_5_.refs_4_ = bf16[2,1088,512]{2,1,0:T(8,128)(2,1)S(1)} custom-call(s32[2]{0:T(128)S(1)} %pad_add_fusion.place_ref, s32[3,80]{1,0:T(4,128)S(1)} %slice_convert_fusion.ids_ref, bf16[80,8192]{1,0:T(8,128)(2,1)S(1)} %collective-permute-done.1.values_ref, bf16[80,8192]{1,0:T(8,128)(2,1)S(1)} %collective-permute-done.2.weights_ref), custom_call_target="tpu_custom_call" | custom-call | flops 5242880 | bytes 5242880 | tf_op jit(solution)/shard_map/pallas_call | solution.py:103
  21.7 2.2 %collective-permute-done.8.refs_1_ = bf16[256,256]{1,0:T(8,128)(2,1)S(1)} collective-permute-done((bf16[256,256]{1,0:T(8,128)(2,1)S(1)}, bf16[256,256]{1,0:T(8,128)(2,1)S(1)}, u32[]{:S(2)}, u32[]{:S(2)}) %collective-permute-start.8) | collective-permute-done | bytes 131104 | tf_op jit(solution)/shard_map/ppermute | solution.py:321
  23.9 1.1 %shard_map.82 = (bf16[512,256]{1,0:T(8,128)(2,1)S(1)}, bf16[512,512]{1,0:T(8,128)(2,1)S(1)}) custom-call(bf16[256,256]{1,0:T(8,128)(2,1)S(1)} %collective-permute-done.7.refs_0_, bf16[256,256]{1,0:T(8,128)(2,1)S(1)} %collective-permute-done.8.refs_1_, bf16[272,256]{1,0:T(8,128)(2,1)S(1)} %shard_map.78.refs_2_.refs_1_, ...), custom_call_target="tpu_custom_call" | custom-call | flops 268435456 | bytes 2400000 | tf_op jit(solution)/shard_map/pallas_call | solution.py:166
  25.1 1.1 %collective-permute-done.4.refs_0_.x_ref.refs_4_ = bf16[256,256]{1,0:T(8,128)(2,1)S(1)} collective-permute-done((bf16[256,256]{1,0:T(8,128)(2,1)S(1)}, bf16[256,256]{1,0:T(8,128)(2,1)S(1)}, u32[]{:S(2)}, u32[]{:S(2)}) %collective-permute-start.4) | collective-permute-done | bytes 131104 | tf_op jit(solution)/shard_map/ppermute | solution.py:321
  26.5 1.4 %collective-permute-start.9 = (bf16[512,256]{1,0:T(8,128)(2,1)S(1)}, bf16[512,256]{1,0:T(8,128)(2,1)S(1)}, u32[]{:S(2)}, u32[]{:S(2)}) collective-permute-start(bf16[512,256]{1,0:T(8,128)(2,1)S(1)} %get-tuple-element.43.refs_5_.refs_0_), channel_id=1, source_target_pairs={{0,4},{1,5},{2,6},{3,7},{4,0},{5,1},{6,2},{7,3},{8,12},{9,13},{10,... | collective-permute-start | bytes 786440 | tf_op jit(solution)/shard_map/ppermute | solution.py:321
  31.6 1.0 %collective-permute-done.13.refs_0_.refs_7_ = bf16[256,256]{1,0:T(8,128)(2,1)S(1)} collective-permute-done((bf16[256,256]{1,0:T(8,128)(2,1)S(1)}, bf16[256,256]{1,0:T(8,128)(2,1)S(1)}, u32[]{:S(2)}, u32[]{:S(2)}) %collective-permute-start.13) | collective-permute-done | bytes 131104 | tf_op jit(solution)/shard_map/ppermute | solution.py:321
  34.6 1.4 %collective-permute-start.12 = (bf16[256,256]{1,0:T(8,128)(2,1)S(1)}, bf16[256,256]{1,0:T(8,128)(2,1)S(1)}, u32[]{:S(2)}, u32[]{:S(2)}) collective-permute-start(bf16[256,256]{1,0:T(8,128)(2,1)S(1)} %shard_map.89), channel_id=1, source_target_pairs={{0,12},{1,13},{2,14},{3,15},{4,8},{5,9},{6,10},{7,11},{8,4},{9,5},... | collective-permute-start | bytes 393224 | tf_op jit(solution)/shard_map/ppermute | solution.py:321
  36.0 1.3 %collective-permute-start.10 = (bf16[256,256]{1,0:T(8,128)(2,1)S(1)}, bf16[256,256]{1,0:T(8,128)(2,1)S(1)}, u32[]{:S(2)}, u32[]{:S(2)}) collective-permute-start(bf16[256,256]{1,0:T(8,128)(2,1)S(1)} %shard_map.88), channel_id=1, source_target_pairs={{0,2},{1,3},{2,0},{3,1},{4,6},{5,7},{6,4},{7,5},{8,10},{9,11},{10,... | collective-permute-start | bytes 393224 | tf_op jit(solution)/shard_map/ppermute | solution.py:321
  37.3 1.9 %collective-permute-done.14.refs_1_ = bf16[256,256]{1,0:T(8,128)(2,1)S(1)} collective-permute-done((bf16[256,256]{1,0:T(8,128)(2,1)S(1)}, bf16[256,256]{1,0:T(8,128)(2,1)S(1)}, u32[]{:S(2)}, u32[]{:S(2)}) %collective-permute-start.14) | collective-permute-done | bytes 131104 | tf_op jit(solution)/shard_map/ppermute | solution.py:321
  39.3 1.4 %collective-permute-start.15 = (bf16[256,256]{1,0:T(8,128)(2,1)S(1)}, bf16[256,256]{1,0:T(8,128)(2,1)S(1)}, u32[]{:S(2)}, u32[]{:S(2)}) collective-permute-start(bf16[256,256]{1,0:T(8,128)(2,1)S(1)} %shard_map.93), channel_id=1, source_target_pairs={{0,8},{1,9},{2,10},{3,11},{4,12},{5,13},{6,14},{7,15},{8,0},{9,1},... | collective-permute-start | bytes 393224 | tf_op jit(solution)/shard_map/ppermute | solution.py:321
  41.4 1.4 %collective-permute-start.17 = (bf16[256,256]{1,0:T(8,128)(2,1)S(1)}, bf16[256,256]{1,0:T(8,128)(2,1)S(1)}, u32[]{:S(2)}, u32[]{:S(2)}) collective-permute-start(bf16[256,256]{1,0:T(8,128)(2,1)S(1)} %get-tuple-element.60.refs_0_), channel_id=1, source_target_pairs={{0,16},{16,0},{1,17},{17,1},{2,18},{18,2},{3,19},{19,3},{4,20},{20... | collective-permute-start | bytes 393224 | tf_op jit(solution)/shard_map/ppermute | solution.py:321
  43.7 3.8 %collective-permute-done.15.refs_1_ = bf16[256,256]{1,0:T(8,128)(2,1)S(1)} collective-permute-done((bf16[256,256]{1,0:T(8,128)(2,1)S(1)}, bf16[256,256]{1,0:T(8,128)(2,1)S(1)}, u32[]{:S(2)}, u32[]{:S(2)}) %collective-permute-start.15) | collective-permute-done | bytes 131104 | tf_op jit(solution)/shard_map/ppermute | solution.py:321
  47.6 1.9 %collective-permute-start.22 = (bf16[256,256]{1,0:T(8,128)(2,1)S(1)}, bf16[256,256]{1,0:T(8,128)(2,1)S(1)}, u32[]{:S(2)}, u32[]{:S(2)}) collective-permute-start(bf16[256,256]{1,0:T(8,128)(2,1)S(1)} %get-tuple-element.51.refs_4_.x_ref.refs_0_.refs_5_), channel_id=1, source_target_pairs={{0,12},{1,13},{2,14},{3,15},{4,8},{5,9},{6,10},{7,11},{8,4},{9,5},... | collective-permute-start | bytes 393224 | tf_op jit(solution)/shard_map/ppermute | solution.py:321
  49.7 5.8 %collective-permute-done.20.refs_0_ = bf16[256,256]{1,0:T(8,128)(2,1)S(1)} collective-permute-done((bf16[256,256]{1,0:T(8,128)(2,1)S(1)}, bf16[256,256]{1,0:T(8,128)(2,1)S(1)}, u32[]{:S(2)}, u32[]{:S(2)}) %collective-permute-start.20) | collective-permute-done | bytes 131104 | tf_op jit(solution)/shard_map/ppermute | solution.py:321
  55.7 2.0 %collective-permute-start.23 = (bf16[256,256]{1,0:T(8,128)(2,1)S(1)}, bf16[256,256]{1,0:T(8,128)(2,1)S(1)}, u32[]{:S(2)}, u32[]{:S(2)}) collective-permute-start(bf16[256,256]{1,0:T(8,128)(2,1)S(1)} %collective-permute-done.22.refs_0_.refs_3_), channel_id=1, source_target_pairs={{0,2},{1,3},{2,0},{3,1},{4,6},{5,7},{6,4},{7,5},{8,10},{9,11},{10,... | collective-permute-start | bytes 393224 | tf_op jit(solution)/shard_map/ppermute | solution.py:321
  57.8 3.4 %collective-permute-done.24.refs_1_ = bf16[256,256]{1,0:T(8,128)(2,1)S(1)} collective-permute-done((bf16[256,256]{1,0:T(8,128)(2,1)S(1)}, bf16[256,256]{1,0:T(8,128)(2,1)S(1)}, u32[]{:S(2)}, u32[]{:S(2)}) %collective-permute-start.24) | collective-permute-done | bytes 131104 | tf_op jit(solution)/shard_map/ppermute | solution.py:321
  61.2 1.1 %shard_map.98 = (bf16[512,256]{1,0:T(8,128)(2,1)S(1)}, bf16[512,512]{1,0:T(8,128)(2,1)S(1)}) custom-call(bf16[256,256]{1,0:T(8,128)(2,1)S(1)} %collective-permute-done.20.refs_0_, bf16[256,256]{1,0:T(8,128)(2,1)S(1)} %collective-permute-done.24.refs_1_, bf16[256,256]{1,0:T(8,128)(2,1)S(1)} %get-tuple-element.62.refs_2_.refs_1_, ...), custom_call_target="tpu_custom_call" | custom-call | flops 268435456 | bytes 2400000 | tf_op jit(solution)/shard_map/pallas_call | solution.py:166
  64.2 1.4 %collective-permute-start.28 = (bf16[256,256]{1,0:T(8,128)(2,1)S(1)}, bf16[256,256]{1,0:T(8,128)(2,1)S(1)}, u32[]{:S(2)}, u32[]{:S(2)}) collective-permute-start(bf16[256,256]{1,0:T(8,128)(2,1)S(1)} %get-tuple-element.64.refs_5_), channel_id=1, source_target_pairs={{0,2},{1,3},{2,0},{3,1},{4,6},{5,7},{6,4},{7,5},{8,10},{9,11},{10,... | collective-permute-start | bytes 393224 | tf_op jit(solution)/shard_map/ppermute | solution.py:321
  68.9 1.2 %collective-permute-start.31 = (bf16[256,256]{1,0:T(8,128)(2,1)S(1)}, bf16[256,256]{1,0:T(8,128)(2,1)S(1)}, u32[]{:S(2)}, u32[]{:S(2)}) collective-permute-start(bf16[256,256]{1,0:T(8,128)(2,1)S(1)} %get-tuple-element.69), channel_id=1, source_target_pairs={{0,2},{1,3},{2,0},{3,1},{4,6},{5,7},{6,4},{7,5},{8,10},{9,11},{10,... | collective-permute-start | bytes 393224 | tf_op jit(solution)/shard_map/ppermute | solution.py:321
  70.5 2.4 %collective-permute-start.29 = (bf16[256,256]{1,0:T(8,128)(2,1)S(1)}, bf16[256,256]{1,0:T(8,128)(2,1)S(1)}, u32[]{:S(2)}, u32[]{:S(2)}) collective-permute-start(bf16[256,256]{1,0:T(8,128)(2,1)S(1)} %shard_map.105), channel_id=1, source_target_pairs={{0,12},{1,13},{2,14},{3,15},{4,8},{5,9},{6,10},{7,11},{8,4},{9,5},... | collective-permute-start | bytes 393224 | tf_op jit(solution)/shard_map/ppermute | solution.py:321
  73.7 1.3 %collective-permute-start.27 = (bf16[256,256]{1,0:T(8,128)(2,1)S(1)}, bf16[256,256]{1,0:T(8,128)(2,1)S(1)}, u32[]{:S(2)}, u32[]{:S(2)}) collective-permute-start(bf16[256,256]{1,0:T(8,128)(2,1)S(1)} %shard_map.104), channel_id=1, source_target_pairs={{0,2},{1,3},{2,0},{3,1},{4,6},{5,7},{6,4},{7,5},{8,10},{9,11},{10,... | collective-permute-start | bytes 393224 | tf_op jit(solution)/shard_map/ppermute | solution.py:321
  75.3 1.4 %collective-permute-start.32 = (bf16[256,256]{1,0:T(8,128)(2,1)S(1)}, bf16[256,256]{1,0:T(8,128)(2,1)S(1)}, u32[]{:S(2)}, u32[]{:S(2)}) collective-permute-start(bf16[256,256]{1,0:T(8,128)(2,1)S(1)} %shard_map.109), channel_id=1, source_target_pairs={{0,8},{1,9},{2,10},{3,11},{4,12},{5,13},{6,14},{7,15},{8,0},{9,1},... | collective-permute-start | bytes 393224 | tf_op jit(solution)/shard_map/ppermute | solution.py:321
  78.9 3.9 %collective-permute-done.32.refs_1_ = bf16[256,256]{1,0:T(8,128)(2,1)S(1)} collective-permute-done((bf16[256,256]{1,0:T(8,128)(2,1)S(1)}, bf16[256,256]{1,0:T(8,128)(2,1)S(1)}, u32[]{:S(2)}, u32[]{:S(2)}) %collective-permute-start.32) | collective-permute-done | bytes 131104 | tf_op jit(solution)/shard_map/ppermute | solution.py:321
  (93 shorter events, 21.6 us)
Async XLA Ops:
  0.6 19.0 %collective-permute-start.1 = (bf16[80,8192]{1,0:T(8,128)(2,1)}, bf16[80,8192]{1,0:T(8,128)(2,1)S(1)}, u32[]{:S(2)}, u32[]{:S(2)}) collective-permute-start(bf16[80,8192]{1,0:T(8,128)(2,1)} %bitcast.5), channel_id=1, source_target_pairs={{0,1},{1,0},{2,3},{3,2},{4,5},{5,4},{6,7},{7,6},{8,9},{9,8},{10,11... | collective-permute-start | bytes 3932168 | tf_op jit(solution)/shard_map/ppermute | solution.py:321
  1.1 18.5 %collective-permute-start.2 = (bf16[80,8192]{1,0:T(8,128)(2,1)}, bf16[80,8192]{1,0:T(8,128)(2,1)S(1)}, u32[]{:S(2)}, u32[]{:S(2)}) collective-permute-start(bf16[80,8192]{1,0:T(8,128)(2,1)} %bitcast.7), channel_id=1, source_target_pairs={{0,1},{1,0},{2,3},{3,2},{4,5},{5,4},{6,7},{7,6},{8,9},{9,8},{10,11... | collective-permute-start | bytes 3932168 | tf_op jit(solution)/shard_map/ppermute | solution.py:321
  2.2 9.3 %collective-permute-start.3 = (bf16[256,256]{1,0:T(8,128)(2,1)S(1)}, bf16[256,256]{1,0:T(8,128)(2,1)S(1)}, u32[]{:S(2)}, u32[]{:S(2)}) collective-permute-start(bf16[256,256]{1,0:T(8,128)(2,1)S(1)} %shard_map.77.x_ref.refs_0_.refs_5_), channel_id=1, source_target_pairs={{0,2},{1,3},{2,0},{3,1},{4,6},{5,7},{6,4},{7,5},{8,10},{9,11},{10,... | collective-permute-start | bytes 393224 | tf_op jit(solution)/shard_map/ppermute | solution.py:321
  5.2 10.9 %collective-permute-start.7 = (bf16[256,256]{1,0:T(8,128)(2,1)S(1)}, bf16[256,256]{1,0:T(8,128)(2,1)S(1)}, u32[]{:S(2)}, u32[]{:S(2)}) collective-permute-start(bf16[256,256]{1,0:T(8,128)(2,1)S(1)} %shard_map.77.x_ref.refs_0_.refs_5_), channel_id=1, source_target_pairs={{0,4},{1,5},{2,6},{3,7},{4,0},{5,1},{6,2},{7,3},{8,12},{9,13},{10,... | collective-permute-start | bytes 393224 | tf_op jit(solution)/shard_map/ppermute | solution.py:321
  6.8 10.8 %collective-permute-start.5 = (bf16[256,256]{1,0:T(8,128)(2,1)S(1)}, bf16[256,256]{1,0:T(8,128)(2,1)S(1)}, u32[]{:S(2)}, u32[]{:S(2)}) collective-permute-start(bf16[256,256]{1,0:T(8,128)(2,1)S(1)} %shard_map.77.x_ref.refs_0_.refs_5_), channel_id=1, source_target_pairs={{0,12},{1,13},{2,14},{3,15},{4,8},{5,9},{6,10},{7,11},{8,4},{9,5},... | collective-permute-start | bytes 393224 | tf_op jit(solution)/shard_map/ppermute | solution.py:321
  11.6 6.6 %collective-permute-start = (bf16[272,256]{1,0:T(8,128)(2,1)S(1)}, bf16[272,256]{1,0:T(8,128)(2,1)S(1)}, u32[]{:S(2)}, u32[]{:S(2)}) collective-permute-start(bf16[272,256]{1,0:T(8,128)(2,1)S(1)} %shard_map.78.refs_2_.refs_1_), channel_id=1, source_target_pairs={{0,1},{1,0},{2,3},{3,2},{4,5},{5,4},{6,7},{7,6},{8,9},{9,8},{10,11... | collective-permute-start | bytes 417800 | tf_op jit(solution)/shard_map/ppermute | solution.py:321
  16.1 10.1 %collective-permute-start.4 = (bf16[256,256]{1,0:T(8,128)(2,1)S(1)}, bf16[256,256]{1,0:T(8,128)(2,1)S(1)}, u32[]{:S(2)}, u32[]{:S(2)}) collective-permute-start(bf16[256,256]{1,0:T(8,128)(2,1)S(1)} %shard_map.81), channel_id=1, source_target_pairs={{0,8},{1,9},{2,10},{3,11},{4,12},{5,13},{6,14},{7,15},{8,0},{9,1},... | collective-permute-start | bytes 393224 | tf_op jit(solution)/shard_map/ppermute | solution.py:321
  17.6 6.4 %collective-permute-start.8 = (bf16[256,256]{1,0:T(8,128)(2,1)S(1)}, bf16[256,256]{1,0:T(8,128)(2,1)S(1)}, u32[]{:S(2)}, u32[]{:S(2)}) collective-permute-start(bf16[256,256]{1,0:T(8,128)(2,1)S(1)} %collective-permute-done.7.refs_0_), channel_id=1, source_target_pairs={{0,2},{1,3},{2,0},{3,1},{4,6},{5,7},{6,4},{7,5},{8,10},{9,11},{10,... | collective-permute-start | bytes 393224 | tf_op jit(solution)/shard_map/ppermute | solution.py:321
  18.2 9.6 %collective-permute-start.6 = (bf16[256,256]{1,0:T(8,128)(2,1)S(1)}, bf16[256,256]{1,0:T(8,128)(2,1)S(1)}, u32[]{:S(2)}, u32[]{:S(2)}) collective-permute-start(bf16[256,256]{1,0:T(8,128)(2,1)S(1)} %collective-permute-done.5.refs_0_.refs_3_), channel_id=1, source_target_pairs={{0,2},{1,3},{2,0},{3,1},{4,6},{5,7},{6,4},{7,5},{8,10},{9,11},{10,... | collective-permute-start | bytes 393224 | tf_op jit(solution)/shard_map/ppermute | solution.py:321
  26.2 6.4 %collective-permute-start.13 = (bf16[256,256]{1,0:T(8,128)(2,1)S(1)}, bf16[256,256]{1,0:T(8,128)(2,1)S(1)}, u32[]{:S(2)}, u32[]{:S(2)}) collective-permute-start(bf16[256,256]{1,0:T(8,128)(2,1)S(1)} %shard_map.91), channel_id=1, source_target_pairs={{0,2},{1,3},{2,0},{3,1},{4,6},{5,7},{6,4},{7,5},{8,10},{9,11},{10,... | collective-permute-start | bytes 393224 | tf_op jit(solution)/shard_map/ppermute | solution.py:321
  26.5 9.5 %collective-permute-start.9 = (bf16[512,256]{1,0:T(8,128)(2,1)S(1)}, bf16[512,256]{1,0:T(8,128)(2,1)S(1)}, u32[]{:S(2)}, u32[]{:S(2)}) collective-permute-start(bf16[512,256]{1,0:T(8,128)(2,1)S(1)} %get-tuple-element.43.refs_5_.refs_0_), channel_id=1, source_target_pairs={{0,4},{1,5},{2,6},{3,7},{4,0},{5,1},{6,2},{7,3},{8,12},{9,13},{10,... | collective-permute-start | bytes 786440 | tf_op jit(solution)/shard_map/ppermute | solution.py:321
  28.5 6.1 %collective-permute-start.11 = (bf16[256,256]{1,0:T(8,128)(2,1)S(1)}, bf16[256,256]{1,0:T(8,128)(2,1)S(1)}, u32[]{:S(2)}, u32[]{:S(2)}) collective-permute-start(bf16[256,256]{1,0:T(8,128)(2,1)S(1)} %get-tuple-element.44.refs_5_), channel_id=1, source_target_pairs={{0,2},{1,3},{2,0},{3,1},{4,6},{5,7},{6,4},{7,5},{8,10},{9,11},{10,... | collective-permute-start | bytes 393224 | tf_op jit(solution)/shard_map/ppermute | solution.py:321
  33.2 6.0 %collective-permute-start.14 = (bf16[256,256]{1,0:T(8,128)(2,1)S(1)}, bf16[256,256]{1,0:T(8,128)(2,1)S(1)}, u32[]{:S(2)}, u32[]{:S(2)}) collective-permute-start(bf16[256,256]{1,0:T(8,128)(2,1)S(1)} %get-tuple-element.49), channel_id=1, source_target_pairs={{0,2},{1,3},{2,0},{3,1},{4,6},{5,7},{6,4},{7,5},{8,10},{9,11},{10,... | collective-permute-start | bytes 393224 | tf_op jit(solution)/shard_map/ppermute | solution.py:321
  34.6 8.3 %collective-permute-start.12 = (bf16[256,256]{1,0:T(8,128)(2,1)S(1)}, bf16[256,256]{1,0:T(8,128)(2,1)S(1)}, u32[]{:S(2)}, u32[]{:S(2)}) collective-permute-start(bf16[256,256]{1,0:T(8,128)(2,1)S(1)} %shard_map.89), channel_id=1, source_target_pairs={{0,12},{1,13},{2,14},{3,15},{4,8},{5,9},{6,10},{7,11},{8,4},{9,5},... | collective-permute-start | bytes 393224 | tf_op jit(solution)/shard_map/ppermute | solution.py:321
  36.0 7.6 %collective-permute-start.10 = (bf16[256,256]{1,0:T(8,128)(2,1)S(1)}, bf16[256,256]{1,0:T(8,128)(2,1)S(1)}, u32[]{:S(2)}, u32[]{:S(2)}) collective-permute-start(bf16[256,256]{1,0:T(8,128)(2,1)S(1)} %shard_map.88), channel_id=1, source_target_pairs={{0,2},{1,3},{2,0},{3,1},{4,6},{5,7},{6,4},{7,5},{8,10},{9,11},{10,... | collective-permute-start | bytes 393224 | tf_op jit(solution)/shard_map/ppermute | solution.py:321
  39.3 8.2 %collective-permute-start.15 = (bf16[256,256]{1,0:T(8,128)(2,1)S(1)}, bf16[256,256]{1,0:T(8,128)(2,1)S(1)}, u32[]{:S(2)}, u32[]{:S(2)}) collective-permute-start(bf16[256,256]{1,0:T(8,128)(2,1)S(1)} %shard_map.93), channel_id=1, source_target_pairs={{0,8},{1,9},{2,10},{3,11},{4,12},{5,13},{6,14},{7,15},{8,0},{9,1},... | collective-permute-start | bytes 393224 | tf_op jit(solution)/shard_map/ppermute | solution.py:321
  41.4 8.1 %collective-permute-start.17 = (bf16[256,256]{1,0:T(8,128)(2,1)S(1)}, bf16[256,256]{1,0:T(8,128)(2,1)S(1)}, u32[]{:S(2)}, u32[]{:S(2)}) collective-permute-start(bf16[256,256]{1,0:T(8,128)(2,1)S(1)} %get-tuple-element.60.refs_0_), channel_id=1, source_target_pairs={{0,16},{16,0},{1,17},{17,1},{2,18},{18,2},{3,19},{19,3},{4,20},{20... | collective-permute-start | bytes 393224 | tf_op jit(solution)/shard_map/ppermute | solution.py:321
  42.9 6.6 %collective-permute-start.18 = (bf16[256,256]{1,0:T(8,128)(2,1)S(1)}, bf16[256,256]{1,0:T(8,128)(2,1)S(1)}, u32[]{:S(2)}, u32[]{:S(2)}) collective-permute-start(bf16[256,256]{1,0:T(8,128)(2,1)S(1)} %get-tuple-element.61), channel_id=1, source_target_pairs={{0,17},{1,16},{2,19},{3,18},{4,21},{5,20},{6,23},{7,22},{8,25},{9,... | collective-permute-start | bytes 393224 | tf_op jit(solution)/shard_map/ppermute | solution.py:407
  42.9 6.6 %collective-permute-start.16 = (bf16[256,256]{1,0:T(8,128)(2,1)S(1)}, bf16[256,256]{1,0:T(8,128)(2,1)S(1)}, u32[]{:S(2)}, u32[]{:S(2)}) collective-permute-start(bf16[256,256]{1,0:T(8,128)(2,1)S(1)} %get-tuple-element.61), channel_id=1, source_target_pairs={{0,1},{1,0},{2,3},{3,2},{4,5},{5,4},{6,7},{7,6},{8,9},{9,8},{10,11... | collective-permute-start | bytes 393224 | tf_op jit(solution)/shard_map/ppermute | solution.py:321
  47.6 8.0 %collective-permute-start.20 = (bf16[256,256]{1,0:T(8,128)(2,1)S(1)}, bf16[256,256]{1,0:T(8,128)(2,1)S(1)}, u32[]{:S(2)}, u32[]{:S(2)}) collective-permute-start(bf16[256,256]{1,0:T(8,128)(2,1)S(1)} %get-tuple-element.51.refs_4_.x_ref.refs_0_.refs_5_), channel_id=1, source_target_pairs={{0,4},{1,5},{2,6},{3,7},{4,0},{5,1},{6,2},{7,3},{8,12},{9,13},{10,... | collective-permute-start | bytes 393224 | tf_op jit(solution)/shard_map/ppermute | solution.py:321
  47.6 8.1 %collective-permute-start.22 = (bf16[256,256]{1,0:T(8,128)(2,1)S(1)}, bf16[256,256]{1,0:T(8,128)(2,1)S(1)}, u32[]{:S(2)}, u32[]{:S(2)}) collective-permute-start(bf16[256,256]{1,0:T(8,128)(2,1)S(1)} %get-tuple-element.51.refs_4_.x_ref.refs_0_.refs_5_), channel_id=1, source_target_pairs={{0,12},{1,13},{2,14},{3,15},{4,8},{5,9},{6,10},{7,11},{8,4},{9,5},... | collective-permute-start | bytes 393224 | tf_op jit(solution)/shard_map/ppermute | solution.py:321
  49.6 8.2 %collective-permute-start.19 = (bf16[256,256]{1,0:T(8,128)(2,1)S(1)}, bf16[256,256]{1,0:T(8,128)(2,1)S(1)}, u32[]{:S(2)}, u32[]{:S(2)}) collective-permute-start(bf16[256,256]{1,0:T(8,128)(2,1)S(1)} %get-tuple-element.62.refs_2_.refs_1_), channel_id=1, source_target_pairs={{0,1},{1,0},{2,3},{3,2},{4,5},{5,4},{6,7},{7,6},{8,9},{9,8},{10,11... | collective-permute-start | bytes 393224 | tf_op jit(solution)/shard_map/ppermute | solution.py:321
  55.5 7.1 %collective-permute-start.21 = (bf16[256,256]{1,0:T(8,128)(2,1)S(1)}, bf16[256,256]{1,0:T(8,128)(2,1)S(1)}, u32[]{:S(2)}, u32[]{:S(2)}) collective-permute-start(bf16[256,256]{1,0:T(8,128)(2,1)S(1)} %shard_map.97), channel_id=1, source_target_pairs={{0,8},{1,9},{2,10},{3,11},{4,12},{5,13},{6,14},{7,15},{8,0},{9,1},... | collective-permute-start | bytes 393224 | tf_op jit(solution)/shard_map/ppermute | solution.py:321
  55.7 7.9 %collective-permute-start.23 = (bf16[256,256]{1,0:T(8,128)(2,1)S(1)}, bf16[256,256]{1,0:T(8,128)(2,1)S(1)}, u32[]{:S(2)}, u32[]{:S(2)}) collective-permute-start(bf16[256,256]{1,0:T(8,128)(2,1)S(1)} %collective-permute-done.22.refs_0_.refs_3_), channel_id=1, source_target_pairs={{0,2},{1,3},{2,0},{3,1},{4,6},{5,7},{6,4},{7,5},{8,10},{9,11},{10,... | collective-permute-start | bytes 393224 | tf_op jit(solution)/shard_map/ppermute | solution.py:321
  57.7 9.8 %collective-permute-start.26 = (bf16[256,256]{1,0:T(8,128)(2,1)S(1)}, bf16[256,256]{1,0:T(8,128)(2,1)S(1)}, u32[]{:S(2)}, u32[]{:S(2)}) collective-permute-start(bf16[256,256]{1,0:T(8,128)(2,1)S(1)} %get-tuple-element.51.refs_4_.x_ref.refs_0_.refs_5_), channel_id=1, source_target_pairs={{0,2},{1,3},{2,0},{3,1},{4,6},{5,7},{6,4},{7,5},{8,10},{9,11},{10,... | collective-permute-start | bytes 393224 | tf_op jit(solution)/shard_map/ppermute | solution.py:321
  63.6 10.1 %collective-permute-start.25 = (bf16[512,256]{1,0:T(8,128)(2,1)S(1)}, bf16[512,256]{1,0:T(8,128)(2,1)S(1)}, u32[]{:S(2)}, u32[]{:S(2)}) collective-permute-start(bf16[512,256]{1,0:T(8,128)(2,1)S(1)} %get-tuple-element.63.refs_5_.refs_0_), channel_id=1, source_target_pairs={{0,4},{1,5},{2,6},{3,7},{4,0},{5,1},{6,2},{7,3},{8,12},{9,13},{10,... | collective-permute-start | bytes 786440 | tf_op jit(solution)/shard_map/ppermute | solution.py:321
  64.2 6.3 %collective-permute-start.28 = (bf16[256,256]{1,0:T(8,128)(2,1)S(1)}, bf16[256,256]{1,0:T(8,128)(2,1)S(1)}, u32[]{:S(2)}, u32[]{:S(2)}) collective-permute-start(bf16[256,256]{1,0:T(8,128)(2,1)S(1)} %get-tuple-element.64.refs_5_), channel_id=1, source_target_pairs={{0,2},{1,3},{2,0},{3,1},{4,6},{5,7},{6,4},{7,5},{8,10},{9,11},{10,... | collective-permute-start | bytes 393224 | tf_op jit(solution)/shard_map/ppermute | solution.py:321
  68.9 6.4 %collective-permute-start.31 = (bf16[256,256]{1,0:T(8,128)(2,1)S(1)}, bf16[256,256]{1,0:T(8,128)(2,1)S(1)}, u32[]{:S(2)}, u32[]{:S(2)}) collective-permute-start(bf16[256,256]{1,0:T(8,128)(2,1)S(1)} %get-tuple-element.69), channel_id=1, source_target_pairs={{0,2},{1,3},{2,0},{3,1},{4,6},{5,7},{6,4},{7,5},{8,10},{9,11},{10,... | collective-permute-start | bytes 393224 | tf_op jit(solution)/shard_map/ppermute | solution.py:321
  70.5 7.8 %collective-permute-start.29 = (bf16[256,256]{1,0:T(8,128)(2,1)S(1)}, bf16[256,256]{1,0:T(8,128)(2,1)S(1)}, u32[]{:S(2)}, u32[]{:S(2)}) collective-permute-start(bf16[256,256]{1,0:T(8,128)(2,1)S(1)} %shard_map.105), channel_id=1, source_target_pairs={{0,12},{1,13},{2,14},{3,15},{4,8},{5,9},{6,10},{7,11},{8,4},{9,5},... | collective-permute-start | bytes 393224 | tf_op jit(solution)/shard_map/ppermute | solution.py:321
  75.3 7.6 %collective-permute-start.32 = (bf16[256,256]{1,0:T(8,128)(2,1)S(1)}, bf16[256,256]{1,0:T(8,128)(2,1)S(1)}, u32[]{:S(2)}, u32[]{:S(2)}) collective-permute-start(bf16[256,256]{1,0:T(8,128)(2,1)S(1)} %shard_map.109), channel_id=1, source_target_pairs={{0,8},{1,9},{2,10},{3,11},{4,12},{5,13},{6,14},{7,15},{8,0},{9,1},... | collective-permute-start | bytes 393224 | tf_op jit(solution)/shard_map/ppermute | solution.py:321
  76.7 6.9 %collective-permute-start.34 = (bf16[256,256]{1,0:T(8,128)(2,1)S(1)}, bf16[256,256]{1,0:T(8,128)(2,1)S(1)}, u32[]{:S(2)}, u32[]{:S(2)}) collective-permute-start(bf16[256,256]{1,0:T(8,128)(2,1)S(1)} %get-tuple-element.80.refs_0_), channel_id=1, source_target_pairs={{0,16},{16,0},{1,17},{17,1},{2,18},{18,2},{3,19},{19,3},{4,20},{20... | collective-permute-start | bytes 393224 | tf_op jit(solution)/shard_map/ppermute | solution.py:321
  77.7 6.0 %collective-permute-start.35 = (bf16[256,256]{1,0:T(8,128)(2,1)S(1)}, bf16[256,256]{1,0:T(8,128)(2,1)S(1)}, u32[]{:S(2)}, u32[]{:S(2)}) collective-permute-start(bf16[256,256]{1,0:T(8,128)(2,1)S(1)} %get-tuple-element.81), channel_id=1, source_target_pairs={{0,17},{1,16},{2,19},{3,18},{4,21},{5,20},{6,23},{7,22},{8,25},{9,... | collective-permute-start | bytes 393224 | tf_op jit(solution)/shard_map/ppermute | solution.py:407
  (11 other events, 41.2 us)
